TPU v7x, 128 devices: a whole 4x4x4 slice. The times are simulated.
128 devices in a mesh: ctx: 16 (over y, x), head: 2 (over core), dp: 4 (over z).
Axes of the slice: x: 4, y: 4, z: 4, core: 2. Of those that a mesh axis runs over, the one named last changes fastest.
Arguments:
- x_in: bfloat16 [8192, 8192], P(('dp', 'ctx'), 'head'), parts along dimension 0, may hold values from -6 to 6
- bc_in: bfloat16 [8192, 2, 512], P(('dp', 'ctx'), None, 'head'), parts along dimension 0, may hold values from -4 to 4
- conv_x: float32 [4, 8192], P(None, 'head'), may hold values from -3 to 3
- conv_bc: float32 [4, 2, 512], P(None, None, 'head'), may hold values from -3 to 3
- dt_raw: float32 [64, 8192], P('head', ('dp', 'ctx')), parts along dimension 1, may hold values from -4 to 1
- rate: float32 [64], P('head'), may hold values from 0.0003 to 0.1
- grad_ssd: bfloat16 [8192, 8192], P(('dp', 'ctx'), 'head'), parts along dimension 0, may hold values from -6 to 6
- query: bfloat16 [8192, 4096], P(('dp', 'ctx'), 'head'), parts along dimension 0, may hold values from -6 to 6
- key: bfloat16 [8192, 512], P(('dp', 'ctx'), 'head'), parts along dimension 0, may hold values from -6 to 6
- value: bfloat16 [8192, 512], P(('dp', 'ctx'), 'head'), parts along dimension 0, may hold values from -6 to 6
- d_out: bfloat16 [8192, 4096], P(('dp', 'ctx'), 'head'), parts along dimension 0, may hold values from -6 to 6
- doc_lengths: int32 [16], P('dp'), parts along dimension 0, may hold values from 1 to 1024, 2048 in all
Outputs:
- d_x_in: bfloat16 [8192, 8192], P(('dp', 'ctx'), 'head'), parts along dimension 0
- d_bc_in: bfloat16 [8192, 2, 512], P(('dp', 'ctx'), None, 'head'), parts along dimension 0
- d_dt_raw: float32 [64, 8192], P('head', ('dp', 'ctx')), parts along dimension 1
- d_conv_x: float32 [16, 8192], P('dp', 'head'), parts along dimension 0
- d_conv_bc: float32 [16, 2, 512], P('dp', None, 'head'), parts along dimension 0
- d_query: bfloat16 [8192, 4096], P(('dp', 'ctx'), 'head'), parts along dimension 0
- d_key: bfloat16 [8192, 512], P(('dp', 'ctx'), 'head'), parts along dimension 0
- d_value: bfloat16 [8192, 512], P(('dp', 'ctx'), 'head'), parts along dimension 0
There are 4 independent parts, one for each index of `dp`. A program takes and returns all parts, laid end to end along the dimension named above; an argument that names none is the same for every part. Nothing has to cross between parts.
Inputs may be any that keep to these rules, and one draw needn't show every extreme that they name: `doc_lengths`: document lengths that fill the 2048 positions in order; the longest is exactly 1024.
All inputs are finite; a program needn't handle non-finite values.
Results may differ from a plain program's by a relative error of at most 0.018.
Values may be sent and summed in bfloat16 or wider, within the bound.
No kernel may reach another device: no remote copies, remote signals or barrier semaphores. Data moves between devices by JAX's collectives and lax.ppermute only.
A program may use at most 192 MiB of HBM per device.

v0:
```python
import jax
import jax.numpy as jnp
from jax import lax
from jax.sharding import PartitionSpec as P

P_SIZE = 128
N = 128
HD = 128
STRETCH = 128


HIGH = lax.Precision.HIGHEST
NEG_BIG = -1e30


def from_behind(x, axis, by):
    devices = lax.axis_size(axis)
    pairs = [(i, i + by) for i in range(devices) if 0 <= i + by < devices]
    return lax.ppermute(x, axis, pairs)


def entering(part, axis, combine, identity, reverse):
    count = lax.axis_size(axis)
    place = lax.axis_index(axis)
    ahead = count - 1 - place if reverse else place
    gathered = jax.tree.map(lambda a: lax.all_gather(a, axis), part)
    state = jax.tree.map(lambda a, e: jnp.zeros_like(a) + jnp.asarray(e, a.dtype), part, identity)

    def one(lap, state):
        source = count - 1 - lap if reverse else lap
        return combine(
            state, jax.tree.map(lambda a: lax.dynamic_index_in_dim(a, source, 0, False), gathered)
        )

    return lax.fori_loop(0, ahead, one, state)


def from_behind_2(x, axis, by):
    devices = lax.axis_size(axis)
    return lax.ppermute(x, axis, [(i, (i + by) % devices) for i in range(devices)])


def doc_starts(doc_lengths):
    doc_ends = jnp.cumsum(doc_lengths)
    return doc_ends - doc_lengths


def segment_of(positions, starts):
    hits = (positions[:, None] >= starts[None, :]).astype(jnp.int32)
    return jnp.sum(hits, axis=1) - 1


def start_flags(positions, starts):
    return jnp.any(positions[:, None] == starts[None, :], axis=1).astype(jnp.float32)


def conv_silu(extended, weight, seg_ext):
    tap_count = weight.shape[0]
    row_count = extended.shape[0] - tap_count + 1
    last_seg = seg_ext[tap_count - 1 :]
    shape_tail = (1,) * (extended.ndim - 1)
    running = jnp.zeros((row_count,) + extended.shape[1:], jnp.float32)
    for tap_index in range(tap_count):
        keep_mask = (seg_ext[tap_index : tap_index + row_count] == last_seg).astype(jnp.float32)
        running = running + extended[tap_index : tap_index + row_count] * weight[
            tap_index
        ] * keep_mask.reshape((row_count,) + shape_tail)
    return jax.nn.silu(running)


def block_terms(x_conv, b_matrix, c_matrix, step_size, flags, rate_grid):
    log_decay = -step_size * rate_grid
    cum_log = jnp.cumsum(log_decay, axis=1)
    count_ids = jnp.cumsum(flags, axis=1)
    span = x_conv.shape[1]
    order_ids = jnp.arange(span, dtype=jnp.int32)
    causal = order_ids[:, None] >= order_ids[None, :]
    same_doc = (count_ids[:, :, None] == count_ids[:, None, :]) & causal[None]
    log_gap = cum_log[:, :, None] - cum_log[:, None, :]
    decay_grid = jnp.exp(jnp.where(same_doc[:, :, :, None, None], log_gap, NEG_BIG))
    inner_cb = jnp.einsum("ktgn,ksgn->ktsg", c_matrix, b_matrix, precision=HIGH)
    scores = decay_grid * inner_cb[..., None] * step_size[:, None]
    y_intra = jnp.einsum("ktsge,ksgep->ktgep", scores, x_conv, precision=HIGH)
    keep_mask = (count_ids == 0).astype(jnp.float32)
    lead_decay = jnp.exp(cum_log) * keep_mask[:, :, None, None]
    tail_same = count_ids == count_ids[:, -1:]
    tail_decay = (
        jnp.exp(jnp.where(tail_same[:, :, None, None], cum_log[:, -1:] - cum_log, NEG_BIG))
        * step_size
    )
    s_local = jnp.einsum("ksge,ksgep,ksgn->kgepn", tail_decay, x_conv, b_matrix, precision=HIGH)
    block_decay = jnp.exp(cum_log[:, -1]) * keep_mask[:, -1][:, None, None]
    return (y_intra, lead_decay, s_local, block_decay)


def chain_output(y_intra, lead_decay, c_matrix, s_local, block_decay, start_state):

    def advance(state_now, block_item):
        s_add, factor = block_item
        return (factor[:, :, None, None] * state_now + s_add, state_now)

    final_state, inits = lax.scan(advance, start_state, (s_local, block_decay))
    carried = jnp.einsum("ktgn,kgepn->ktgep", c_matrix, inits, precision=HIGH)
    return (y_intra + lead_decay[..., None] * carried, final_state)


def combine(earlier, later):
    return (earlier[0] * later[0], later[0][..., None, None] * earlier[1] + later[1])


def shards(
    x_in, bc_in, conv_x, conv_bc, dt_raw, rate, grad_ssd, query, key, value, d_out, doc_lengths
):
    row_count = x_in.shape[0]
    tap_count = conv_x.shape[0]
    head_count = dt_raw.shape[0]
    group_count = bc_in.shape[2] // N
    per_group = head_count // group_count
    block_count = row_count // STRETCH
    ctx_place = lax.axis_index("ctx")
    starts = doc_starts(doc_lengths)
    row_ids = jnp.arange(row_count, dtype=jnp.int32)
    positions = ctx_place * row_count + row_ids
    ext_ids = (
        ctx_place * row_count
        - (tap_count - 1)
        + jnp.arange(row_count + tap_count - 1, dtype=jnp.int32)
    )
    seg_ext = segment_of(ext_ids, starts)
    flags = start_flags(positions, starts).reshape(block_count, STRETCH)
    rate_grid = rate.reshape(group_count, per_group)
    tail_x, tail_bc = from_behind(
        (x_in[row_count - tap_count + 1 :], bc_in[row_count - tap_count + 1 :]), "ctx", 1
    )
    ext_x = jnp.concatenate([tail_x, x_in]).astype(jnp.float32)
    ext_bc = jnp.concatenate([tail_bc, bc_in]).astype(jnp.float32)

    def local_terms(x_values, bc_values, weight_x, weight_bc, dt_values):
        x_conv = conv_silu(x_values, weight_x, seg_ext).reshape(
            block_count, STRETCH, group_count, per_group, P_SIZE
        )
        bc_conv = conv_silu(bc_values, weight_bc, seg_ext)
        b_matrix = bc_conv[:, 0].reshape(block_count, STRETCH, group_count, N)
        c_matrix = bc_conv[:, 1].reshape(block_count, STRETCH, group_count, N)
        step_size = jax.nn.softplus(dt_values).T.reshape(
            block_count, STRETCH, group_count, per_group
        )
        y_intra, lead_decay, s_local, block_decay = block_terms(
            x_conv, b_matrix, c_matrix, step_size, flags, rate_grid
        )
        return (y_intra, lead_decay, c_matrix, s_local, block_decay)

    pieces, pull_terms = jax.vjp(local_terms, ext_x, ext_bc, conv_x, conv_bc, dt_raw)
    y_intra, lead_decay, c_matrix, s_local, block_decay = pieces

    def fold_block(running, block_item):
        s_add, factor = block_item
        return ((running[0] * factor, factor[..., None, None] * running[1] + s_add), None)

    unit_factor = jnp.ones((group_count, per_group), jnp.float32)
    zero_state = jnp.zeros((group_count, per_group, P_SIZE, N), jnp.float32)
    (shard_factor, shard_state), _ = lax.scan(
        fold_block, (unit_factor, zero_state), (s_local, block_decay)
    )
    _, start_state = entering(
        (shard_factor, shard_state), "ctx", combine, (unit_factor, zero_state), False
    )

    def finish(y_part, lead_part, c_part, s_part, decay_part, state_in):
        return chain_output(y_part, lead_part, c_part, s_part, decay_part, state_in)

    (y_out, state_out), pull_finish = jax.vjp(
        finish, y_intra, lead_decay, c_matrix, s_local, block_decay, start_state
    )
    grad_y = grad_ssd.astype(jnp.float32).reshape(
        block_count, STRETCH, group_count, per_group, P_SIZE
    )
    own_grad = pull_finish((grad_y, jnp.zeros_like(state_out)))[5]
    _, grad_out = entering(
        (shard_factor, own_grad), "ctx", combine, (unit_factor, zero_state), True
    )
    finish_cots = pull_finish((grad_y, grad_out))
    grad_ext_x, grad_ext_bc, grad_wx, grad_wbc, grad_dt = pull_terms(tuple(finish_cots[:5]))
    back_x, back_bc = (
        from_behind(grad_ext_x[: tap_count - 1].astype(jnp.bfloat16), "ctx", -1).astype(
            jnp.float32
        ),
        from_behind(grad_ext_bc[: tap_count - 1].astype(jnp.bfloat16), "ctx", -1).astype(
            jnp.float32
        ),
    )
    own_x = grad_ext_x[tap_count - 1 :]
    own_bc = grad_ext_bc[tap_count - 1 :]
    split_row = row_count - tap_count + 1
    grad_x_in = jnp.concatenate([own_x[:split_row], own_x[split_row:] + back_x]).astype(
        jnp.bfloat16
    )
    grad_bc_in = jnp.concatenate([own_bc[:split_row], own_bc[split_row:] + back_bc]).astype(
        jnp.bfloat16
    )
    grad_wx, grad_wbc = (
        lax.psum(grad_wx.astype(jnp.bfloat16), "ctx").astype(jnp.float32),
        lax.psum(grad_wbc.astype(jnp.bfloat16), "ctx").astype(jnp.float32),
    )
    head_dim = HD
    kv_count = key.shape[1] // head_dim
    q_per = query.shape[1] // head_dim // kv_count
    score_scale = head_dim ** (-0.5)
    shard_total = lax.axis_size("ctx")
    key_grid = key.reshape(row_count, kv_count, head_dim)
    value_grid = value.reshape(row_count, kv_count, head_dim)
    set_rows = query.shape[0]
    query_sets = [
        (
            query.reshape(set_rows, kv_count, q_per, head_dim),
            d_out.reshape(set_rows, kv_count, q_per, head_dim),
            positions,
            segment_of(positions, starts),
        )
    ]
    set_total = len(query_sets)

    def allowed_for(qset, first_row, key_total):
        key_pos = first_row + jnp.arange(key_total, dtype=jnp.int32)
        key_seg = segment_of(key_pos, starts)
        return (qset[2][:, None] >= key_pos[None, :]) & (qset[3][:, None] == key_seg[None, :])

    def stats_one(running, qset, key_rows, value_rows, first_row):

        def stats_compute(state):
            row_top, exp_total, weighted = state
            allowed = allowed_for(qset, first_row, key_rows.shape[0])[None, None]
            scores = (
                jnp.einsum("igqd,jgd->gqij", qset[0], key_rows, preferred_element_type=jnp.float32)
                * score_scale
            )
            scores = jnp.where(allowed, scores, NEG_BIG)
            d_prob = jnp.einsum(
                "igqd,jgd->gqij", qset[1], value_rows, preferred_element_type=jnp.float32
            )
            new_top = jnp.maximum(row_top, jnp.max(scores, axis=-1))
            exp_weights = jnp.where(allowed, jnp.exp(scores - new_top[..., None]), 0.0)
            factor = jnp.exp(row_top - new_top)
            return (new_top, jnp.sum(exp_weights, axis=-1), jnp.sum(exp_weights * d_prob, axis=-1))

        return lax.cond(first_row <= qset[2][-1], stats_compute, lambda state: state, running)

    def stats_piece(running, block_pair, first_row):
        return tuple(
            (
                stats_one(
                    running[set_index],
                    query_sets[set_index],
                    block_pair[0],
                    block_pair[1],
                    first_row,
                )
                for set_index in range(set_total)
            )
        )

    stat_init = tuple(
        (
            (
                jnp.full((kv_count, q_per, qset[0].shape[0]), NEG_BIG, jnp.float32),
                jnp.zeros((kv_count, q_per, qset[0].shape[0]), jnp.float32),
                jnp.zeros((kv_count, q_per, qset[0].shape[0]), jnp.float32),
            )
            for qset in query_sets
        )
    )

    def grads_one(qset, stat_pair, key_rows, value_rows, first_row):
        log_total, delta_att = stat_pair
        set_rows = qset[0].shape[0]
        key_total = key_rows.shape[0]

        def grads_compute(start_row):
            allowed = allowed_for(qset, start_row, key_total)[None, None]
            scores = (
                jnp.einsum("igqd,jgd->gqij", qset[0], key_rows, preferred_element_type=jnp.float32)
                * score_scale
            )
            prob_f = jnp.where(
                allowed, jnp.exp(jnp.where(allowed, scores, NEG_BIG) - log_total[..., None]), 0.0
            )
            d_prob = jnp.einsum(
                "igqd,jgd->gqij", qset[1], value_rows, preferred_element_type=jnp.float32
            )
            d_score = prob_f * (d_prob - delta_att[..., None])
            prob_b = prob_f.astype(jnp.bfloat16)
            score_b = d_score.astype(jnp.bfloat16)
            grad_q = (
                jnp.einsum("gqij,jgd->igqd", score_b, key_rows, preferred_element_type=jnp.float32)
                * score_scale
            )
            grad_k = (
                jnp.einsum("gqij,igqd->jgd", score_b, qset[0], preferred_element_type=jnp.float32)
                * score_scale
            )
            grad_v = jnp.einsum(
                "gqij,igqd->jgd", prob_b, qset[1], preferred_element_type=jnp.float32
            )
            return (grad_q, grad_k, grad_v)

        def skipped(start_row):
            return (
                jnp.zeros((set_rows, kv_count, q_per, head_dim), jnp.float32),
                jnp.zeros((key_total, kv_count, head_dim), jnp.float32),
                jnp.zeros((key_total, kv_count, head_dim), jnp.float32),
            )

        return lax.cond(first_row <= qset[2][-1], grads_compute, skipped, first_row)

    def block_all(key_rows, value_rows, first_row, stat_pairs):
        set_grads = [grads_one(query_sets[0], stat_pairs[0], key_rows, value_rows, first_row)]
        grad_k = set_grads[0][1]
        grad_v = set_grads[0][2]
        return (tuple((member[0] for member in set_grads)), grad_k, grad_v)

    zero_kv = jnp.zeros((row_count, kv_count, head_dim), jnp.float32)
    zero_q = tuple(
        (
            jnp.zeros((qset[0].shape[0], kv_count, q_per, head_dim), jnp.float32)
            for qset in query_sets
        )
    )
    stats = stats_piece(
        stat_init,
        (
            lax.all_gather(key_grid, "ctx", axis=0, tiled=True),
            lax.all_gather(value_grid, "ctx", axis=0, tiled=True),
        ),
        jnp.int32(0),
    )
    stat_pairs = [(running[0] + jnp.log(running[1]), running[2] / running[1]) for running in stats]

    def cycle_turn(turn_number, running):
        key_rows, value_rows, k_sum, v_sum, q_sums = running
        holder_index = (ctx_place + turn_number) % shard_total
        q_parts, grad_k, grad_v = block_all(
            key_rows, value_rows, holder_index * row_count, stat_pairs
        )
        key_rows, value_rows = from_behind_2((key_rows, value_rows), "ctx", -1)
        k_sum, v_sum = from_behind_2((k_sum + grad_k, v_sum + grad_v), "ctx", -1)
        return (
            key_rows,
            value_rows,
            k_sum,
            v_sum,
            tuple((q_sums[set_index] + q_parts[set_index] for set_index in range(set_total))),
        )

    key_rows, value_rows, k_sum, v_sum, q_sums = lax.fori_loop(
        0, shard_total - 1, cycle_turn, (key_grid, value_grid, zero_kv, zero_kv, zero_q)
    )
    holder_index = (ctx_place + shard_total - 1) % shard_total
    q_parts, grad_k, grad_v = block_all(key_rows, value_rows, holder_index * row_count, stat_pairs)
    grad_k_all, grad_v_all = (
        from_behind_2((k_sum + grad_k).astype(jnp.bfloat16), "ctx", -1).astype(jnp.float32),
        from_behind_2((v_sum + grad_v).astype(jnp.bfloat16), "ctx", -1).astype(jnp.float32),
    )
    q_sums = tuple((q_sums[set_index] + q_parts[set_index] for set_index in range(set_total)))
    q_width = kv_count * q_per * head_dim
    d_query = q_sums[0].reshape(row_count, q_width).astype(jnp.bfloat16)
    d_key = grad_k_all.reshape(row_count, kv_count * head_dim).astype(jnp.bfloat16)
    d_value = grad_v_all.reshape(row_count, kv_count * head_dim).astype(jnp.bfloat16)
    return (grad_x_in, grad_bc_in, grad_dt, grad_wx, grad_wbc, d_query, d_key, d_value)


def solution(mesh):
    in_specs = (
        P(("dp", "ctx"), "head"),
        P(("dp", "ctx"), None, "head"),
        P(None, "head"),
        P(None, None, "head"),
        P("head", ("dp", "ctx")),
        P("head"),
        P(("dp", "ctx"), "head"),
        P(("dp", "ctx"), "head"),
        P(("dp", "ctx"), "head"),
        P(("dp", "ctx"), "head"),
        P(("dp", "ctx"), "head"),
        P("dp"),
    )
    out_specs = (
        P(("dp", "ctx"), "head"),
        P(("dp", "ctx"), None, "head"),
        P("head", ("dp", "ctx")),
        P("dp", "head"),
        P("dp", None, "head"),
        P(("dp", "ctx"), "head"),
        P(("dp", "ctx"), "head"),
        P(("dp", "ctx"), "head"),
    )
    return jax.shard_map(shards, mesh=mesh, in_specs=in_specs, out_specs=out_specs, check_vma=False)
```

profile of v0, /device:TPU:0, one launch (start us, length us, event | category | flops | bytes accessed | tf_op | source)
XLA Modules:
  0.0 908.6 jit_solution(14618762775431349911)
XLA Ops:
  8.1 3.5 collective-permute-start.4
  27.1 3.4 fusion.62
  31.4 3.4 collective-permute-start.5
  37.7 24.6 %all-gather = f32[16,1,2,16]{3,2,1,0:T(2,128)} all-gather(f32[1,1,2,16]{3,2,1,0:T(2,128)S(1)} %copy.266), channel_id=2, replica_groups=mesh['ctx'=16,'head'=2,'dp'=4] {'ctx'}, dimensions={0}, use_global_device_ids=true | all-gather | bytes 2176 | tf_op jit(solution)/shard_map/all_gather | solution.py:26
  64.5 165.2 %all-gather.12.cloned.1.call-done = f32[32,16,128,128]{3,2,1,0:T(8,128)} async-done(((f32[2,16,128,128]{3,2,1,0:T(8,128)}), f32[32,16,128,128]{3,2,1,0:T(8,128)}) %all-gather.12.cloned.1.call-update) | async-done | bytes 33554448 | tf_op jit(solution)/shard_map/all_gather | solution.py:26
  229.9 40.2 %while.15 = (s32[]{:T(128)}, f32[2,16,128,128]{3,2,1,0:T(8,128)S(1)}, s32[]{:T(128)}, f32[16,2,16]{2,1,0:T(2,128)}, f32[16,2,16,128,128]{4,3,2,1,0:T(8,128)}, /*index=5*/s32[]{:T(128)}, s32[]{:T(128)}, s32[]{:T(128)}, s32[]{:T(128)}) while((s32[]{:T(128)}, f32[2,16,128,128]{3,2,1,0:T(8,128)S(1)}, s32[]{:T(128)}, f32[16,2,16]{2,1,0:T(2,128)}, ...), condition=%wide.region_6.7_spmd, body=%wide.region_5.6_spmd.sunk | while | flops 1048582 | bytes 6291995 | solution.py:35
  272.1 3.1 bitcast_add_fusion.2
  275.3 3.0 copy.276
  278.3 8.0 multiply_reduce_fusion.3
  288.2 2.9 copy.278
  291.1 4.9 fusion.59
  307.6 13.1 %all-gather.10.cloned.1.call-done = bf16[2048,2,128]{0,2,1:T(8,128)(2,1)} async-done(((bf16[128,2,128]{0,2,1:T(8,128)(2,1)}), bf16[2048,2,128]{0,2,1:T(8,128)(2,1)}) %all-gather.10.cloned.1.call-update) | async-done | bytes 1048592 | tf_op jit(solution)/shard_map/all_gather | solution.py:332
  320.7 18.1 %conditional.3 = (f32[2,8,128]{2,1,0:T(8,128)}, f32[2,8,128]{2,1,0:T(8,128)S(1)}, f32[2,8,128]{2,1,0:T(8,128)S(1)}) conditional(s32[]{:T(128)} %convert_element_type.157, () %tuple.104, (s32[128]{0:T(128)}, s32[128]{0:T(128)}, s32[4]{0:T(128)}, bf16[2048,2,128]{0,2,1:T(8,128)(2,1)}, bf16[128,2,8,128]{0,3,2,1:T(8,128)(2,1)}, ...), branch_computations={%region_28.29_spmd, %region_29.34_spmd} | conditional | flops 2207012864 | bytes 58844228 | solution.py:246
  323.0 4.1 fusion.1
  327.8 6.3 fusion
  334.1 4.7 fusion.2
  340.8 389.5 %while.33 = (s32[]{:T(128)}, bf16[128,2,128]{2,0,1:T(8,128)(2,1)}, bf16[128,2,128]{2,0,1:T(8,128)(2,1)}, f32[128,2,128]{2,0,1:T(8,128)}, f32[128,2,128]{2,0,1:T(...) while((s32[]{:T(128)}, bf16[128,2,128]{2,0,1:T(8,128)(2,1)}, ...), condition=%wide.region_38.39_spmd.clone, body=%wide.region_34.38_spmd.clone.sunk | while | flops 338577024 | bytes 18896092 | solution.py:354
  349.6 6.1 conditional.7
  361.6 4.1 collective-permute-done.3
  365.6 4.5 collective-permute-done.2
  372.3 4.2 collective-permute-start
  380.6 5.9 collective-permute-start.3
  395.5 3.3 collective-permute-start
  403.0 6.1 collective-permute-start.3
  415.7 4.2 collective-permute-done.2
  422.0 5.7 collective-permute-start
  431.9 5.9 collective-permute-start.3
  444.1 4.2 collective-permute-done.2
  450.5 5.7 collective-permute-start
  460.4 5.9 collective-permute-start.3
  472.5 4.2 collective-permute-done.2
  478.8 5.7 collective-permute-start
  488.7 5.9 collective-permute-start.3
  500.7 4.2 collective-permute-done.2
  507.0 5.7 collective-permute-start
  517.0 5.9 collective-permute-start.3
  528.9 4.2 collective-permute-done.2
  535.2 5.7 collective-permute-start
  545.1 5.9 collective-permute-start.3
  556.9 4.2 collective-permute-done.2
  563.3 5.7 collective-permute-start
  573.2 5.9 collective-permute-start.3
  585.0 4.3 collective-permute-done.2
  591.4 5.6 collective-permute-start
  601.2 5.9 collective-permute-start.3
  611.0 2.8 collective-permute-done.2
  616.0 3.3 collective-permute-start
  623.6 5.9 collective-permute-start.3
  638.3 4.0 collective-permute-start
  646.6 5.9 collective-permute-start.3
  656.4 2.9 collective-permute-done.2
  661.5 4.4 collective-permute-start
  670.1 5.9 collective-permute-start.3
  680.0 3.5 collective-permute-done.2
  685.6 3.9 collective-permute-start
  693.7 5.9 collective-permute-start.3
  708.5 4.2 collective-permute-start
  716.9 5.9 collective-permute-start.3
  726.8 2.8 collective-permute-done.2
  731.2 10.9 %collective-permute-start.8 = (bf16[128,2,128]{2,0,1:T(8,128)(2,1)S(1)}, bf16[128,2,128]{2,0,1:T(8,128)(2,1)S(1)}, u32[]{:S(2)}, u32[]{:S(2)}) collective-permute-start(bf16[128,2,128]{2,0,1:T(8,128)(2,1)S(1)} %add_convert_fusion.2), channel_id=1, source_target_pairs={{0,120},{8,0},{16,8},{24,16},{32,24},{40,32},{48,40},{56,48},{64,5... | collective-permute-start | bytes 196616 | tf_op jit(solution)/shard_map/ppermute | solution.py:40
  755.5 3.8 fusion.68
  760.3 4.2 fusion.72
  773.2 3.5 fusion.75
  785.6 113.9 %all-reduce.20 = (bf16[4,4096]{1,0:T(4,128)(2,1)S(1)}, bf16[4,2,256]{2,1,0:T(2,128)(2,1)S(1)}) all-reduce(bf16[4,4096]{1,0:T(4,128)(2,1)S(1)} %copy-done.46, bf16[4,2,256]{2,1,0:T(2,128)(2,1)S(1)} %add_convert_fusion.4), channel_id=1, replica_groups=mesh['ctx'=16,'head'=2,'dp'=4] {'ctx'}, use_global_device_ids=true, to_apply=%region_21.22 | all-reduce | flops 18432 | bytes 73728 | tf_op jit(solution)/shard_map/psum | solution.py:202
  (587 shorter events, 295.2 us)
Async XLA Ops:
  7.2 222.5 %all-gather.12.cloned.1.call-start = ((), (), s32[]{:S(2)}) async-start(), calls=%async_computation.2 | async-start | bytes 35651584 | tf_op jit(solution)/shard_map/all_gather | solution.py:26
  8.1 17.4 %collective-permute-start.4 = (bf16[3,2,256]{0,2,1:T(8,128)(2,1)S(1)}, bf16[3,2,256]{0,2,1:T(8,128)(2,1)S(1)}, u32[]{:S(2)}, u32[]{:S(2)}) collective-permute-start(bf16[3,2,256]{0,2,1:T(8,128)(2,1)S(1)} %copy.269), channel_id=1, source_target_pairs={{0,8},{8,16},{16,24},{24,32},{32,40},{40,48},{48,56},{56,64},{64,7... | collective-permute-start | bytes 9224 | tf_op jit(solution)/shard_map/ppermute | solution.py:19
  30.5 277.1 %all-gather.8.cloned.1.call-start = ((), (), s32[]{:S(2)}) async-start(), calls=%async_computation | async-start | bytes 1114112 | tf_op jit(solution)/shard_map/all_gather | solution.py:331
  31.3 289.4 %all-gather.10.cloned.1.call-start = ((), (), s32[]{:S(2)}) async-start(), calls=%async_computation.1 | async-start | bytes 1114112 | tf_op jit(solution)/shard_map/all_gather | solution.py:332
  31.4 31.4 %collective-permute-start.5 = (bf16[3,4096]{1,0:T(4,128)(2,1)S(1)}, bf16[3,4096]{1,0:T(4,128)(2,1)S(1)}, u32[]{:S(2)}, u32[]{:S(2)}) collective-permute-start(bf16[3,4096]{1,0:T(4,128)(2,1)S(1)} %slice.149), channel_id=1, source_target_pairs={{0,8},{8,16},{16,24},{24,32},{32,40},{40,48},{48,56},{56,64},{64,7... | collective-permute-start | bytes 73736 | tf_op jit(solution)/shard_map/ppermute | solution.py:19
  35.6 732.7 %all-gather.14.cloned.1.call-start = ((), (), s32[]{:S(2)}) async-start(), calls=%async_computation.3 | async-start | bytes 35651584 | tf_op jit(solution)/shard_map/all_gather | solution.py:26
  342.3 19.3 %collective-permute-start = (bf16[128,2,128]{2,0,1:T(8,128)(2,1)}, bf16[128,2,128]{2,0,1:T(8,128)(2,1)}, u32[]{:S(2)}, u32[]{:S(2)}) collective-permute-start(bf16[128,2,128]{2,0,1:T(8,128)(2,1)} %copy.397), channel_id=1, source_target_pairs={{0,120},{8,0},{16,8},{24,16},{32,24},{40,32},{48,40},{56,48},{64,5... | collective-permute-start | bytes 196616 | tf_op jit(solution)/shard_map/while/body/eval_jaxpr/ppermute | solution.py:40
  346.4 15.1 %collective-permute-start.1 = (bf16[128,2,128]{2,0,1:T(8,128)(2,1)}, bf16[128,2,128]{2,0,1:T(8,128)(2,1)}, u32[]{:S(2)}, u32[]{:S(2)}) collective-permute-start(bf16[128,2,128]{2,0,1:T(8,128)(2,1)} %copy.398), channel_id=1, source_target_pairs={{0,120},{8,0},{16,8},{24,16},{32,24},{40,32},{48,40},{56,48},{64,5... | collective-permute-start | bytes 196616 | tf_op jit(solution)/shard_map/while/body/eval_jaxpr/ppermute | solution.py:40
  356.3 9.3 %collective-permute-start.3 = (f32[128,2,128]{2,0,1:T(8,128)}, f32[128,2,128]{2,0,1:T(8,128)S(1)}, u32[]{:S(2)}, u32[]{:S(2)}) collective-permute-start(f32[128,2,128]{2,0,1:T(8,128)} %add.401), channel_id=1, source_target_pairs={{0,120},{8,0},{16,8},{24,16},{32,24},{40,32},{48,40},{56,48},{64,5... | collective-permute-start | bytes 393224 | tf_op jit(solution)/shard_map/while/body/eval_jaxpr/ppermute | solution.py:40
  358.7 11.4 %collective-permute-start.2 = (f32[128,2,128]{2,0,1:T(8,128)}, f32[128,2,128]{2,0,1:T(8,128)S(1)}, u32[]{:S(2)}, u32[]{:S(2)}) collective-permute-start(f32[128,2,128]{2,0,1:T(8,128)} %add.400), channel_id=1, source_target_pairs={{0,120},{8,0},{16,8},{24,16},{32,24},{40,32},{48,40},{56,48},{64,5... | collective-permute-start | bytes 393224 | tf_op jit(solution)/shard_map/while/body/eval_jaxpr/ppermute | solution.py:40
  372.3 18.2 %collective-permute-start = (bf16[128,2,128]{2,0,1:T(8,128)(2,1)}, bf16[128,2,128]{2,0,1:T(8,128)(2,1)}, u32[]{:S(2)}, u32[]{:S(2)}) collective-permute-start(bf16[128,2,128]{2,0,1:T(8,128)(2,1)} %copy.397), channel_id=1, source_target_pairs={{0,120},{8,0},{16,8},{24,16},{32,24},{40,32},{48,40},{56,48},{64,5... | collective-permute-start | bytes 196616 | tf_op jit(solution)/shard_map/while/body/eval_jaxpr/ppermute | solution.py:40
  377.9 12.6 %collective-permute-start.1 = (bf16[128,2,128]{2,0,1:T(8,128)(2,1)}, bf16[128,2,128]{2,0,1:T(8,128)(2,1)}, u32[]{:S(2)}, u32[]{:S(2)}) collective-permute-start(bf16[128,2,128]{2,0,1:T(8,128)(2,1)} %copy.398), channel_id=1, source_target_pairs={{0,120},{8,0},{16,8},{24,16},{32,24},{40,32},{48,40},{56,48},{64,5... | collective-permute-start | bytes 196616 | tf_op jit(solution)/shard_map/while/body/eval_jaxpr/ppermute | solution.py:40
  380.6 9.8 %collective-permute-start.3 = (f32[128,2,128]{2,0,1:T(8,128)}, f32[128,2,128]{2,0,1:T(8,128)S(1)}, u32[]{:S(2)}, u32[]{:S(2)}) collective-permute-start(f32[128,2,128]{2,0,1:T(8,128)} %add.401), channel_id=1, source_target_pairs={{0,120},{8,0},{16,8},{24,16},{32,24},{40,32},{48,40},{56,48},{64,5... | collective-permute-start | bytes 393224 | tf_op jit(solution)/shard_map/while/body/eval_jaxpr/ppermute | solution.py:40
  395.5 17.6 %collective-permute-start = (bf16[128,2,128]{2,0,1:T(8,128)(2,1)}, bf16[128,2,128]{2,0,1:T(8,128)(2,1)}, u32[]{:S(2)}, u32[]{:S(2)}) collective-permute-start(bf16[128,2,128]{2,0,1:T(8,128)(2,1)} %copy.397), channel_id=1, source_target_pairs={{0,120},{8,0},{16,8},{24,16},{32,24},{40,32},{48,40},{56,48},{64,5... | collective-permute-start | bytes 196616 | tf_op jit(solution)/shard_map/while/body/eval_jaxpr/ppermute | solution.py:40
  400.3 12.8 %collective-permute-start.1 = (bf16[128,2,128]{2,0,1:T(8,128)(2,1)}, bf16[128,2,128]{2,0,1:T(8,128)(2,1)}, u32[]{:S(2)}, u32[]{:S(2)}) collective-permute-start(bf16[128,2,128]{2,0,1:T(8,128)(2,1)} %copy.398), channel_id=1, source_target_pairs={{0,120},{8,0},{16,8},{24,16},{32,24},{40,32},{48,40},{56,48},{64,5... | collective-permute-start | bytes 196616 | tf_op jit(solution)/shard_map/while/body/eval_jaxpr/ppermute | solution.py:40
  403.0 12.6 %collective-permute-start.3 = (f32[128,2,128]{2,0,1:T(8,128)}, f32[128,2,128]{2,0,1:T(8,128)S(1)}, u32[]{:S(2)}, u32[]{:S(2)}) collective-permute-start(f32[128,2,128]{2,0,1:T(8,128)} %add.401), channel_id=1, source_target_pairs={{0,120},{8,0},{16,8},{24,16},{32,24},{40,32},{48,40},{56,48},{64,5... | collective-permute-start | bytes 393224 | tf_op jit(solution)/shard_map/while/body/eval_jaxpr/ppermute | solution.py:40
  410.7 9.2 %collective-permute-start.2 = (f32[128,2,128]{2,0,1:T(8,128)}, f32[128,2,128]{2,0,1:T(8,128)S(1)}, u32[]{:S(2)}, u32[]{:S(2)}) collective-permute-start(f32[128,2,128]{2,0,1:T(8,128)} %add.400), channel_id=1, source_target_pairs={{0,120},{8,0},{16,8},{24,16},{32,24},{40,32},{48,40},{56,48},{64,5... | collective-permute-start | bytes 393224 | tf_op jit(solution)/shard_map/while/body/eval_jaxpr/ppermute | solution.py:40
  422.0 19.8 %collective-permute-start = (bf16[128,2,128]{2,0,1:T(8,128)(2,1)}, bf16[128,2,128]{2,0,1:T(8,128)(2,1)}, u32[]{:S(2)}, u32[]{:S(2)}) collective-permute-start(bf16[128,2,128]{2,0,1:T(8,128)(2,1)} %copy.397), channel_id=1, source_target_pairs={{0,120},{8,0},{16,8},{24,16},{32,24},{40,32},{48,40},{56,48},{64,5... | collective-permute-start | bytes 196616 | tf_op jit(solution)/shard_map/while/body/eval_jaxpr/ppermute | solution.py:40
  429.2 12.6 %collective-permute-start.1 = (bf16[128,2,128]{2,0,1:T(8,128)(2,1)}, bf16[128,2,128]{2,0,1:T(8,128)(2,1)}, u32[]{:S(2)}, u32[]{:S(2)}) collective-permute-start(bf16[128,2,128]{2,0,1:T(8,128)(2,1)} %copy.398), channel_id=1, source_target_pairs={{0,120},{8,0},{16,8},{24,16},{32,24},{40,32},{48,40},{56,48},{64,5... | collective-permute-start | bytes 196616 | tf_op jit(solution)/shard_map/while/body/eval_jaxpr/ppermute | solution.py:40
  431.9 12.2 %collective-permute-start.3 = (f32[128,2,128]{2,0,1:T(8,128)}, f32[128,2,128]{2,0,1:T(8,128)S(1)}, u32[]{:S(2)}, u32[]{:S(2)}) collective-permute-start(f32[128,2,128]{2,0,1:T(8,128)} %add.401), channel_id=1, source_target_pairs={{0,120},{8,0},{16,8},{24,16},{32,24},{40,32},{48,40},{56,48},{64,5... | collective-permute-start | bytes 393224 | tf_op jit(solution)/shard_map/while/body/eval_jaxpr/ppermute | solution.py:40
  439.4 8.9 collective-permute-start.2
  450.5 19.8 %collective-permute-start = (bf16[128,2,128]{2,0,1:T(8,128)(2,1)}, bf16[128,2,128]{2,0,1:T(8,128)(2,1)}, u32[]{:S(2)}, u32[]{:S(2)}) collective-permute-start(bf16[128,2,128]{2,0,1:T(8,128)(2,1)} %copy.397), channel_id=1, source_target_pairs={{0,120},{8,0},{16,8},{24,16},{32,24},{40,32},{48,40},{56,48},{64,5... | collective-permute-start | bytes 196616 | tf_op jit(solution)/shard_map/while/body/eval_jaxpr/ppermute | solution.py:40
  457.6 12.6 %collective-permute-start.1 = (bf16[128,2,128]{2,0,1:T(8,128)(2,1)}, bf16[128,2,128]{2,0,1:T(8,128)(2,1)}, u32[]{:S(2)}, u32[]{:S(2)}) collective-permute-start(bf16[128,2,128]{2,0,1:T(8,128)(2,1)} %copy.398), channel_id=1, source_target_pairs={{0,120},{8,0},{16,8},{24,16},{32,24},{40,32},{48,40},{56,48},{64,5... | collective-permute-start | bytes 196616 | tf_op jit(solution)/shard_map/while/body/eval_jaxpr/ppermute | solution.py:40
  460.4 12.1 %collective-permute-start.3 = (f32[128,2,128]{2,0,1:T(8,128)}, f32[128,2,128]{2,0,1:T(8,128)S(1)}, u32[]{:S(2)}, u32[]{:S(2)}) collective-permute-start(f32[128,2,128]{2,0,1:T(8,128)} %add.401), channel_id=1, source_target_pairs={{0,120},{8,0},{16,8},{24,16},{32,24},{40,32},{48,40},{56,48},{64,5... | collective-permute-start | bytes 393224 | tf_op jit(solution)/shard_map/while/body/eval_jaxpr/ppermute | solution.py:40
  467.9 8.8 collective-permute-start.2
  478.8 19.8 %collective-permute-start = (bf16[128,2,128]{2,0,1:T(8,128)(2,1)}, bf16[128,2,128]{2,0,1:T(8,128)(2,1)}, u32[]{:S(2)}, u32[]{:S(2)}) collective-permute-start(bf16[128,2,128]{2,0,1:T(8,128)(2,1)} %copy.397), channel_id=1, source_target_pairs={{0,120},{8,0},{16,8},{24,16},{32,24},{40,32},{48,40},{56,48},{64,5... | collective-permute-start | bytes 196616 | tf_op jit(solution)/shard_map/while/body/eval_jaxpr/ppermute | solution.py:40
  486.0 12.6 %collective-permute-start.1 = (bf16[128,2,128]{2,0,1:T(8,128)(2,1)}, bf16[128,2,128]{2,0,1:T(8,128)(2,1)}, u32[]{:S(2)}, u32[]{:S(2)}) collective-permute-start(bf16[128,2,128]{2,0,1:T(8,128)(2,1)} %copy.398), channel_id=1, source_target_pairs={{0,120},{8,0},{16,8},{24,16},{32,24},{40,32},{48,40},{56,48},{64,5... | collective-permute-start | bytes 196616 | tf_op jit(solution)/shard_map/while/body/eval_jaxpr/ppermute | solution.py:40
  488.7 12.0 %collective-permute-start.3 = (f32[128,2,128]{2,0,1:T(8,128)}, f32[128,2,128]{2,0,1:T(8,128)S(1)}, u32[]{:S(2)}, u32[]{:S(2)}) collective-permute-start(f32[128,2,128]{2,0,1:T(8,128)} %add.401), channel_id=1, source_target_pairs={{0,120},{8,0},{16,8},{24,16},{32,24},{40,32},{48,40},{56,48},{64,5... | collective-permute-start | bytes 393224 | tf_op jit(solution)/shard_map/while/body/eval_jaxpr/ppermute | solution.py:40
  496.2 8.7 collective-permute-start.2
  507.0 19.8 %collective-permute-start = (bf16[128,2,128]{2,0,1:T(8,128)(2,1)}, bf16[128,2,128]{2,0,1:T(8,128)(2,1)}, u32[]{:S(2)}, u32[]{:S(2)}) collective-permute-start(bf16[128,2,128]{2,0,1:T(8,128)(2,1)} %copy.397), channel_id=1, source_target_pairs={{0,120},{8,0},{16,8},{24,16},{32,24},{40,32},{48,40},{56,48},{64,5... | collective-permute-start | bytes 196616 | tf_op jit(solution)/shard_map/while/body/eval_jaxpr/ppermute | solution.py:40
  514.2 12.6 %collective-permute-start.1 = (bf16[128,2,128]{2,0,1:T(8,128)(2,1)}, bf16[128,2,128]{2,0,1:T(8,128)(2,1)}, u32[]{:S(2)}, u32[]{:S(2)}) collective-permute-start(bf16[128,2,128]{2,0,1:T(8,128)(2,1)} %copy.398), channel_id=1, source_target_pairs={{0,120},{8,0},{16,8},{24,16},{32,24},{40,32},{48,40},{56,48},{64,5... | collective-permute-start | bytes 196616 | tf_op jit(solution)/shard_map/while/body/eval_jaxpr/ppermute | solution.py:40
  517.0 11.9 %collective-permute-start.3 = (f32[128,2,128]{2,0,1:T(8,128)}, f32[128,2,128]{2,0,1:T(8,128)S(1)}, u32[]{:S(2)}, u32[]{:S(2)}) collective-permute-start(f32[128,2,128]{2,0,1:T(8,128)} %add.401), channel_id=1, source_target_pairs={{0,120},{8,0},{16,8},{24,16},{32,24},{40,32},{48,40},{56,48},{64,5... | collective-permute-start | bytes 393224 | tf_op jit(solution)/shard_map/while/body/eval_jaxpr/ppermute | solution.py:40
  524.5 8.6 collective-permute-start.2
  535.2 19.7 %collective-permute-start = (bf16[128,2,128]{2,0,1:T(8,128)(2,1)}, bf16[128,2,128]{2,0,1:T(8,128)(2,1)}, u32[]{:S(2)}, u32[]{:S(2)}) collective-permute-start(bf16[128,2,128]{2,0,1:T(8,128)(2,1)} %copy.397), channel_id=1, source_target_pairs={{0,120},{8,0},{16,8},{24,16},{32,24},{40,32},{48,40},{56,48},{64,5... | collective-permute-start | bytes 196616 | tf_op jit(solution)/shard_map/while/body/eval_jaxpr/ppermute | solution.py:40
  542.4 12.6 %collective-permute-start.1 = (bf16[128,2,128]{2,0,1:T(8,128)(2,1)}, bf16[128,2,128]{2,0,1:T(8,128)(2,1)}, u32[]{:S(2)}, u32[]{:S(2)}) collective-permute-start(bf16[128,2,128]{2,0,1:T(8,128)(2,1)} %copy.398), channel_id=1, source_target_pairs={{0,120},{8,0},{16,8},{24,16},{32,24},{40,32},{48,40},{56,48},{64,5... | collective-permute-start | bytes 196616 | tf_op jit(solution)/shard_map/while/body/eval_jaxpr/ppermute | solution.py:40
  545.1 11.8 %collective-permute-start.3 = (f32[128,2,128]{2,0,1:T(8,128)}, f32[128,2,128]{2,0,1:T(8,128)S(1)}, u32[]{:S(2)}, u32[]{:S(2)}) collective-permute-start(f32[128,2,128]{2,0,1:T(8,128)} %add.401), channel_id=1, source_target_pairs={{0,120},{8,0},{16,8},{24,16},{32,24},{40,32},{48,40},{56,48},{64,5... | collective-permute-start | bytes 393224 | tf_op jit(solution)/shard_map/while/body/eval_jaxpr/ppermute | solution.py:40
  552.6 8.6 collective-permute-start.2
  563.3 19.7 %collective-permute-start = (bf16[128,2,128]{2,0,1:T(8,128)(2,1)}, bf16[128,2,128]{2,0,1:T(8,128)(2,1)}, u32[]{:S(2)}, u32[]{:S(2)}) collective-permute-start(bf16[128,2,128]{2,0,1:T(8,128)(2,1)} %copy.397), channel_id=1, source_target_pairs={{0,120},{8,0},{16,8},{24,16},{32,24},{40,32},{48,40},{56,48},{64,5... | collective-permute-start | bytes 196616 | tf_op jit(solution)/shard_map/while/body/eval_jaxpr/ppermute | solution.py:40
  570.5 12.6 %collective-permute-start.1 = (bf16[128,2,128]{2,0,1:T(8,128)(2,1)}, bf16[128,2,128]{2,0,1:T(8,128)(2,1)}, u32[]{:S(2)}, u32[]{:S(2)}) collective-permute-start(bf16[128,2,128]{2,0,1:T(8,128)(2,1)} %copy.398), channel_id=1, source_target_pairs={{0,120},{8,0},{16,8},{24,16},{32,24},{40,32},{48,40},{56,48},{64,5... | collective-permute-start | bytes 196616 | tf_op jit(solution)/shard_map/while/body/eval_jaxpr/ppermute | solution.py:40
  573.2 11.8 %collective-permute-start.3 = (f32[128,2,128]{2,0,1:T(8,128)}, f32[128,2,128]{2,0,1:T(8,128)S(1)}, u32[]{:S(2)}, u32[]{:S(2)}) collective-permute-start(f32[128,2,128]{2,0,1:T(8,128)} %add.401), channel_id=1, source_target_pairs={{0,120},{8,0},{16,8},{24,16},{32,24},{40,32},{48,40},{56,48},{64,5... | collective-permute-start | bytes 393224 | tf_op jit(solution)/shard_map/while/body/eval_jaxpr/ppermute | solution.py:40
  580.7 8.6 collective-permute-start.2
  591.4 19.6 %collective-permute-start = (bf16[128,2,128]{2,0,1:T(8,128)(2,1)}, bf16[128,2,128]{2,0,1:T(8,128)(2,1)}, u32[]{:S(2)}, u32[]{:S(2)}) collective-permute-start(bf16[128,2,128]{2,0,1:T(8,128)(2,1)} %copy.397), channel_id=1, source_target_pairs={{0,120},{8,0},{16,8},{24,16},{32,24},{40,32},{48,40},{56,48},{64,5... | collective-permute-start | bytes 196616 | tf_op jit(solution)/shard_map/while/body/eval_jaxpr/ppermute | solution.py:40
  598.5 12.6 %collective-permute-start.1 = (bf16[128,2,128]{2,0,1:T(8,128)(2,1)}, bf16[128,2,128]{2,0,1:T(8,128)(2,1)}, u32[]{:S(2)}, u32[]{:S(2)}) collective-permute-start(bf16[128,2,128]{2,0,1:T(8,128)(2,1)} %copy.398), channel_id=1, source_target_pairs={{0,120},{8,0},{16,8},{24,16},{32,24},{40,32},{48,40},{56,48},{64,5... | collective-permute-start | bytes 196616 | tf_op jit(solution)/shard_map/while/body/eval_jaxpr/ppermute | solution.py:40
  601.2 9.8 %collective-permute-start.3 = (f32[128,2,128]{2,0,1:T(8,128)}, f32[128,2,128]{2,0,1:T(8,128)S(1)}, u32[]{:S(2)}, u32[]{:S(2)}) collective-permute-start(f32[128,2,128]{2,0,1:T(8,128)} %add.401), channel_id=1, source_target_pairs={{0,120},{8,0},{16,8},{24,16},{32,24},{40,32},{48,40},{56,48},{64,5... | collective-permute-start | bytes 393224 | tf_op jit(solution)/shard_map/while/body/eval_jaxpr/ppermute | solution.py:40
  616.0 17.4 %collective-permute-start = (bf16[128,2,128]{2,0,1:T(8,128)(2,1)}, bf16[128,2,128]{2,0,1:T(8,128)(2,1)}, u32[]{:S(2)}, u32[]{:S(2)}) collective-permute-start(bf16[128,2,128]{2,0,1:T(8,128)(2,1)} %copy.397), channel_id=1, source_target_pairs={{0,120},{8,0},{16,8},{24,16},{32,24},{40,32},{48,40},{56,48},{64,5... | collective-permute-start | bytes 196616 | tf_op jit(solution)/shard_map/while/body/eval_jaxpr/ppermute | solution.py:40
  620.8 12.6 %collective-permute-start.1 = (bf16[128,2,128]{2,0,1:T(8,128)(2,1)}, bf16[128,2,128]{2,0,1:T(8,128)(2,1)}, u32[]{:S(2)}, u32[]{:S(2)}) collective-permute-start(bf16[128,2,128]{2,0,1:T(8,128)(2,1)} %copy.398), channel_id=1, source_target_pairs={{0,120},{8,0},{16,8},{24,16},{32,24},{40,32},{48,40},{56,48},{64,5... | collective-permute-start | bytes 196616 | tf_op jit(solution)/shard_map/while/body/eval_jaxpr/ppermute | solution.py:40
  623.6 9.8 %collective-permute-start.3 = (f32[128,2,128]{2,0,1:T(8,128)}, f32[128,2,128]{2,0,1:T(8,128)S(1)}, u32[]{:S(2)}, u32[]{:S(2)}) collective-permute-start(f32[128,2,128]{2,0,1:T(8,128)} %add.401), channel_id=1, source_target_pairs={{0,120},{8,0},{16,8},{24,16},{32,24},{40,32},{48,40},{56,48},{64,5... | collective-permute-start | bytes 393224 | tf_op jit(solution)/shard_map/while/body/eval_jaxpr/ppermute | solution.py:40
  638.3 18.1 %collective-permute-start = (bf16[128,2,128]{2,0,1:T(8,128)(2,1)}, bf16[128,2,128]{2,0,1:T(8,128)(2,1)}, u32[]{:S(2)}, u32[]{:S(2)}) collective-permute-start(bf16[128,2,128]{2,0,1:T(8,128)(2,1)} %copy.397), channel_id=1, source_target_pairs={{0,120},{8,0},{16,8},{24,16},{32,24},{40,32},{48,40},{56,48},{64,5... | collective-permute-start | bytes 196616 | tf_op jit(solution)/shard_map/while/body/eval_jaxpr/ppermute | solution.py:40
  643.8 12.6 %collective-permute-start.1 = (bf16[128,2,128]{2,0,1:T(8,128)(2,1)}, bf16[128,2,128]{2,0,1:T(8,128)(2,1)}, u32[]{:S(2)}, u32[]{:S(2)}) collective-permute-start(bf16[128,2,128]{2,0,1:T(8,128)(2,1)} %copy.398), channel_id=1, source_target_pairs={{0,120},{8,0},{16,8},{24,16},{32,24},{40,32},{48,40},{56,48},{64,5... | collective-permute-start | bytes 196616 | tf_op jit(solution)/shard_map/while/body/eval_jaxpr/ppermute | solution.py:40
  646.6 9.8 %collective-permute-start.3 = (f32[128,2,128]{2,0,1:T(8,128)}, f32[128,2,128]{2,0,1:T(8,128)S(1)}, u32[]{:S(2)}, u32[]{:S(2)}) collective-permute-start(f32[128,2,128]{2,0,1:T(8,128)} %add.401), channel_id=1, source_target_pairs={{0,120},{8,0},{16,8},{24,16},{32,24},{40,32},{48,40},{56,48},{64,5... | collective-permute-start | bytes 393224 | tf_op jit(solution)/shard_map/while/body/eval_jaxpr/ppermute | solution.py:40
  654.1 5.3 collective-permute-start.2
  661.5 18.5 %collective-permute-start = (bf16[128,2,128]{2,0,1:T(8,128)(2,1)}, bf16[128,2,128]{2,0,1:T(8,128)(2,1)}, u32[]{:S(2)}, u32[]{:S(2)}) collective-permute-start(bf16[128,2,128]{2,0,1:T(8,128)(2,1)} %copy.397), channel_id=1, source_target_pairs={{0,120},{8,0},{16,8},{24,16},{32,24},{40,32},{48,40},{56,48},{64,5... | collective-permute-start | bytes 196616 | tf_op jit(solution)/shard_map/while/body/eval_jaxpr/ppermute | solution.py:40
  667.4 12.6 %collective-permute-start.1 = (bf16[128,2,128]{2,0,1:T(8,128)(2,1)}, bf16[128,2,128]{2,0,1:T(8,128)(2,1)}, u32[]{:S(2)}, u32[]{:S(2)}) collective-permute-start(bf16[128,2,128]{2,0,1:T(8,128)(2,1)} %copy.398), channel_id=1, source_target_pairs={{0,120},{8,0},{16,8},{24,16},{32,24},{40,32},{48,40},{56,48},{64,5... | collective-permute-start | bytes 196616 | tf_op jit(solution)/shard_map/while/body/eval_jaxpr/ppermute | solution.py:40
  670.1 9.8 %collective-permute-start.3 = (f32[128,2,128]{2,0,1:T(8,128)}, f32[128,2,128]{2,0,1:T(8,128)S(1)}, u32[]{:S(2)}, u32[]{:S(2)}) collective-permute-start(f32[128,2,128]{2,0,1:T(8,128)} %add.401), channel_id=1, source_target_pairs={{0,120},{8,0},{16,8},{24,16},{32,24},{40,32},{48,40},{56,48},{64,5... | collective-permute-start | bytes 393224 | tf_op jit(solution)/shard_map/while/body/eval_jaxpr/ppermute | solution.py:40
  677.6 5.9 collective-permute-start.2
  685.6 17.9 %collective-permute-start = (bf16[128,2,128]{2,0,1:T(8,128)(2,1)}, bf16[128,2,128]{2,0,1:T(8,128)(2,1)}, u32[]{:S(2)}, u32[]{:S(2)}) collective-permute-start(bf16[128,2,128]{2,0,1:T(8,128)(2,1)} %copy.397), channel_id=1, source_target_pairs={{0,120},{8,0},{16,8},{24,16},{32,24},{40,32},{48,40},{56,48},{64,5... | collective-permute-start | bytes 196616 | tf_op jit(solution)/shard_map/while/body/eval_jaxpr/ppermute | solution.py:40
  690.9 12.6 %collective-permute-start.1 = (bf16[128,2,128]{2,0,1:T(8,128)(2,1)}, bf16[128,2,128]{2,0,1:T(8,128)(2,1)}, u32[]{:S(2)}, u32[]{:S(2)}) collective-permute-start(bf16[128,2,128]{2,0,1:T(8,128)(2,1)} %copy.398), channel_id=1, source_target_pairs={{0,120},{8,0},{16,8},{24,16},{32,24},{40,32},{48,40},{56,48},{64,5... | collective-permute-start | bytes 196616 | tf_op jit(solution)/shard_map/while/body/eval_jaxpr/ppermute | solution.py:40
  693.7 9.8 %collective-permute-start.3 = (f32[128,2,128]{2,0,1:T(8,128)}, f32[128,2,128]{2,0,1:T(8,128)S(1)}, u32[]{:S(2)}, u32[]{:S(2)}) collective-permute-start(f32[128,2,128]{2,0,1:T(8,128)} %add.401), channel_id=1, source_target_pairs={{0,120},{8,0},{16,8},{24,16},{32,24},{40,32},{48,40},{56,48},{64,5... | collective-permute-start | bytes 393224 | tf_op jit(solution)/shard_map/while/body/eval_jaxpr/ppermute | solution.py:40
  708.5 18.3 %collective-permute-start = (bf16[128,2,128]{2,0,1:T(8,128)(2,1)}, bf16[128,2,128]{2,0,1:T(8,128)(2,1)}, u32[]{:S(2)}, u32[]{:S(2)}) collective-permute-start(bf16[128,2,128]{2,0,1:T(8,128)(2,1)} %copy.397), channel_id=1, source_target_pairs={{0,120},{8,0},{16,8},{24,16},{32,24},{40,32},{48,40},{56,48},{64,5... | collective-permute-start | bytes 196616 | tf_op jit(solution)/shard_map/while/body/eval_jaxpr/ppermute | solution.py:40
  714.2 12.6 %collective-permute-start.1 = (bf16[128,2,128]{2,0,1:T(8,128)(2,1)}, bf16[128,2,128]{2,0,1:T(8,128)(2,1)}, u32[]{:S(2)}, u32[]{:S(2)}) collective-permute-start(bf16[128,2,128]{2,0,1:T(8,128)(2,1)} %copy.398), channel_id=1, source_target_pairs={{0,120},{8,0},{16,8},{24,16},{32,24},{40,32},{48,40},{56,48},{64,5... | collective-permute-start | bytes 196616 | tf_op jit(solution)/shard_map/while/body/eval_jaxpr/ppermute | solution.py:40
  716.9 9.8 %collective-permute-start.3 = (f32[128,2,128]{2,0,1:T(8,128)}, f32[128,2,128]{2,0,1:T(8,128)S(1)}, u32[]{:S(2)}, u32[]{:S(2)}) collective-permute-start(f32[128,2,128]{2,0,1:T(8,128)} %add.401), channel_id=1, source_target_pairs={{0,120},{8,0},{16,8},{24,16},{32,24},{40,32},{48,40},{56,48},{64,5... | collective-permute-start | bytes 393224 | tf_op jit(solution)/shard_map/while/body/eval_jaxpr/ppermute | solution.py:40
  731.2 14.7 %collective-permute-start.8 = (bf16[128,2,128]{2,0,1:T(8,128)(2,1)S(1)}, bf16[128,2,128]{2,0,1:T(8,128)(2,1)S(1)}, u32[]{:S(2)}, u32[]{:S(2)}) collective-permute-start(bf16[128,2,128]{2,0,1:T(8,128)(2,1)S(1)} %add_convert_fusion.2), channel_id=1, source_target_pairs={{0,120},{8,0},{16,8},{24,16},{32,24},{40,32},{48,40},{56,48},{64,5... | collective-permute-start | bytes 196616 | tf_op jit(solution)/shard_map/ppermute | solution.py:40
  754.0 12.3 %collective-permute-start.6 = (bf16[3,4096]{1,0:T(4,128)(2,1)}, bf16[3,4096]{1,0:T(4,128)(2,1)}, u32[]{:S(2)}, u32[]{:S(2)}) collective-permute-start(bf16[3,4096]{1,0:T(4,128)(2,1)} %slice.179), channel_id=1, source_target_pairs={{8,0},{16,8},{24,16},{32,24},{40,32},{48,40},{56,48},{64,56},{72,6... | collective-permute-start | bytes 73736 | tf_op jit(solution)/shard_map/ppermute | solution.py:19
  784.2 116.6 %collective-permute-start.7 = (bf16[3,2,256]{0,2,1:T(8,128)(2,1)S(1)}, bf16[3,2,256]{0,2,1:T(8,128)(2,1)S(1)}, u32[]{:S(2)}, u32[]{:S(2)}) collective-permute-start(bf16[3,2,256]{0,2,1:T(8,128)(2,1)S(1)} %slice.182), channel_id=1, source_target_pairs={{8,0},{16,8},{24,16},{32,24},{40,32},{48,40},{56,48},{64,56},{72,6... | collective-permute-start | bytes 9224 | tf_op jit(solution)/shard_map/ppermute | solution.py:19
  (104 other events, 1686.6 us)
Sparse Core Ops, SparseCore 0:
  30.6 199.0 all-gather.11
  232.4 42.9 all-gather.7
  278.1 42.6 all-gather.9
  322.7 269.9 all-gather.13
where the time goes:
time: 919 us; the launch traced here: 909 us
  waiting for transfers between devices  255 us (28%)
  starting transfers between devices  178 us (19%)
  other arithmetic  148 us (16%)
  blocking collectives  139 us (15%)
  local copies, waits for them, and re-layouts  116 us (13%)
  matrix products  43.1 us (5%)
  between operations  17.1 us (2%)
  loops' own time  11.9 us (1%)
    ppermute x62, starting transfers between devices, from_behind_2(): lax.ppermute(x, axis, [(i, (i + by) % devices) for i in range(devices)])  169 us
    all_gather x2, waiting for transfers between devices, entering(): gathered = jax.tree.map(lambda a: lax.all_gather(a, axis), part)  165 us
    psum x1, blocking collectives, shards(): lax.psum(grad_wx.astype(jnp.bfloat16), 'ctx').astype(jnp.float32)  114 us
    ppermute x62, waiting for transfers between devices, from_behind_2(): lax.ppermute(x, axis, [(i, (i + by) % devices) for i in range(devices)])  77 us
    while x60, local copies, waits for them, and re-layouts  53.9 us
    add x15, other arithmetic, cycle_turn(): q_sums[set_index] + q_parts[set_index]  33.6 us
    add x30, other arithmetic, cycle_turn(): k_sum, v_sum = from_behind_2((k_sum + grad_k, v_sum + grad_v), 'ctx', -1)  33.5 us
    add x15, other arithmetic, combine(): later[0][..., None, None] * earlier[1] + later[1]  29.6 us
  transfers between devices with their start and end apart: 70, of which 26 were waited for; matrix products, arithmetic and copies ran while one was open for 30% of the time, Pallas kernels for 0%

commit v1 on v0

v1 whole, which is shorter than its diff:
```python
import jax
import jax.numpy as jnp
from jax import lax
from jax.experimental import pallas as pl
from jax.experimental.pallas import tpu as pltpu
from jax.sharding import PartitionSpec as P

F32 = jnp.float32
BF16 = jnp.bfloat16
HD = 128
BLK = 128
TAPS = 4
BACK = 8
LOG2E = 1.4426950408889634
NEG_BIG = -1e30
HIGHEST = lax.Precision.HIGHEST


def dot_nn(a, b, precision=None):
    return lax.dot_general(
        a, b, (((1,), (0,)), ((), ())), precision=precision, preferred_element_type=F32
    )


def dot_nt(a, b):
    return lax.dot_general(a, b, (((1,), (1,)), ((), ())), preferred_element_type=F32)


def dot_tn(a, b):
    return lax.dot_general(a, b, (((0,), (0,)), ((), ())), preferred_element_type=F32)


def doc_bounds(doc_ref):
    s1 = doc_ref[0]
    s2 = s1 + doc_ref[1]
    s3 = s2 + doc_ref[2]
    return s1, s2, s3


def start_at(pos, bounds):
    s1, s2, s3 = bounds
    return jnp.where(pos >= s3, s3, jnp.where(pos >= s2, s2, jnp.where(pos >= s1, s1, 0)))


def next_start(pos, bounds, total):
    s1, s2, s3 = bounds
    return jnp.where(pos < s1, s1, jnp.where(pos < s2, s2, jnp.where(pos < s3, s3, total)))


def twice(a):
    return jnp.concatenate([a, a], axis=1)


def fold_rows(a):
    return jnp.sum(a.reshape(a.shape[0] // 8, 8, a.shape[1]), axis=0)


def ssm_kernel(
    doc_ref, idx_ref, rate_ref, r_ref, wx_ref, wbc_ref, out_ref,
    xs_s, xp_s, b_s, c_s, dsx_s, dsbc_s, st_s, ds_s,
    cols_s, elt_s, rx_s, ry_s, es_s, tapx_s, tapbc_s,
):
    blocks = r_ref.shape[0]
    total = blocks * BLK
    place = idx_ref[0]
    bounds = doc_bounds(doc_ref)
    rate0 = rate_ref[2 * place]
    rate1 = rate_ref[2 * place + 1]
    group = place // (blocks // 2)
    wx = wx_ref[:, pl.ds(pl.multiple_of(place * 256, 256), 256)]
    wbc = jnp.concatenate(
        [
            wbc_ref[:, pl.ds(pl.multiple_of(group * 128, 128), 128)],
            wbc_ref[:, pl.ds(pl.multiple_of(256 + group * 128, 128), 128)],
        ],
        axis=1,
    )

    raw = jnp.concatenate(
        [
            jnp.sum(r_ref[c, 3 * BLK : 3 * BLK + 16, :].astype(F32), axis=0, keepdims=True)
            for c in range(blocks)
        ],
        axis=0,
    )
    raw = jnp.concatenate([raw[:, :128], raw[:, 128:]], axis=0)
    step = jnp.log(1.0 + jnp.exp(raw))
    sig = 1.0 / (1.0 + jnp.exp(-raw))
    row_ids = lax.broadcasted_iota(jnp.int32, (2 * blocks, 128), 0)
    rate = jnp.where(row_ids < blocks, rate0, rate1)
    ii = lax.broadcasted_iota(jnp.int32, (128, 128), 0)
    jj = lax.broadcasted_iota(jnp.int32, (128, 128), 1)
    cum = dot_nn(-step * rate, (ii <= jj).astype(F32), HIGHEST)
    u_rows = step * jnp.exp(-cum)
    v_rows = jnp.exp(cum)
    last = jnp.broadcast_to(v_rows[:, 127:128], (2 * blocks, 128))
    for c in range(blocks):
        cols_s[c] = jnp.concatenate(
            [
                u_rows[c : c + 1], u_rows[blocks + c : blocks + c + 1],
                v_rows[c : c + 1], v_rows[blocks + c : blocks + c + 1],
                jnp.zeros((4, 128), F32),
            ],
            axis=0,
        )
        elt_s[c] = jnp.broadcast_to(
            jnp.concatenate([last[c : c + 1], last[blocks + c : blocks + c + 1]], axis=1), (8, 256)
        )

    edge = jnp.zeros((8, 256), F32)
    st_s[0] = jnp.zeros((128, 256), F32)

    def columns(c, first):
        cols = cols_s[c].T
        return jnp.concatenate(
            [jnp.broadcast_to(cols[:, first + h : first + h + 1], (128, 128)) for h in (0, 1)],
            axis=1,
        )

    def conv(edge, value, weight, keeps):
        win = jnp.concatenate([edge, value], axis=0)
        pre = value * weight[TAPS - 1 : TAPS]
        for d in range(1, TAPS):
            pre = pre + jnp.where(keeps[d - 1], win[8 - d : 8 - d + BLK], 0.0) * weight[TAPS - 1 - d : TAPS - d]
        sg = 1.0 / (1.0 + jnp.exp(-pre))
        val = pre * sg
        return val, sg + val * (1.0 - sg)

    def forward(c, carry):
        base = pl.multiple_of(c * BLK, BLK)
        edge_x, edge_bc = carry
        x = r_ref[c, 0:BLK].astype(F32)
        bc_raw = r_ref[c, 2 * BLK : 3 * BLK].astype(F32)
        pos = base + ii
        dist = twice(pos - start_at(pos, bounds))
        keeps = [dist >= d for d in range(1, TAPS)]
        xs, dsx = conv(edge_x, x, wx, keeps)
        bc, dsbc = conv(edge_bc, bc_raw, wbc, keeps)
        xs_s[c] = xs
        dsx_s[c] = dsx
        dsbc_s[c] = dsbc
        b = bc[:, :128].astype(BF16)
        b_s[c] = b
        c_s[c] = bc[:, 128:].astype(BF16)
        xp = xs * columns(c, 0)
        xp_s[c] = xp.astype(BF16)
        last_start = start_at(base + BLK - 1, bounds)
        xpm = jnp.where(twice(pos) >= last_start, xp, 0.0).astype(BF16)
        elt = elt_s[c][0:1]
        keep = jnp.where(last_start < base, elt, 0.0)
        st_s[c + 1] = keep * st_s[c] + elt * dot_tn(b, xpm)
        return x[BLK - 8 :], bc_raw[BLK - 8 :]

    lax.fori_loop(0, blocks, forward, (edge, edge))

    ds_s[...] = jnp.zeros((128, 256), F32)
    tapx_s[...] = jnp.zeros((TAPS, 8, 256), F32)
    tapbc_s[...] = jnp.zeros((TAPS, 8, 256), F32)
    lane2 = lax.broadcasted_iota(jnp.int32, (16, 256), 1)
    row2 = lax.broadcasted_iota(jnp.int32, (16, 256), 0)
    pick = (lane2 // 128 == row2).astype(BF16)

    def head_sums(a):
        hi = a.astype(BF16)
        lo = (a - hi.astype(F32)).astype(BF16)
        return (dot_nt(pick, hi) + dot_nt(pick, lo))[0:8]

    def conv_back(grad, edge, raw_in, weight, ends, taps):
        win = jnp.concatenate([grad, edge], axis=0)
        total_grad = grad * weight[TAPS - 1 : TAPS]
        taps[TAPS - 1] += fold_rows(grad * raw_in)
        for d in range(1, TAPS):
            moved = jnp.where(ends[d - 1], win[d : d + BLK], 0.0)
            total_grad = total_grad + moved * weight[TAPS - 1 - d : TAPS - d]
            taps[TAPS - 1 - d] += fold_rows(moved * raw_in)
        return total_grad

    def backward(lap, carry):
        c = blocks - 1 - lap
        base = pl.multiple_of(c * BLK, BLK)
        pos = base + ii
        start = start_at(pos, bounds)
        last_start = start_at(base + BLK - 1, bounds)
        causal = (jj <= ii) & (base + jj >= start)
        leads = start < base
        tails = pos >= last_start
        b = b_s[c]
        cc = c_s[c]
        xp = xp_s[c]
        xs = xs_s[c]
        g = r_ref[c, BLK : 2 * BLK].astype(F32)
        u = columns(c, 0)
        v = columns(c, 2)
        gv = g * v
        gp = gv.astype(BF16)
        elt = elt_s[c][0:1]
        ds = ds_s[...]
        es_s[c] = fold_rows(ds * st_s[c + 1])
        sb = st_s[c].astype(BF16)
        ds_e = elt * ds
        dsb = ds_e.astype(BF16)
        w = jnp.where(causal, dot_nt(cc, b), 0.0).astype(BF16)
        cm = jnp.where(leads, cc.astype(F32), 0.0).astype(BF16)
        bm = jnp.where(tails, b.astype(F32), 0.0).astype(BF16)
        yv = dot_nn(w, xp) + dot_nn(cm, sb)
        dxp = dot_tn(w, gp) + dot_nn(bm, dsb)
        z = jnp.where(causal, dot_nt(gp, xp), 0.0).astype(BF16)
        dc = dot_nn(z, b) + jnp.where(leads, dot_nt(gp, sb), 0.0)
        db = dot_tn(z, cc) + jnp.where(tails, dot_nt(xp, dsb), 0.0)
        ds_s[...] = jnp.where(last_start < base, ds_e, 0.0) + dot_tn(cm, gp)
        dx = u * dxp
        rx_s[c] = head_sums(xs * dx)
        ry_s[c] = head_sums(gv * yv)
        left = twice(next_start(pos, bounds, total) - pos)
        ends = [left > d for d in range(1, TAPS)]
        edge_x, edge_bc = carry
        pre_x = dx * dsx_s[c]
        pre_bc = jnp.concatenate([db, dc], axis=1) * dsbc_s[c]
        x = r_ref[c, 0:BLK].astype(F32)
        bc_raw = r_ref[c, 2 * BLK : 3 * BLK].astype(F32)
        out_ref[c, 0:BLK] = conv_back(pre_x, edge_x, x, wx, ends, tapx_s).astype(BF16)
        out_ref[c, BLK : 2 * BLK] = conv_back(
            pre_bc, edge_bc, bc_raw, wbc, ends, tapbc_s
        ).astype(BF16)
        return pre_x[0:8], pre_bc[0:8]

    lax.fori_loop(0, blocks, backward, (edge, edge))

    xdx = jnp.concatenate([rx_s[c][h : h + 1] for h in (0, 1) for c in range(blocks)], axis=0)
    gyy = jnp.concatenate([ry_s[c][h : h + 1] for h in (0, 1) for c in range(blocks)], axis=0)
    ends = jnp.concatenate(
        [
            jnp.sum(es_s[c][:, 128 * h : 128 * h + 128], axis=0, keepdims=True)
            for h in (0, 1)
            for c in range(blocks)
        ],
        axis=0,
    )
    d_log = dot_nn(gyy - xdx, (ii >= jj).astype(F32), HIGHEST) + jnp.sum(ends, axis=1, keepdims=True)
    d_raw = (xdx / step - rate * d_log) * sig
    d_raw = jnp.concatenate([d_raw[:blocks], d_raw[blocks:]], axis=1)
    raw_hi = d_raw.astype(BF16).astype(F32)
    raw_lo = d_raw - raw_hi
    tapx = jnp.concatenate([jnp.sum(tapx_s[k], axis=0, keepdims=True) for k in range(TAPS)], axis=0)
    tapbc = jnp.concatenate([jnp.sum(tapbc_s[k], axis=0, keepdims=True) for k in range(TAPS)], axis=0)
    tapx_hi = tapx.astype(BF16).astype(F32)
    rest = jnp.concatenate([tapx_hi, tapx - tapx_hi, tapbc, jnp.zeros((2, 256), F32)], axis=0)
    for c in range(blocks):
        out_ref[c, 2 * BLK : 2 * BLK + 16] = jnp.concatenate(
            [raw_hi[c : c + 1], raw_lo[c : c + 1], rest], axis=0
        ).astype(BF16)


def ssm_core(doc_lengths, place, rate, received, weight_x, weight_bc):
    blocks = received.shape[0]
    smem = pl.BlockSpec(memory_space=pltpu.SMEM)
    vmem = pl.BlockSpec(memory_space=pltpu.VMEM)

    def scratch(*shape, dtype=F32):
        return pltpu.VMEM(shape, dtype)

    return pl.pallas_call(
        ssm_kernel,
        out_shape=jax.ShapeDtypeStruct((blocks, 2 * BLK + 16, 256), BF16),
        in_specs=[smem, smem, smem, vmem, vmem, vmem],
        out_specs=vmem,
        scratch_shapes=[
            scratch(blocks, BLK, 256),
            scratch(blocks, BLK, 256, dtype=BF16),
            scratch(blocks, BLK, 128, dtype=BF16),
            scratch(blocks, BLK, 128, dtype=BF16),
            scratch(blocks, BLK, 256),
            scratch(blocks, BLK, 256),
            scratch(blocks + 1, 128, 256),
            scratch(128, 256),
            scratch(blocks, 8, 128),
            scratch(blocks, 8, 256),
            scratch(blocks, 8, 128),
            scratch(blocks, 8, 128),
            scratch(blocks, 8, 256),
            scratch(TAPS, 8, 256),
            scratch(TAPS, 8, 256),
        ],
        compiler_params=pltpu.CompilerParams(vmem_limit_bytes=56 * 2**20),
        cost_estimate=pl.CostEstimate(flops=3 * 10**9, bytes_accessed=6 * 2**20, transcendentals=4 * 10**6),
        name="mixer",
    )(doc_lengths, place, rate, received, weight_x, weight_bc)


def attention_kernel(doc_ref, r_ref, out_ref, kpad, vpad, ktpad, dk_s, dv_s, s_s, p_s):
    blocks = r_ref.shape[0]
    bounds = doc_bounds(doc_ref)
    scale = HD ** (-0.5)
    reach = BACK + 2
    kpad[0:BACK] = jnp.zeros((BACK, BLK, HD), BF16)
    vpad[0:BACK] = jnp.zeros((BACK, BLK, HD), BF16)
    ktpad[0:BACK] = jnp.zeros((BACK, HD, BLK), BF16)
    dk_s[...] = jnp.zeros(dk_s.shape, F32)
    dv_s[...] = jnp.zeros(dv_s.shape, F32)

    def fill(c, carry):
        k = r_ref[c, 2 * BLK : 3 * BLK]
        kpad[BACK + c] = k
        vpad[BACK + c] = r_ref[c, 3 * BLK : 4 * BLK]
        ktpad[BACK + c] = k.T
        return carry

    lax.fori_loop(0, blocks, fill, 0)
    jrow = lax.broadcasted_iota(jnp.int32, (BLK, 2 * BLK), 0)
    icol = lax.broadcasted_iota(jnp.int32, (BLK, 2 * BLK), 1)

    def rows8(a):
        return a.reshape(BLK // 8, 8, 2 * BLK)

    def turn(i, carry):
        q = jnp.concatenate([r_ref[2 * i, 0:BLK], r_ref[2 * i + 1, 0:BLK]], axis=0)
        do = jnp.concatenate([r_ref[2 * i, BLK : 2 * BLK], r_ref[2 * i + 1, BLK : 2 * BLK]], axis=0)
        first = (2 * i - BACK) * BLK
        ipos = 2 * i * BLK + icol
        start = start_at(ipos, bounds)
        top = jnp.full((8, 2 * BLK), NEG_BIG, F32)
        for b in range(reach):
            jpos = first + b * BLK + jrow
            allowed = jpos >= start
            if b >= BACK:
                allowed = allowed & (jpos <= ipos)
            s = jnp.where(allowed, dot_nt(kpad[2 * i + b], q), NEG_BIG)
            s_s[b] = s
            top = jnp.maximum(top, jnp.max(rows8(s), axis=0))
            p_s[b] = dot_nt(vpad[2 * i + b], do)
        top = jnp.max(top, axis=0, keepdims=True) * (scale * LOG2E)
        norm = jnp.zeros((8, 2 * BLK), F32)
        mean = jnp.zeros((8, 2 * BLK), F32)
        for b in range(reach):
            e = jnp.exp2(s_s[b] * (scale * LOG2E) - top)
            s_s[b] = e
            norm = norm + jnp.sum(rows8(e), axis=0)
            mean = mean + jnp.sum(rows8(e * p_s[b]), axis=0)
        inverse = 1.0 / jnp.sum(norm, axis=0, keepdims=True)
        mean = jnp.sum(mean, axis=0, keepdims=True) * inverse
        dqt = jnp.zeros((HD, 2 * BLK), F32)
        for b in range(reach):
            prob = s_s[b] * inverse
            grad = (prob * (p_s[b] - mean)).astype(BF16)
            dv_s[2 * i + b] += dot_nn(prob.astype(BF16), do)
            dk_s[2 * i + b] += dot_nn(grad, q)
            dqt = dqt + dot_nn(ktpad[2 * i + b], grad)
        dqt = dqt * scale
        out_ref[2 * i, 0:BLK] = dqt[:, :BLK].T.astype(BF16)
        out_ref[2 * i + 1, 0:BLK] = dqt[:, BLK:].T.astype(BF16)
        return carry

    lax.fori_loop(0, blocks // 2, turn, 0)

    def drain(c, carry):
        out_ref[c, BLK : 2 * BLK] = (dk_s[BACK + c] * scale).astype(BF16)
        out_ref[c, 2 * BLK : 3 * BLK] = dv_s[BACK + c].astype(BF16)
        return carry

    lax.fori_loop(0, blocks, drain, 0)


def attention_core(doc_lengths, received):
    blocks = received.shape[0]
    smem = pl.BlockSpec(memory_space=pltpu.SMEM)
    vmem = pl.BlockSpec(memory_space=pltpu.VMEM)
    padded = blocks + BACK
    return pl.pallas_call(
        attention_kernel,
        out_shape=jax.ShapeDtypeStruct((blocks, 3 * BLK, HD), BF16),
        in_specs=[smem, vmem],
        out_specs=vmem,
        scratch_shapes=[
            pltpu.VMEM((padded, BLK, HD), BF16),
            pltpu.VMEM((padded, BLK, HD), BF16),
            pltpu.VMEM((padded, HD, BLK), BF16),
            pltpu.VMEM((padded, BLK, HD), F32),
            pltpu.VMEM((padded, BLK, HD), F32),
            pltpu.VMEM((BACK + 2, BLK, 2 * BLK), F32),
            pltpu.VMEM((BACK + 2, BLK, 2 * BLK), F32),
        ],
        compiler_params=pltpu.CompilerParams(vmem_limit_bytes=40 * 2**20),
        cost_estimate=pl.CostEstimate(flops=4 * 10**9, bytes_accessed=4 * 2**20, transcendentals=3 * 10**6),
        name="attention",
    )(doc_lengths, received)


def swap(a):
    return lax.all_to_all(a, "ctx", 0, 0, tiled=True)


def split3(a):
    hi = lax.reduce_precision(a, 8, 7)
    mid = lax.reduce_precision(a - hi, 8, 7)
    return hi.astype(BF16), mid.astype(BF16), (a - hi - mid).astype(BF16)


def shards(
    x_in, bc_in, conv_x, conv_bc, dt_raw, rate, grad_ssd, query, key, value, d_out, doc_lengths
):
    ctx = lax.axis_size("ctx")
    rows = x_in.shape[0]
    place = lax.axis_index("ctx").astype(jnp.int32).reshape(1)

    def by_head(a, width):
        return a.reshape(rows, ctx, width).transpose(1, 0, 2)

    def by_group(a):
        two = a.reshape(rows, 2, HD).transpose(1, 0, 2)
        return jnp.repeat(two, ctx // 2, axis=0)

    bc_sent = bc_in.reshape(rows, 2, 2, HD).transpose(2, 0, 1, 3).reshape(2, rows, 2 * HD)
    dt_sent = jnp.stack(split3(dt_raw), axis=0).reshape(3, ctx, 2 * rows).transpose(1, 0, 2)
    sent = jnp.concatenate(
        [
            by_head(x_in, 2 * HD),
            by_head(grad_ssd, 2 * HD),
            jnp.repeat(bc_sent, ctx // 2, axis=0),
            jnp.pad(dt_sent, ((0, 0), (0, 13), (0, 0))),
        ],
        axis=1,
    )
    sent_attention = jnp.concatenate(
        [by_head(query, HD), by_head(d_out, HD), by_group(key), by_group(value)], axis=1
    )
    got = swap(sent)
    got_attention = swap(sent_attention)
    back = swap(
        ssm_core(doc_lengths, place, rate, got, conv_x, conv_bc.reshape(TAPS, 4 * HD))
    )
    back_attention = swap(attention_core(doc_lengths, got_attention))

    d_x = back[:, :rows].transpose(1, 0, 2).reshape(rows, ctx * 2 * HD)
    d_bc = jnp.sum(back[:, rows : 2 * rows].astype(F32).reshape(2, ctx // 2, rows, 2, HD), axis=1)
    d_bc = d_bc.transpose(1, 2, 0, 3).reshape(rows, 2, 2 * HD).astype(BF16)
    small = back[:, 2 * rows :].astype(F32)
    d_dt = (small[:, 0] + small[:, 1]).reshape(2 * ctx, rows)
    d_wx = (small[:, 2:6] + small[:, 6:10]).transpose(1, 0, 2).reshape(TAPS, ctx * 2 * HD)
    d_wbc = jnp.sum(small[:, 10:14].reshape(2, ctx // 2, TAPS, 2, HD), axis=1)
    d_wbc = d_wbc.transpose(1, 2, 0, 3).reshape(TAPS, 2, 2 * HD)
    d_query = back_attention[:, :rows].transpose(1, 0, 2).reshape(rows, ctx * HD)

    def group_sum(a):
        summed = jnp.sum(a.astype(F32).reshape(2, ctx // 2, rows, HD), axis=1)
        return summed.transpose(1, 0, 2).reshape(rows, 2 * HD).astype(BF16)

    d_key = group_sum(back_attention[:, rows : 2 * rows])
    d_value = group_sum(back_attention[:, 2 * rows :])
    return (d_x, d_bc, d_dt, d_wx, d_wbc, d_query, d_key, d_value)


def solution(mesh):
    tokens = P(("dp", "ctx"), "head")
    in_specs = (
        tokens,
        P(("dp", "ctx"), None, "head"),
        P(None, "head"),
        P(None, None, "head"),
        P("head", ("dp", "ctx")),
        P("head"),
        tokens,
        tokens,
        tokens,
        tokens,
        tokens,
        P("dp"),
    )
    out_specs = (
        tokens,
        P(("dp", "ctx"), None, "head"),
        P("head", ("dp", "ctx")),
        P("dp", "head"),
        P("dp", None, "head"),
        tokens,
        tokens,
        tokens,
    )
    return jax.shard_map(shards, mesh=mesh, in_specs=in_specs, out_specs=out_specs, check_vma=False)
```

time: 919 us -> 170 us (0.18); the launches traced: 909 us -> 170 us
  waiting for transfers between devices: 255 us -> 73.9 us
  starting transfers between devices: 178 us -> 22.5 us
  other arithmetic: 148 us -> 8.33 us
  blocking collectives: 139 us -> 0 us
  local copies, waits for them, and re-layouts: 116 us -> 24.3 us
  matrix products: 43.1 us -> 0 us
  Pallas kernels: 0 us -> 39.6 us
  between operations: 17.1 us -> 0.97 us
  loops' own time: 11.9 us -> 0 us
    all_gather x4 -> x0, waiting for transfers between devices: 178 us -> none  [the longest x2 165 us: entering(): gathered = jax.tree.map(lambda a: lax.all_gather(a, axis), part)]
    ppermute x66 -> x0, starting transfers between devices: 178 us -> none  [the longest x62 169 us: from_behind_2(): lax.ppermute(x, axis, [(i, (i + by) % devices) for i in range(devices)])]
    psum x1 -> x0, blocking collectives: 114 us -> none  [shards(): lax.psum(grad_wx.astype(jnp.bfloat16), 'ctx').astype(jnp.float32)]
    add x64 -> x1, other arithmetic: 98.6 us -> 0.62 us  [shards(): d_dt = (small[:, 0] + small[:, 1]).reshape(2 * ctx, rows)]
    ppermute x66 -> x0, waiting for transfers between devices: 77 us -> none  [the longest x62 77 us: from_behind_2(): lax.ppermute(x, axis, [(i, (i + by) % devices) for i in range(devices)])]
    all_to_all x0 -> x4, waiting for transfers between devices: none -> 73.9 us  [swap(): return lax.all_to_all(a, 'ctx', 0, 0, tiled=True)]
    while x60 -> x0, local copies, waits for them, and re-layouts: 53.9 us -> none
    dot_general x18 -> x0, matrix products: 43.1 us -> none  [the longest x3 11 us: block_terms(): jnp.einsum('ksge,ksgep,ksgn->kgepn', tail_decay, x_conv, b_matrix, precis...]
  transfers between devices with their start and end apart: 70 -> 4, of which waited for: 26 -> 3; matrix products, arithmetic and copies ran while one was open for 30% -> 10% of each run, Pallas kernels for 0% -> 23%
where the time goes in v1:
time: 170 us
  waiting for transfers between devices  73.9 us (43%)
  Pallas kernels  39.6 us (23%)
  local copies, waits for them, and re-layouts  24.3 us (14%)
  starting transfers between devices  22.5 us (13%)
  other arithmetic  8.33 us (5%)
    all_to_all x4, waiting for transfers between devices, swap(): return lax.all_to_all(a, 'ctx', 0, 0, tiled=True)  73.9 us
    pallas_call x1, Pallas kernels, ssm_core(): pl.pallas_call(ssm_kernel, out_shape=jax.ShapeDtypeStruct((blocks, 2 * BL...  23.3 us
    all_to_all x4, starting transfers between devices, swap(): return lax.all_to_all(a, 'ctx', 0, 0, tiled=True)  22.5 us
    pallas_call x1, Pallas kernels, attention_core(): pl.pallas_call(attention_kernel, out_shape=jax.ShapeDtypeStruct((blocks,...  16.3 us
    unnamed x29, local copies, waits for them, and re-layouts  13.9 us
    reshape x4, local copies, waits for them, and re-layouts, by_head(): return a.reshape(rows, ctx, width).transpose(1, 0, 2)  4.37 us
  transfers between devices with their start and end apart: 4, of which 3 were waited for; matrix products, arithmetic and copies ran while one was open for 10% of the time, Pallas kernels for 23%

profile of v1, /device:TPU:0, one launch (start us, length us, event | category | flops | bytes accessed | tf_op | source)
XLA Modules:
  0.0 169.6 jit_solution(8475653133831968487)
XLA Ops:
  0.6 0.0 copy-start.5
  0.6 0.0 copy-start.6
  0.7 1.3 copy.93
  2.0 0.3 copy.94
  2.3 1.3 copy.95
  3.6 0.3 copy.96
  3.9 0.0 copy-done.5
  4.0 0.0 copy-done.6
  4.0 0.1 broadcast_in_dim.10
  4.1 0.1 broadcast_in_dim.11
  4.2 0.0 copy-start.7
  4.2 0.0 copy-start.3
  4.2 1.5 pad_maximum_fusion
  5.8 7.1 %all-to-all-start.2 = ((bf16[16,512,128]{2,1,0:T(8,128)(2,1)}), bf16[16,512,128]{2,1,0:T(8,128)(2,1)S(1)}, u32[]{:S(2)}, u32[]{:S(2)}) async-start(bf16[16,512,128]{2,1,0:T(8,128)(2,1)} %pad_maximum_fusion), calls=%async_computation.2 | async-start | bytes 4194304 | tf_op jit(solution)/shard_map/all_to_all | solution.py:389
  12.9 0.0 copy-done.7
  13.0 0.0 copy-done.3
  13.0 1.3 copy.80
  14.3 0.0 copy-start.4
  14.3 1.5 copy.81
  15.8 2.3 %copy.82 = bf16[128,4096]{0,1:T(8,128)(2,1)} copy(bf16[128,4096]{1,0:T(8,128)(2,1)} %param.18) | data formatting | bytes 2097152 | tf_op args[6]
  18.1 2.3 %copy.83 = bf16[128,16,256]{2,0,1:T(8,128)(2,1)} copy(bf16[128,16,256]{0,2,1:T(8,128)(2,1)} %bitcast.53) | data formatting | bytes 2097152 | tf_op jit(solution)/shard_map/reshape | solution.py:406
  20.4 0.0 copy-done.4
  20.4 0.1 copy.84
  20.5 0.1 copy.86
  20.6 0.1 maximum_bitcast_fusion
  20.7 0.1 broadcast_in_dim.9
  20.8 2.9 %fusion.1 = bf16[16,400,256]{2,1,0:T(8,128)(2,1)} fusion(bf16[16,3,256]{2,1,0:T(4,128)(2,1)S(1)} %maximum_bitcast_fusion, bf16[16,128,256]{2,1,0:T(8,128)(2,1)S(1)} %bitcast.50, bf16[16,128,256]{2,1,0:T(8,128)(2,1)} %bitcast.49, bf16[16,128,256]{2,1,0:T(8,128)(2,1)S(1)} %bitcast.48), kind=kLoop, calls=%fused_computation.2 | loop fusion | flops 16384000 | bytes 6447104 | tf_op jit(solution)/shard_map/concatenate | solution.py:414
  23.7 0.0 copy-start.1
  23.7 20.9 %all-to-all-done.2.r_ref = bf16[16,512,128]{2,1,0:T(8,128)(2,1)S(1)} async-done(((bf16[16,512,128]{2,1,0:T(8,128)(2,1)}), bf16[16,512,128]{2,1,0:T(8,128)(2,1)S(1)}, u32[]{:S(2)}, u32[]{:S(2)}) %all-to-all-start.2) | async-done | bytes 2097184 | tf_op jit(solution)/shard_map/all_to_all | solution.py:389
  44.5 4.5 %all-to-all-start = ((bf16[16,400,256]{2,1,0:T(8,128)(2,1)}), bf16[16,400,256]{2,1,0:T(8,128)(2,1)}, u32[]{:S(2)}, u32[]{:S(2)}) async-start(bf16[16,400,256]{2,1,0:T(8,128)(2,1)} %fusion.1), calls=%async_computation | async-start | bytes 6553600 | tf_op jit(solution)/shard_map/all_to_all | solution.py:389
  49.1 0.0 copy-done.1
  49.1 0.0 copy-start.8
  49.1 16.3 %attention.1 = bf16[16,384,128]{2,1,0:T(8,128)(2,1)S(1)} custom-call(s32[4]{0:T(128)S(1)} %copy-done.1, bf16[16,512,128]{2,1,0:T(8,128)(2,1)S(1)} %all-to-all-done.2.r_ref), custom_call_target="tpu_custom_call" | custom-call | flops 4000000000 | bytes 4194304 | tf_op jit(solution)/shard_map/attention/pallas_call | solution.py:368
  65.4 0.0 copy-start
  65.4 1.1 copy-done
  66.5 28.4 %all-to-all-done.r_ref = bf16[16,400,256]{2,1,0:T(8,128)(2,1)} async-done(((bf16[16,400,256]{2,1,0:T(8,128)(2,1)}), bf16[16,400,256]{2,1,0:T(8,128)(2,1)}, u32[]{:S(2)}, u32[]{:S(2)}) %all-to-all-start) | async-done | bytes 3276832 | tf_op jit(solution)/shard_map/all_to_all | solution.py:389
  95.0 3.7 %all-to-all-start.3 = ((bf16[16,384,128]{2,1,0:T(8,128)(2,1)}), bf16[16,384,128]{2,1,0:T(8,128)(2,1)S(1)}, u32[]{:S(2)}, u32[]{:S(2)}) async-start(bf16[16,384,128]{2,1,0:T(8,128)(2,1)} %copy-done), calls=%async_computation.3 | async-start | bytes 3145728 | tf_op jit(solution)/shard_map/all_to_all | solution.py:389
  98.7 0.0 copy-done.8
  98.7 0.6 copy.108
  99.3 23.3 %mixer.1 = bf16[16,272,256]{2,1,0:T(8,128)(2,1)} custom-call(s32[4]{0:T(128)} %doc_ref.3, s32[1]{0:T(128)} %bitcast.idx_ref, f32[32]{0:T(128)} %rate_ref.1, bf16[16,400,256]{2,1,0:T(8,128)(2,1)} %all-to-all-done.r_ref, f32[4,4096]{1,0:T(4,128)} %wx_ref.1, f32[4,512]{1,0:T(4,128)} %bitcast.74), custom_call_target="tpu_custom_call" | custom-call | flops 3000000000 | bytes 6291456 | tf_op jit(solution)/shard_map/mixer/pallas_call | solution.py:262
  122.6 0.0 all-to-all-done.3
  122.6 0.0 copy-start.2
  122.6 1.2 copy-done.2
  123.7 7.2 %all-to-all-start.1 = ((bf16[16,272,256]{2,1,0:T(8,128)(2,1)}), bf16[16,272,256]{2,1,0:T(8,128)(2,1)S(1)}, u32[]{:S(2)}, u32[]{:S(2)}) async-start(bf16[16,272,256]{2,1,0:T(8,128)(2,1)} %mixer.1), calls=%async_computation.1 | async-start | bytes 4456448 | tf_op jit(solution)/shard_map/all_to_all | solution.py:389
  130.9 1.4 bitcast_reduce_fusion
  132.2 0.1 copy.100
  132.4 0.7 copy.105
  133.1 0.1 copy.101
  133.2 0.7 copy.106
  134.0 1.1 slice_bitcast_fusion.1
  135.1 0.3 copy.99
  135.4 1.0 copy.104
  136.4 24.6 %all-to-all-done.1 = bf16[16,272,256]{2,1,0:T(8,128)(2,1)S(1)} async-done(((bf16[16,272,256]{2,1,0:T(8,128)(2,1)}), bf16[16,272,256]{2,1,0:T(8,128)(2,1)S(1)}, u32[]{:S(2)}, u32[]{:S(2)}) %all-to-all-start.1) | async-done | bytes 2228256 | tf_op jit(solution)/shard_map/all_to_all | solution.py:389
  161.0 0.7 fusion.4
  161.7 0.6 slice_add_fusion.1
  162.4 0.6 copy_bitcast_fusion
  163.0 1.2 fusion.3
  164.2 1.6 copy.90
  165.9 1.3 copy.102
  167.2 0.3 reshape.113
  167.4 1.2 reduce
  168.6 0.1 copy.91
  168.8 0.8 copy.103
  (12 shorter events, 0.2 us)
Async XLA Ops:
  0.6 3.3 %copy-start.5 = (bf16[128,256]{1,0:T(8,128)(2,1)S(1)}, bf16[128,256]{1,0:T(8,128)(2,1)}, u32[]{:S(2)}) copy-start(bf16[128,256]{1,0:T(8,128)(2,1)} %param.20) | copy-start | bytes 196612
  0.6 3.3 %copy-start.6 = (bf16[128,256]{1,0:T(8,128)(2,1)S(1)}, bf16[128,256]{1,0:T(8,128)(2,1)}, u32[]{:S(2)}) copy-start(bf16[128,256]{1,0:T(8,128)(2,1)} %param.21) | copy-start | bytes 196612
  4.2 8.7 %copy-start.7 = (f32[32,128]{1,0:T(8,128)S(1)}, f32[32,128]{1,0:T(8,128)}, u32[]{:S(2)}) copy-start(f32[32,128]{1,0:T(8,128)} %param.16) | copy-start | bytes 49156
  4.2 8.7 %copy-start.3 = (bf16[128,4096]{1,0:T(8,128)(2,1)S(1)}, bf16[128,4096]{1,0:T(8,128)(2,1)}, u32[]{:S(2)}) copy-start(bf16[128,4096]{1,0:T(8,128)(2,1)} %param.12) | copy-start | bytes 3145732
  5.8 38.8 %all-to-all-start.2 = ((bf16[16,512,128]{2,1,0:T(8,128)(2,1)}), bf16[16,512,128]{2,1,0:T(8,128)(2,1)S(1)}, u32[]{:S(2)}, u32[]{:S(2)}) async-start(bf16[16,512,128]{2,1,0:T(8,128)(2,1)} %pad_maximum_fusion), calls=%async_computation.2 | async-start | bytes 4194304 | tf_op jit(solution)/shard_map/all_to_all | solution.py:389
  14.3 6.1 %copy-start.4 = (bf16[128,2,256]{2,1,0:T(2,128)(2,1)S(1)}, bf16[128,2,256]{2,1,0:T(2,128)(2,1)}, u32[]{:S(2)}) copy-start(bf16[128,2,256]{2,1,0:T(2,128)(2,1)} %param.13) | copy-start | bytes 393220
  23.7 25.4 %copy-start.1 = (s32[4]{0:T(128)S(1)}, s32[4]{0:T(128)}, u32[]{:S(2)}) copy-start(s32[4]{0:T(128)} %doc_ref.3) | copy-start | bytes 52
  44.5 50.4 %all-to-all-start = ((bf16[16,400,256]{2,1,0:T(8,128)(2,1)}), bf16[16,400,256]{2,1,0:T(8,128)(2,1)}, u32[]{:S(2)}, u32[]{:S(2)}) async-start(bf16[16,400,256]{2,1,0:T(8,128)(2,1)} %fusion.1), calls=%async_computation | async-start | bytes 6553600 | tf_op jit(solution)/shard_map/all_to_all | solution.py:389
  49.1 49.6 %copy-start.8 = (f32[4,2,256]{2,1,0:T(2,128)S(1)}, f32[4,2,256]{2,1,0:T(2,128)}, u32[]{:S(2)}) copy-start(f32[4,2,256]{2,1,0:T(2,128)} %param.15) | copy-start | bytes 24580
  65.4 1.2 copy-start
  95.0 27.6 %all-to-all-start.3 = ((bf16[16,384,128]{2,1,0:T(8,128)(2,1)}), bf16[16,384,128]{2,1,0:T(8,128)(2,1)S(1)}, u32[]{:S(2)}, u32[]{:S(2)}) async-start(bf16[16,384,128]{2,1,0:T(8,128)(2,1)} %copy-done), calls=%async_computation.3 | async-start | bytes 3145728 | tf_op jit(solution)/shard_map/all_to_all | solution.py:389
  122.6 1.2 copy-start.2
  123.7 37.3 %all-to-all-start.1 = ((bf16[16,272,256]{2,1,0:T(8,128)(2,1)}), bf16[16,272,256]{2,1,0:T(8,128)(2,1)S(1)}, u32[]{:S(2)}, u32[]{:S(2)}) async-start(bf16[16,272,256]{2,1,0:T(8,128)(2,1)} %mixer.1), calls=%async_computation.1 | async-start | bytes 4456448 | tf_op jit(solution)/shard_map/all_to_all | solution.py:389

commit v2 on v1

v2 whole, which is shorter than its diff:
```python
import jax
import jax.numpy as jnp
from jax import lax
from jax.experimental import pallas as pl
from jax.experimental.pallas import tpu as pltpu
from jax.sharding import PartitionSpec as P

F32 = jnp.float32
BF16 = jnp.bfloat16
HD = 128
BLK = 128
TAPS = 4
BACK = 8
LOG2E = 1.4426950408889634
NEG_BIG = -1e30
UNROLL = 4


def dot_nn(a, b):
    return lax.dot_general(a, b, (((1,), (0,)), ((), ())), preferred_element_type=F32)


def dot_nt(a, b):
    return lax.dot_general(a, b, (((1,), (1,)), ((), ())), preferred_element_type=F32)


def dot_tn(a, b):
    return lax.dot_general(a, b, (((0,), (0,)), ((), ())), preferred_element_type=F32)


def doc_bounds(doc_ref):
    s1 = doc_ref[0]
    s2 = s1 + doc_ref[1]
    s3 = s2 + doc_ref[2]
    return s1, s2, s3


def start_at(pos, bounds):
    s1, s2, s3 = bounds
    return jnp.where(pos >= s3, s3, jnp.where(pos >= s2, s2, jnp.where(pos >= s1, s1, 0)))


def next_start(pos, bounds, total):
    s1, s2, s3 = bounds
    return jnp.where(pos < s1, s1, jnp.where(pos < s2, s2, jnp.where(pos < s3, s3, total)))


def twice(a):
    return jnp.concatenate([a, a], axis=1)


def fold_rows(a):
    return jnp.sum(a.reshape(a.shape[0] // 8, 8, a.shape[1]), axis=0)


def split3(a):
    hi = a.astype(BF16)
    rest = a - hi.astype(F32)
    mid = rest.astype(BF16)
    return hi, mid, (rest - mid.astype(F32)).astype(BF16)


def dot_exact(a, ones):
    rows = a.shape[0]
    out = dot_nn(jnp.concatenate(split3(a), axis=0), ones.astype(BF16))
    return out[:rows] + out[rows : 2 * rows] + out[2 * rows :]


def ssm_kernel(
    doc_ref, idx_ref, rate_ref, r_ref, wx_ref, wbc_ref, out_ref,
    xs_s, xp_s, u_s, b_s, c_s, bm_s, cm_s, dsx_s, dsbc_s, st_s, ds_s,
    cols_s, elt_s, x2_s, y2_s, es_s, tapx_s, tapbc_s,
):
    blocks = r_ref.shape[0]
    total = blocks * BLK
    place = idx_ref[0]
    bounds = doc_bounds(doc_ref)
    rate0 = rate_ref[2 * place]
    rate1 = rate_ref[2 * place + 1]
    group = place // (blocks // 2)
    wx = wx_ref[:, pl.ds(pl.multiple_of(place * 256, 256), 256)]
    wbc = jnp.concatenate(
        [
            wbc_ref[:, pl.ds(pl.multiple_of(group * 128, 128), 128)],
            wbc_ref[:, pl.ds(pl.multiple_of(256 + group * 128, 128), 128)],
        ],
        axis=1,
    )

    for c in range(blocks):
        row = jnp.sum(r_ref[c, 3 * BLK : 3 * BLK + 16, :].astype(F32), axis=0, keepdims=True)
        x2_s[c : c + 1] = row[:, :128]
        x2_s[blocks + c : blocks + c + 1] = row[:, 128:]
    raw = x2_s[...]
    step = jnp.log(1.0 + jnp.exp(raw))
    sig = 1.0 / (1.0 + jnp.exp(-raw))
    row_ids = lax.broadcasted_iota(jnp.int32, (2 * blocks, 128), 0)
    rate = jnp.where(row_ids < blocks, rate0, rate1)
    ii = lax.broadcasted_iota(jnp.int32, (128, 128), 0)
    jj = lax.broadcasted_iota(jnp.int32, (128, 128), 1)
    cum = dot_exact(-step * rate, (ii <= jj).astype(F32))
    v_rows = jnp.exp(cum)
    u_hi, u_lo, _ = split3(step * jnp.exp(-cum))
    v_hi, v_lo, _ = split3(v_rows)
    last = jnp.broadcast_to(v_rows[:, 127:128], (2 * blocks, 128))
    pieces = [a.astype(F32) for a in (u_hi, u_lo, v_hi, v_lo)]
    for c in range(blocks):
        rows = [a[at : at + 1] for a in pieces for at in (c, blocks + c)]
        cols_s[c] = jnp.concatenate(rows, axis=0)
        elt_s[c] = jnp.broadcast_to(
            jnp.concatenate([last[c : c + 1], last[blocks + c : blocks + c + 1]], axis=1), (8, 256)
        )
    row8 = lax.broadcasted_iota(jnp.int32, (8, 512), 0)
    lane8 = lax.broadcasted_iota(jnp.int32, (8, 512), 1) // 128
    spread = ((lane8 // 2 == row8 // 4) & (lane8 % 2 == row8 % 2)).astype(BF16)

    edge = jnp.zeros((8, 256), F32)
    st_s[0] = jnp.zeros((128, 256), F32)

    def conv(edge, value, weight, keeps):
        win = jnp.concatenate([edge, value], axis=0)
        pre = value * weight[TAPS - 1 : TAPS]
        for d in range(1, TAPS):
            pre = pre + jnp.where(keeps[d - 1], win[8 - d : 8 - d + BLK], 0.0) * weight[TAPS - 1 - d : TAPS - d]
        sg = 0.5 * jnp.tanh(0.5 * pre) + 0.5
        val = pre * sg
        return val, sg + val * (1.0 - sg)

    def forward(c, carry):
        base = pl.multiple_of(c * BLK, BLK)
        edge_x, edge_bc = carry
        x = r_ref[c, 0:BLK].astype(F32)
        bc_raw = r_ref[c, 2 * BLK : 3 * BLK].astype(F32)
        pos = base + ii
        start = start_at(pos, bounds)
        last_start = start_at(base + BLK - 1, bounds)
        tails = pos >= last_start
        dist = pos - start
        keeps = [twice(dist >= d) for d in range(1, TAPS)]
        xs, dsx = conv(edge_x, x, wx, keeps)
        bc, dsbc = conv(edge_bc, bc_raw, wbc, keeps)
        xs_s[c] = xs
        dsx_s[c] = dsx
        dsbc_s[c] = dsbc
        b = bc[:, :128]
        cc = bc[:, 128:]
        b_s[c] = b.astype(BF16)
        c_s[c] = cc.astype(BF16)
        bm = jnp.where(tails, b, 0.0).astype(BF16)
        bm_s[c] = bm
        cm_s[c] = jnp.where(start < base, cc, 0.0).astype(BF16)
        u = dot_tn(cols_s[c].astype(BF16), spread[:, :256])
        u_s[c] = u
        xp = (xs * u).astype(BF16)
        xp_s[c] = xp
        elt = elt_s[c][0:1]
        keep = jnp.where(last_start < base, elt, 0.0)
        st_s[c + 1] = keep * st_s[c] + elt * dot_tn(bm, xp)
        return x[BLK - 8 :], bc_raw[BLK - 8 :]

    lax.fori_loop(0, blocks, forward, (edge, edge), unroll=UNROLL)

    ds_s[...] = jnp.zeros((128, 256), F32)
    tapx_s[...] = jnp.zeros((TAPS, 8, 256), F32)
    tapbc_s[...] = jnp.zeros((TAPS, 8, 256), F32)
    lane2 = lax.broadcasted_iota(jnp.int32, (16, 256), 1)
    row2 = lax.broadcasted_iota(jnp.int32, (16, 256), 0)
    pick = (lane2 // 128 == row2).astype(BF16)

    def head_sums(out, c, a):
        sums = dot_nt(pick, a.astype(BF16))
        out[pl.ds(c, 1)] = sums[0:1]
        out[pl.ds(blocks + c, 1)] = sums[1:2]

    def conv_back(grad, edge, raw_in, weight, ends, taps):
        win = jnp.concatenate([grad, edge], axis=0)
        total_grad = grad * weight[TAPS - 1 : TAPS]
        taps[TAPS - 1] += fold_rows(grad * raw_in)
        for d in range(1, TAPS):
            moved = jnp.where(ends[d - 1], win[d : d + BLK], 0.0)
            total_grad = total_grad + moved * weight[TAPS - 1 - d : TAPS - d]
            taps[TAPS - 1 - d] += fold_rows(moved * raw_in)
        return total_grad

    def backward(lap, carry):
        c = blocks - 1 - lap
        base = pl.multiple_of(c * BLK, BLK)
        pos = base + ii
        start = start_at(pos, bounds)
        last_start = start_at(base + BLK - 1, bounds)
        causal = (jj <= ii) & (base + jj >= start)
        leads = start < base
        tails = pos >= last_start
        b = b_s[c]
        cc = c_s[c]
        xp = xp_s[c]
        cm = cm_s[c]
        gv = r_ref[c, BLK : 2 * BLK].astype(F32) * dot_tn(cols_s[c].astype(BF16), spread[:, 256:])
        gp = gv.astype(BF16)
        elt = elt_s[c][0:1]
        ds = ds_s[...]
        es_s[pl.ds(pl.multiple_of(c * 8, 8), 8)] = fold_rows(ds * st_s[c + 1])
        sb = st_s[c].astype(BF16)
        ds_e = elt * ds
        dsb = ds_e.astype(BF16)
        ds_s[...] = jnp.where(last_start < base, ds_e, 0.0) + dot_tn(cm, gp)
        w = jnp.where(causal, dot_nt(cc, b), 0.0).astype(BF16)
        yv = dot_nn(w, xp) + dot_nn(cm, sb)
        dxp = dot_tn(w, gp) + dot_nn(bm_s[c], dsb)
        z = jnp.where(causal, dot_nt(gp, xp), 0.0).astype(BF16)
        dc = dot_nn(z, b) + jnp.where(leads, dot_nt(gp, sb), 0.0)
        db = dot_tn(z, cc) + jnp.where(tails, dot_nt(xp, dsb), 0.0)
        dx = u_s[c] * dxp
        head_sums(x2_s, c, xs_s[c] * dx)
        head_sums(y2_s, c, gv * yv)
        left = next_start(pos, bounds, total) - pos
        ends = [twice(left > d) for d in range(1, TAPS)]
        edge_x, edge_bc = carry
        pre_x = dx * dsx_s[c]
        pre_bc = jnp.concatenate([db, dc], axis=1) * dsbc_s[c]
        x = r_ref[c, 0:BLK].astype(F32)
        bc_raw = r_ref[c, 2 * BLK : 3 * BLK].astype(F32)
        out_ref[c, 0:BLK] = conv_back(pre_x, edge_x, x, wx, ends, tapx_s).astype(BF16)
        out_ref[c, BLK : 2 * BLK] = conv_back(
            pre_bc, edge_bc, bc_raw, wbc, ends, tapbc_s
        ).astype(BF16)
        return pre_x[0:8], pre_bc[0:8]

    lax.fori_loop(0, blocks, backward, (edge, edge), unroll=UNROLL)

    xdx = x2_s[...]
    carry_sum = jnp.sum(es_s[...].reshape(blocks, 8, 256), axis=1)
    carry_sum = jnp.concatenate([carry_sum[:, :128], carry_sum[:, 128:]], axis=0)
    d_log = dot_exact(y2_s[...] - xdx, (ii >= jj).astype(F32))
    d_log = d_log + jnp.sum(carry_sum, axis=1, keepdims=True)
    d_raw = (xdx / step - rate * d_log) * sig
    d_raw = jnp.concatenate([d_raw[:blocks], d_raw[blocks:]], axis=1)
    raw_hi = d_raw.astype(BF16).astype(F32)
    raw_lo = d_raw - raw_hi
    tapx = jnp.concatenate([jnp.sum(tapx_s[k], axis=0, keepdims=True) for k in range(TAPS)], axis=0)
    tapbc = jnp.concatenate([jnp.sum(tapbc_s[k], axis=0, keepdims=True) for k in range(TAPS)], axis=0)
    tapx_hi = tapx.astype(BF16).astype(F32)
    rest = jnp.concatenate([tapx_hi, tapx - tapx_hi, tapbc, jnp.zeros((2, 256), F32)], axis=0)
    for c in range(blocks):
        out_ref[c, 2 * BLK : 2 * BLK + 16] = jnp.concatenate(
            [raw_hi[c : c + 1], raw_lo[c : c + 1], rest], axis=0
        ).astype(BF16)


def ssm_core(doc_lengths, place, rate, received, weight_x, weight_bc):
    blocks = received.shape[0]
    smem = pl.BlockSpec(memory_space=pltpu.SMEM)
    vmem = pl.BlockSpec(memory_space=pltpu.VMEM)

    def scratch(*shape, dtype=F32):
        return pltpu.VMEM(shape, dtype)

    return pl.pallas_call(
        ssm_kernel,
        out_shape=jax.ShapeDtypeStruct((blocks, 2 * BLK + 16, 256), BF16),
        in_specs=[smem, smem, smem, vmem, vmem, vmem],
        out_specs=vmem,
        scratch_shapes=[
            scratch(blocks, BLK, 256),
            scratch(blocks, BLK, 256, dtype=BF16),
            scratch(blocks, BLK, 256),
            scratch(blocks, BLK, 128, dtype=BF16),
            scratch(blocks, BLK, 128, dtype=BF16),
            scratch(blocks, BLK, 128, dtype=BF16),
            scratch(blocks, BLK, 128, dtype=BF16),
            scratch(blocks, BLK, 256),
            scratch(blocks, BLK, 256),
            scratch(blocks + 1, 128, 256),
            scratch(128, 256),
            scratch(blocks, 8, 128),
            scratch(blocks, 8, 256),
            scratch(2 * blocks, 128),
            scratch(2 * blocks, 128),
            scratch(8 * blocks, 256),
            scratch(TAPS, 8, 256),
            scratch(TAPS, 8, 256),
        ],
        compiler_params=pltpu.CompilerParams(vmem_limit_bytes=24 * 2**20),
        cost_estimate=pl.CostEstimate(flops=3 * 10**9, bytes_accessed=6 * 2**20, transcendentals=4 * 10**6),
        name="mixer",
    )(doc_lengths, place, rate, received, weight_x, weight_bc)


def attention_kernel(
    doc_ref, idx_ref, q_ref, do_ref, got_ref, kv0, kv1, kv2, kv3, kv4,
    dq_own, dq_sent, d0, d1, d2, d3, d4, kt_s, dk_s, dv_s, s_s, p_s,
):
    kv_refs = (kv4, kv3, kv2, kv1, kv0)
    d_refs = (d4, d3, d2, d1, d0)
    count = 2 * len(kv_refs)
    bounds = doc_bounds(doc_ref)
    scale = HD ** (-0.5)
    place = idx_ref[0]
    odd = lax.rem(place, 2)
    base = (place - odd) * BLK
    jrow = lax.broadcasted_iota(jnp.int32, (BLK, 2 * BLK), 0)
    icol = lax.broadcasted_iota(jnp.int32, (BLK, 2 * BLK), 1)
    start = start_at(base + icol[0:1], bounds) - base
    heads = got_ref.shape[1] // (2 * HD)

    def rows8(a):
        return a.reshape(BLK // 8, 8, 2 * BLK)

    def half(b):
        return slice((b % 2) * BLK, (b % 2 + 1) * BLK)

    def key_rows(b):
        return kv_refs[b // 2][half(b), 0:HD]

    def value_rows(b):
        return kv_refs[b // 2][half(b), HD : 2 * HD]

    def in_order(own, other):
        first = jnp.where(odd == 0, own, other)
        second = jnp.where(odd == 0, other, own)
        return jnp.concatenate([first, second], axis=0)

    for b in range(count):
        kt_s[b] = key_rows(b).T
    dk_s[...] = jnp.zeros(dk_s.shape, F32)
    dv_s[...] = jnp.zeros(dv_s.shape, F32)

    def turn(head, carry):
        at = pl.multiple_of(head * HD, HD)
        own_at = pl.multiple_of((odd * heads + head) * HD, HD)
        q = in_order(q_ref[:, pl.ds(own_at, HD)], got_ref[:, pl.ds(at, HD)])
        do = in_order(
            do_ref[:, pl.ds(own_at, HD)], got_ref[:, pl.ds(pl.multiple_of(heads * HD + at, HD), HD)]
        )
        top = jnp.full((8, 2 * BLK), NEG_BIG, F32)
        for b in range(count):
            allowed = jrow >= start + (BACK - b) * BLK
            if b >= BACK:
                allowed = allowed & (jrow + (b - BACK) * BLK <= icol)
            s = jnp.where(allowed, dot_nt(key_rows(b), q), NEG_BIG)
            s_s[b] = s
            top = jnp.maximum(top, jnp.max(rows8(s), axis=0))
            p_s[b] = dot_nt(value_rows(b), do)
        top = jnp.max(top, axis=0, keepdims=True) * (scale * LOG2E)
        norm = jnp.zeros((8, 2 * BLK), F32)
        mean = jnp.zeros((8, 2 * BLK), F32)
        for b in range(count):
            e = jnp.exp2(s_s[b] * (scale * LOG2E) - top)
            s_s[b] = e
            norm = norm + jnp.sum(rows8(e), axis=0)
            mean = mean + jnp.sum(rows8(e * p_s[b]), axis=0)
        inverse = 1.0 / jnp.sum(norm, axis=0, keepdims=True)
        mean = jnp.sum(mean, axis=0, keepdims=True) * inverse
        dqt = jnp.zeros((HD, 2 * BLK), F32)
        for b in range(count):
            prob = s_s[b] * inverse
            grad = (prob * (p_s[b] - mean)).astype(BF16)
            dv_s[b] += dot_nn(prob.astype(BF16), do)
            dk_s[b] += dot_nn(grad, q)
            dqt = dqt + dot_nn(kt_s[b], grad)
        dqt = dqt * scale
        first = dqt[:, :BLK].T
        second = dqt[:, BLK:].T
        dq_own[:, pl.ds(at, HD)] = jnp.where(odd == 0, first, second).astype(BF16)
        dq_sent[:, pl.ds(at, HD)] = jnp.where(odd == 0, second, first).astype(BF16)
        return carry

    lax.fori_loop(0, heads, turn, 0)
    for b in range(count):
        out = d_refs[b // 2]
        out[half(b), 0:HD] = (dk_s[b] * scale).astype(out.dtype)
        out[half(b), HD : 2 * HD] = dv_s[b].astype(out.dtype)


def attention_core(doc_lengths, place, query, d_out, got, kv_pairs):
    smem = pl.BlockSpec(memory_space=pltpu.SMEM)
    vmem = pl.BlockSpec(memory_space=pltpu.VMEM)
    pairs = len(kv_pairs)
    count = 2 * pairs
    rows, width = query.shape
    part = jax.ShapeDtypeStruct((rows, width // 2), BF16)
    kv_shape = kv_pairs[0].shape
    outs = [part, part, jax.ShapeDtypeStruct(kv_shape, F32)]
    outs += [jax.ShapeDtypeStruct(kv_shape, BF16)] * (pairs - 1)
    return pl.pallas_call(
        attention_kernel,
        out_shape=outs,
        in_specs=[smem, smem] + [vmem] * (3 + pairs),
        out_specs=[vmem] * (2 + pairs),
        scratch_shapes=[
            pltpu.VMEM((count, HD, BLK), BF16),
            pltpu.VMEM((count, BLK, HD), F32),
            pltpu.VMEM((count, BLK, HD), F32),
            pltpu.VMEM((count, BLK, 2 * BLK), F32),
            pltpu.VMEM((count, BLK, 2 * BLK), F32),
        ],
        compiler_params=pltpu.CompilerParams(vmem_limit_bytes=16 * 2**20),
        cost_estimate=pl.CostEstimate(flops=4 * 10**9, bytes_accessed=4 * 2**20, transcendentals=3 * 10**6),
        name="attention",
    )(doc_lengths, place, query, d_out, got, *kv_pairs)


def shift(a, by):
    devices = lax.axis_size("ctx")
    return lax.ppermute(
        a, "ctx", [(i, i + by) for i in range(devices) if 0 <= i + by < devices]
    )


def partner(a):
    return lax.ppermute(a, "ctx", [(i, i ^ 1) for i in range(lax.axis_size("ctx"))])


def pack_kernel(x_ref, g_ref, bc_ref, dt_ref, out_ref, buf, in_sems, out_sems):
    blocks = out_ref.shape[0]
    loads = []
    for d in range(blocks):
        lanes = pl.ds(d * 2 * HD, 2 * HD)
        pair = [
            pltpu.make_async_copy(src, buf.at[d, pl.ds(at * BLK, BLK)], in_sems.at[2 * d + at])
            for at, src in enumerate((x_ref.at[:, lanes], g_ref.at[:, lanes]))
        ]
        for one in pair:
            one.start()
        loads.append(pair)
    for d in range(blocks):
        buf[d, 2 * BLK : 3 * BLK] = bc_ref[d // (blocks // 2)]
        raw = jnp.concatenate([dt_ref[2 * d : 2 * d + 1], dt_ref[2 * d + 1 : 2 * d + 2]], axis=1)
        hi = raw.astype(BF16).astype(F32)
        mid = (raw - hi).astype(BF16).astype(F32)
        parts = [hi, mid, raw - hi - mid, jnp.zeros((13, 2 * BLK), F32)]
        buf[d, 3 * BLK : 3 * BLK + 16] = jnp.concatenate(parts, axis=0).astype(BF16)
    stores = []
    for d in range(blocks):
        for one in loads[d]:
            one.wait()
        stores.append(pltpu.make_async_copy(buf.at[d], out_ref.at[d], out_sems.at[d]))
        stores[-1].start()
    for one in stores:
        one.wait()


def pack(x_in, grad, bc_sent, dt_raw, blocks):
    hbm = pl.BlockSpec(memory_space=pltpu.HBM)
    vmem = pl.BlockSpec(memory_space=pltpu.VMEM)
    return pl.pallas_call(
        pack_kernel,
        out_shape=jax.ShapeDtypeStruct((blocks, 3 * BLK + 16, 2 * HD), BF16),
        in_specs=[hbm, hbm, vmem, vmem],
        out_specs=hbm,
        scratch_shapes=[
            pltpu.VMEM((blocks, 3 * BLK + 16, 2 * HD), BF16),
            pltpu.SemaphoreType.DMA((2 * blocks,)),
            pltpu.SemaphoreType.DMA((blocks,)),
        ],
        cost_estimate=pl.CostEstimate(flops=0, bytes_accessed=7 * 2**20, transcendentals=0),
        name="pack",
    )(x_in, grad, bc_sent, dt_raw)


def unpack_kernel(part, dx_ref, dbc_ref, dt_ref, wx_ref, wbc_ref, sems):
    blocks = part.shape[0]
    half = blocks // 2
    copies = []
    for d in range(blocks):
        lanes = pl.ds(d * 2 * HD, 2 * HD)
        copies.append(pltpu.make_async_copy(part.at[d, pl.ds(0, BLK)], dx_ref.at[:, lanes], sems.at[d]))
        copies[-1].start()
    for group in range(2):
        at = [group * half + d for d in range(half)]
        total = part[at[0], BLK : 2 * BLK].astype(F32)
        taps = part[at[0], 2 * BLK : 2 * BLK + 16].astype(F32)
        for d in at[1:]:
            total = total + part[d, BLK : 2 * BLK].astype(F32)
            taps = taps + part[d, 2 * BLK : 2 * BLK + 16].astype(F32)
        for which in range(2):
            lanes = slice(which * HD, (which + 1) * HD)
            out = slice((2 * which + group) * HD, (2 * which + group + 1) * HD)
            dbc_ref[:, out] = total[:, lanes].astype(BF16)
            wbc_ref[:, which, group * HD : (group + 1) * HD] = taps[10:14, lanes]
    for d in range(blocks):
        small = part[d, 2 * BLK : 2 * BLK + 16].astype(F32)
        raw = small[0:1] + small[1:2]
        dt_ref[2 * d : 2 * d + 1] = raw[:, :BLK]
        dt_ref[2 * d + 1 : 2 * d + 2] = raw[:, BLK:]
        wx_ref[:, d * 2 * HD : (d + 1) * 2 * HD] = small[2:6] + small[6:10]
    for done in copies:
        done.wait()


def unpack(received):
    blocks = received.shape[0]
    hbm = pl.BlockSpec(memory_space=pltpu.HBM)
    vmem = pl.BlockSpec(memory_space=pltpu.VMEM)
    return pl.pallas_call(
        unpack_kernel,
        out_shape=[
            jax.ShapeDtypeStruct((BLK, blocks * 2 * HD), BF16),
            jax.ShapeDtypeStruct((BLK, 4 * HD), BF16),
            jax.ShapeDtypeStruct((2 * blocks, BLK), F32),
            jax.ShapeDtypeStruct((TAPS, blocks * 2 * HD), F32),
            jax.ShapeDtypeStruct((TAPS, 2, 2 * HD), F32),
        ],
        in_specs=[vmem],
        out_specs=[hbm, vmem, vmem, vmem, vmem],
        scratch_shapes=[pltpu.SemaphoreType.DMA((blocks,))],
        compiler_params=pltpu.CompilerParams(vmem_limit_bytes=8 * 2**20),
        cost_estimate=pl.CostEstimate(flops=10**6, bytes_accessed=4 * 2**20, transcendentals=0),
        name="unpack",
    )(received)


def gate_kernel(*refs):
    pass


def gate(value, *others):
    hbm = pl.BlockSpec(memory_space=pltpu.HBM)
    anywhere = pl.BlockSpec(memory_space=pl.ANY)
    return pl.pallas_call(
        gate_kernel,
        out_shape=jax.ShapeDtypeStruct(value.shape, value.dtype),
        in_specs=[hbm] + [anywhere] * len(others),
        out_specs=hbm,
        input_output_aliases={0: 0},
        name="gate",
    )(value, *others)


def kv_sum_kernel(idx_ref, own, r1, r2, r3, r4, after, mine, sent):
    total = own[...]
    for got in (r1, r2, r3, r4):
        total = total + got[...].astype(F32)
    rows = mine.shape[0]
    first = total[:rows].astype(BF16)
    second = total[rows:].astype(BF16)
    odd = lax.rem(idx_ref[0], 2)
    mine[...] = jnp.where(odd == 0, first, second)
    sent[...] = jnp.where(odd == 0, second, first)


def kv_total(place, own, received, after):
    vmem = pl.BlockSpec(memory_space=pltpu.VMEM)
    half = jax.ShapeDtypeStruct((own.shape[0] // 2, own.shape[1]), BF16)
    return pl.pallas_call(
        kv_sum_kernel,
        out_shape=[half, half],
        in_specs=[pl.BlockSpec(memory_space=pltpu.SMEM)]
        + [vmem] * (1 + len(received))
        + [pl.BlockSpec(memory_space=pl.ANY)],
        out_specs=[vmem, vmem],
        name="kv_total",
    )(place, own, *received, after)


def kv_place_kernel(idx_ref, mine, other, dk_ref, dv_ref):
    odd = lax.rem(idx_ref[0], 2)
    a = mine[...]
    b = other[...]
    first = jnp.where(odd == 0, a, b)
    second = jnp.where(odd == 0, b, a)
    dk_ref[...] = jnp.concatenate([first[:, :HD], second[:, :HD]], axis=1)
    dv_ref[...] = jnp.concatenate([first[:, HD:], second[:, HD:]], axis=1)


def kv_place(place, mine, other):
    vmem = pl.BlockSpec(memory_space=pltpu.VMEM)
    return pl.pallas_call(
        kv_place_kernel,
        out_shape=[jax.ShapeDtypeStruct(mine.shape, BF16)] * 2,
        in_specs=[pl.BlockSpec(memory_space=pltpu.SMEM), vmem, vmem],
        out_specs=[vmem, vmem],
        name="kv_place",
    )(place, mine, other)


def swap(a):
    return lax.all_to_all(a, "ctx", 0, 0, tiled=True)


def shards(
    x_in, bc_in, conv_x, conv_bc, dt_raw, rate, grad_ssd, query, key, value, d_out, doc_lengths
):
    ctx = lax.axis_size("ctx")
    rows = x_in.shape[0]
    place = lax.axis_index("ctx").astype(jnp.int32).reshape(1)

    odd = place[0] % 2

    def half(a, which):
        return lax.dynamic_slice_in_dim(a, which * (a.shape[1] // 2), a.shape[1] // 2, 1)

    def pick(own, other):
        return jnp.where(odd == 0, own, other), jnp.where(odd == 0, other, own)

    bc_sent = bc_in.reshape(rows, 2, 2, HD).transpose(2, 0, 1, 3).reshape(2, rows, 2 * HD)
    packed = pack(x_in, grad_ssd, bc_sent, dt_raw, ctx)
    kv_own = jnp.concatenate([half(key, odd), half(value, odd)], axis=1)
    kv_got = partner(jnp.concatenate([half(key, 1 - odd), half(value, 1 - odd)], axis=1))
    kv_pair = gate(jnp.concatenate(pick(kv_own, kv_got), axis=0), packed)
    got_qo = partner(jnp.concatenate([half(query, 1 - odd), half(d_out, 1 - odd)], axis=1))
    kv_pairs = [kv_pair] + [shift(kv_pair, 2 * by) for by in range(1, BACK // 2 + 1)]
    got = swap(gate(packed, got_qo, *kv_pairs[1:]))
    dq_own, dq_sent, *d_kv = attention_core(doc_lengths, place, query, d_out, got_qo, kv_pairs)
    place_after, *d_kv = lax.optimization_barrier((place, *d_kv))
    mixed = ssm_core(
        doc_lengths, place_after, rate, got, conv_x, conv_bc.reshape(TAPS, 4 * HD)
    )
    dq_got = partner(dq_sent)
    received = [shift(d_kv[by], -2 * by) for by in range(1, BACK // 2 + 1)]
    back = swap(gate(mixed, dq_got, *received))
    mine, sent = kv_total(place, d_kv[0], received, mixed)
    d_key, d_value = kv_place(place, mine, partner(sent))
    d_query = jnp.concatenate(pick(dq_own, dq_got), axis=1)
    d_x, d_bc, d_dt, d_wx, d_wbc = unpack(back)
    return (
        d_x,
        d_bc.reshape(rows, 2, 2 * HD),
        d_dt,
        d_wx,
        d_wbc,
        d_query,
        d_key,
        d_value,
    )


def solution(mesh):
    tokens = P(("dp", "ctx"), "head")
    in_specs = (
        tokens,
        P(("dp", "ctx"), None, "head"),
        P(None, "head"),
        P(None, None, "head"),
        P("head", ("dp", "ctx")),
        P("head"),
        tokens,
        tokens,
        tokens,
        tokens,
        tokens,
        P("dp"),
    )
    out_specs = (
        tokens,
        P(("dp", "ctx"), None, "head"),
        P("head", ("dp", "ctx")),
        P("dp", "head"),
        P("dp", None, "head"),
        tokens,
        tokens,
        tokens,
    )
    return jax.shard_map(shards, mesh=mesh, in_specs=in_specs, out_specs=out_specs, check_vma=False)
```

time: 170 us -> 149 us (0.88)
  waiting for transfers between devices: 73.9 us -> 49.6 us
  starting transfers between devices: 22.5 us -> 36.4 us
  other arithmetic: 8.33 us -> 2.56 us
  local copies, waits for them, and re-layouts: 24.3 us -> 18.6 us
    all_to_all x4 -> x2, waiting for transfers between devices: 73.9 us -> 18.2 us  [swap(): return lax.all_to_all(a, 'ctx', 0, 0, tiled=True)]
    ppermute x0 -> x12, waiting for transfers between devices: none -> 31.4 us  [the longest x4 26.7 us: partner(): lax.ppermute(a, 'ctx', [(i, i ^ 1) for i in range(lax.axis_size('ctx'))])]
    ppermute x0 -> x12, starting transfers between devices: none -> 26.5 us  [the longest x8 20.4 us: shift(): lax.ppermute(a, 'ctx', [(i, i + by) for i in range(devices) if 0 <= i + b...]
    all_to_all x4 -> x2, starting transfers between devices: 22.5 us -> 9.93 us  [swap(): return lax.all_to_all(a, 'ctx', 0, 0, tiled=True)]
    pallas_call x1 -> x8, Pallas kernels: 16.3 us -> 24.4 us  [the longest x1 15.4 us: attention_core(): pl.pallas_call(attention_kernel, out_shape=outs, in_specs=[smem, smem] +...]
    pallas_call x1, Pallas kernels: 23.3 us -> 15.8 us  [ssm_core(): pl.pallas_call(ssm_kernel, out_shape=jax.ShapeDtypeStruct((blocks, 2 * BL...]
    reshape x9 -> x1, local copies, waits for them, and re-layouts: 5.34 us -> 0.69 us  [shards(): d_bc.reshape(rows, 2, 2 * HD)]
    transpose x5 -> x0, local copies, waits for them, and re-layouts: 2.99 us -> none  [the longest x1 1.61 us: shards(): d_x = back[:, :rows].transpose(1, 0, 2).reshape(rows, ctx * 2 * HD)]
  transfers between devices with their start and end apart: 4 -> 14, of which waited for: 3 -> 4; matrix products, arithmetic and copies ran while one was open for 10% -> 4% of each run, Pallas kernels for 23% -> 26%
where the time goes in v2:
time: 149 us; the launch traced here: 148 us
  waiting for transfers between devices  49.6 us (33%)
  Pallas kernels  40.2 us (27%)
  starting transfers between devices  36.4 us (24%)
  local copies, waits for them, and re-layouts  18.6 us (12%)
  other arithmetic  2.56 us (2%)
    ppermute x4, waiting for transfers between devices, partner(): lax.ppermute(a, 'ctx', [(i, i ^ 1) for i in range(lax.axis_size('ctx'))])  26.7 us
    ppermute x8, starting transfers between devices, shift(): lax.ppermute(a, 'ctx', [(i, i + by) for i in range(devices) if 0 <= i + b...  20.4 us
    all_to_all x2, waiting for transfers between devices, swap(): return lax.all_to_all(a, 'ctx', 0, 0, tiled=True)  18.2 us
    pallas_call x1, Pallas kernels, ssm_core(): pl.pallas_call(ssm_kernel, out_shape=jax.ShapeDtypeStruct((blocks, 2 * BL...  15.8 us
    pallas_call x1, Pallas kernels, attention_core(): pl.pallas_call(attention_kernel, out_shape=outs, in_specs=[smem, smem] +...  15.4 us
    unnamed x48, local copies, waits for them, and re-layouts  15.2 us
    all_to_all x2, starting transfers between devices, swap(): return lax.all_to_all(a, 'ctx', 0, 0, tiled=True)  9.93 us
    ppermute x4, starting transfers between devices, partner(): lax.ppermute(a, 'ctx', [(i, i ^ 1) for i in range(lax.axis_size('ctx'))])  6.14 us
  transfers between devices with their start and end apart: 14, of which 4 were waited for; matrix products, arithmetic and copies ran while one was open for 4% of the time, Pallas kernels for 26%

profile of v2, /device:TPU:0, one launch (start us, length us, event | category | flops | bytes accessed | tf_op | source)
XLA Modules:
  0.0 148.4 jit_solution(14950007956450524588)
XLA Ops:
  0.6 0.0 copy-start
  0.7 0.9 constant_dynamic-slice_fusion.2
  1.5 1.7 %collective-permute-start.1 = (bf16[128,256]{1,0:T(8,128)(2,1)S(1)}, bf16[128,256]{1,0:T(8,128)(2,1)S(1)}, u32[]{:S(2)}, u32[]{:S(2)}) collective-permute-start(bf16[128,256]{1,0:T(8,128)(2,1)S(1)} %pad_maximum_fusion.4), channel_id=1, source_target_pairs={{0,8},{8,0},{16,24},{24,16},{32,40},{40,32},{48,56},{56,48},{64,72... | collective-permute-start | bytes 196616 | tf_op jit(solution)/shard_map/ppermute | solution.py:411
  3.2 1.1 constant_dynamic-slice_fusion.4
  4.3 0.5 collective-permute-start
  4.8 0.0 copy-done
  4.8 0.1 bitcast_bitcast_fusion
  4.9 0.7 reshape.33.bc_ref
  5.7 3.9 %pack.1.refs_1_.refs_0_ = bf16[16,400,256]{2,1,0:T(8,128)(2,1)} custom-call(bf16[128,4096]{1,0:T(8,128)(2,1)} %x_ref.1, bf16[128,4096]{1,0:T(8,128)(2,1)} %g_ref.1, bf16[2,128,256]{2,1,0:T(8,128)(2,1)} %reshape.33.bc_ref, f32[32,128]{1,0:T(8,128)} %dt_ref.1), custom_call_target="tpu_custom_call" | custom-call | bytes 7340032 | tf_op jit(solution)/shard_map/pack/pallas_call | solution.py:446
  9.6 0.0 collective-permute-done.1
  9.6 0.7 pad_maximum_fusion.2.refs_0_
  10.3 5.0 %collective-permute-start.2 = (bf16[256,256]{1,0:T(8,128)(2,1)}, bf16[256,256]{1,0:T(8,128)(2,1)S(1)}, u32[]{:S(2)}, u32[]{:S(2)}) collective-permute-start(bf16[256,256]{1,0:T(8,128)(2,1)} %gate.3.kv0), channel_id=1, source_target_pairs={{0,16},{8,24},{16,32},{24,40},{32,48},{40,56},{48,64},{56,72},{64,... | collective-permute-start | bytes 393224 | tf_op jit(solution)/shard_map/ppermute | solution.py:405
  15.3 3.5 %collective-permute-start.3 = (bf16[256,256]{1,0:T(8,128)(2,1)}, bf16[256,256]{1,0:T(8,128)(2,1)S(1)}, u32[]{:S(2)}, u32[]{:S(2)}) collective-permute-start(bf16[256,256]{1,0:T(8,128)(2,1)} %gate.3.kv0), channel_id=1, source_target_pairs={{0,32},{8,40},{16,48},{24,56},{32,64},{40,72},{48,80},{56,88},{64,... | collective-permute-start | bytes 393224 | tf_op jit(solution)/shard_map/ppermute | solution.py:405
  18.8 4.1 %collective-permute-start.4 = (bf16[256,256]{1,0:T(8,128)(2,1)}, bf16[256,256]{1,0:T(8,128)(2,1)S(1)}, u32[]{:S(2)}, u32[]{:S(2)}) collective-permute-start(bf16[256,256]{1,0:T(8,128)(2,1)} %gate.3.kv0), channel_id=1, source_target_pairs={{0,48},{8,56},{16,64},{24,72},{32,80},{40,88},{48,96},{56,104},{64... | collective-permute-start | bytes 393224 | tf_op jit(solution)/shard_map/ppermute | solution.py:405
  23.0 2.6 %collective-permute-start.5 = (bf16[256,256]{1,0:T(8,128)(2,1)}, bf16[256,256]{1,0:T(8,128)(2,1)S(1)}, u32[]{:S(2)}, u32[]{:S(2)}) collective-permute-start(bf16[256,256]{1,0:T(8,128)(2,1)} %gate.3.kv0), channel_id=1, source_target_pairs={{0,64},{8,72},{16,80},{24,88},{32,96},{40,104},{48,112},{56,120},{... | collective-permute-start | bytes 393224 | tf_op jit(solution)/shard_map/ppermute | solution.py:405
  25.6 0.0 collective-permute-done.2.kv1.refs_2_
  25.6 0.0 copy-start.10
  25.6 0.0 collective-permute-done.3.kv2.refs_3_
  25.6 0.0 copy-start.12
  25.6 0.2 collective-permute-done.4.kv3.refs_4_
  25.8 4.5 %collective-permute-done.5.kv4.refs_5_ = bf16[256,256]{1,0:T(8,128)(2,1)S(1)} collective-permute-done((bf16[256,256]{1,0:T(8,128)(2,1)}, bf16[256,256]{1,0:T(8,128)(2,1)S(1)}, u32[]{:S(2)}, u32[]{:S(2)}) %collective-permute-start.5) | collective-permute-done | bytes 131104 | tf_op jit(solution)/shard_map/ppermute | solution.py:405
  30.3 0.0 collective-permute-done.got_ref.refs_1_
  30.3 0.6 copy-done.16
  30.9 0.8 copy-done.3
  31.7 5.8 %all-to-all-start = ((bf16[16,400,256]{2,1,0:T(8,128)(2,1)}), bf16[16,400,256]{2,1,0:T(8,128)(2,1)S(1)}, u32[]{:S(2)}, u32[]{:S(2)}) async-start(bf16[16,400,256]{2,1,0:T(8,128)(2,1)} %gate.4), calls=%async_computation | async-start | bytes 6553600 | tf_op jit(solution)/shard_map/all_to_all | solution.py:578
  37.6 0.7 copy.25
  38.3 0.0 copy-done.2
  38.3 1.0 copy-done.4
  39.3 1.0 copy-done.8
  40.4 1.0 copy-done.9
  41.4 0.9 copy-done.11
  42.3 0.9 copy-done.13
  43.2 0.9 copy-done.15
  44.1 0.9 copy-done.17
  45.0 15.4 %attention.1 = (bf16[128,1024]{1,0:T(8,128)(2,1)S(1)}, bf16[128,1024]{1,0:T(8,128)(2,1)}, f32[256,256]{1,0:T(8,128)S(1)}, bf16[256,256]{1,0:T(8,128)(2,1)}, bf16...) custom-call(s32[4]{0:T(128)S(1)} %copy-done.19, s32[1]{0:T(128)} %bitcast.idx_ref, ...), custom_call_target="tpu_custom_call" | custom-call | flops 4000000000 | bytes 4194304 | tf_op jit(solution)/shard_map/attention/pallas_call | solution.py:385
  60.4 0.7 copy-done.5
  61.1 0.7 copy-done.6
  61.8 1.3 collective-permute-start.10
  63.1 1.3 collective-permute-start.7
  64.4 1.3 collective-permute-start.8
  65.7 1.3 collective-permute-start.9
  67.0 2.0 %collective-permute-start.6 = (bf16[128,1024]{1,0:T(8,128)(2,1)}, bf16[128,1024]{1,0:T(8,128)(2,1)}, u32[]{:S(2)}, u32[]{:S(2)}) collective-permute-start(bf16[128,1024]{1,0:T(8,128)(2,1)} %get-tuple-element.36), channel_id=1, source_target_pairs={{0,8},{8,0},{16,24},{24,16},{32,40},{40,32},{48,56},{56,48},{64,72... | collective-permute-start | bytes 786440 | tf_op jit(solution)/shard_map/ppermute | solution.py:411
  69.1 18.2 %all-to-all-done.r_ref = bf16[16,400,256]{2,1,0:T(8,128)(2,1)S(1)} async-done(((bf16[16,400,256]{2,1,0:T(8,128)(2,1)}), bf16[16,400,256]{2,1,0:T(8,128)(2,1)S(1)}, u32[]{:S(2)}, u32[]{:S(2)}) %all-to-all-start) | async-done | bytes 3276832 | tf_op jit(solution)/shard_map/all_to_all | solution.py:578
  87.3 0.8 copy-done.18
  88.1 15.8 %mixer.1.after = bf16[16,272,256]{2,1,0:T(8,128)(2,1)S(1)} custom-call(s32[4]{0:T(128)S(1)} %copy-done.19, s32[1]{0:T(128)} %bitcast.idx_ref, f32[32]{0:T(128)S(1)} %copy-done.20, bf16[16,400,256]{2,1,0:T(8,128)(2,1)S(1)} %all-to-all-done.r_ref, f32[4,4096]{1,0:T(4,128)S(1)} %copy-done.18, f32[4,512]{1,0:T(4,128)S(1)} %bitcast.10), custom_call_target="tpu_custom_call" | custom-call | flops 3000000000 | bytes 6291456 | tf_op jit(solution)/shard_map/mixer/pallas_call | solution.py:258
  103.9 1.4 copy-done.1
  105.2 1.4 copy.29.refs_0_
  106.7 0.0 collective-permute-done.10.refs_5_.r4
  106.7 0.0 collective-permute-done.7.refs_2_.r1
  106.7 0.0 collective-permute-done.8.refs_3_.r2
  106.7 0.0 collective-permute-done.9.refs_4_.r3
  106.7 0.0 collective-permute-done.6.refs_1_
  106.7 0.6 copy-done.21
  107.3 4.1 %all-to-all-start.1 = ((bf16[16,272,256]{2,1,0:T(8,128)(2,1)}), bf16[16,272,256]{2,1,0:T(8,128)(2,1)S(1)}, u32[]{:S(2)}, u32[]{:S(2)}) async-start(bf16[16,272,256]{2,1,0:T(8,128)(2,1)} %gate.5), calls=%async_computation.1 | async-start | bytes 4456448 | tf_op jit(solution)/shard_map/all_to_all | solution.py:578
  111.4 1.0 broadcast_select_fusion.1
  112.4 1.9 %kv_total.1 = (bf16[128,256]{1,0:T(8,128)(2,1)}, bf16[128,256]{1,0:T(8,128)(2,1)}) custom-call(s32[1]{0:T(128)} %bitcast.idx_ref, f32[256,256]{1,0:T(8,128)} %copy-done.5, bf16[256,256]{1,0:T(8,128)(2,1)} %collective-permute-done.7.refs_2_.r1, bf16[256,256]{1,0:T(8,128)(2,1)} %collective-permute-done.8.refs_3_.r2, ...), custom_call_target="tpu_custom_call" | custom-call | tf_op jit(solution)/shard_map/kv_total/pallas_call | solution.py:545
  114.3 1.9 %collective-permute-start.11 = (bf16[128,256]{1,0:T(8,128)(2,1)}, bf16[128,256]{1,0:T(8,128)(2,1)S(1)}, u32[]{:S(2)}, u32[]{:S(2)}) collective-permute-start(bf16[128,256]{1,0:T(8,128)(2,1)} %get-tuple-element.49), channel_id=1, source_target_pairs={{0,8},{8,0},{16,24},{24,16},{32,40},{40,32},{48,56},{56,48},{64,72... | collective-permute-start | bytes 196616 | tf_op jit(solution)/shard_map/ppermute | solution.py:411
  116.3 0.8 pad_maximum_fusion.1
  117.1 26.7 %collective-permute-done.11.other = bf16[128,256]{1,0:T(8,128)(2,1)S(1)} collective-permute-done((bf16[128,256]{1,0:T(8,128)(2,1)}, bf16[128,256]{1,0:T(8,128)(2,1)S(1)}, u32[]{:S(2)}, u32[]{:S(2)}) %collective-permute-start.11) | collective-permute-done | bytes 65568 | tf_op jit(solution)/shard_map/ppermute | solution.py:411
  143.8 0.6 copy-done.22
  144.4 1.5 %kv_place.1 = (bf16[128,256]{1,0:T(8,128)(2,1)}, bf16[128,256]{1,0:T(8,128)(2,1)}) custom-call(s32[1]{0:T(128)} %bitcast.idx_ref, bf16[128,256]{1,0:T(8,128)(2,1)} %get-tuple-element.48.mine, bf16[128,256]{1,0:T(8,128)(2,1)} %copy-done.22), custom_call_target="tpu_custom_call" | custom-call | tf_op jit(solution)/shard_map/kv_place/pallas_call | solution.py:568
  145.9 0.0 all-to-all-done.1.part
  145.9 1.7 %unpack.1 = (bf16[128,4096]{1,0:T(8,128)(2,1)}, bf16[128,512]{1,0:T(8,128)(2,1)S(1)}, f32[32,128]{1,0:T(8,128)}, f32[4,4096]{1,0:T(4,128)}, f32[4,2,256]{2,1,0:T(2,128)}) custom-call(bf16[16,272,256]{2,1,0:T(8,128)(2,1)S(1)} %all-to-all-done.1.part), custom_call_target="tpu_custom_call" | custom-call | flops 1000000 | bytes 4194304 | tf_op jit(solution)/shard_map/unpack/pallas_call | solution.py:495
  147.7 0.7 reshape.35
  (32 shorter events, 0.1 us)
Async XLA Ops:
  0.6 4.2 %copy-start = (bf16[128,2,256]{2,1,0:T(2,128)(2,1)S(1)}, bf16[128,2,256]{2,1,0:T(2,128)(2,1)}, u32[]{:S(2)}) copy-start(bf16[128,2,256]{2,1,0:T(2,128)(2,1)} %param.13) | copy-start | bytes 393220
  1.5 8.0 %collective-permute-start.1 = (bf16[128,256]{1,0:T(8,128)(2,1)S(1)}, bf16[128,256]{1,0:T(8,128)(2,1)S(1)}, u32[]{:S(2)}, u32[]{:S(2)}) collective-permute-start(bf16[128,256]{1,0:T(8,128)(2,1)S(1)} %pad_maximum_fusion.4), channel_id=1, source_target_pairs={{0,8},{8,0},{16,24},{24,16},{32,40},{40,32},{48,56},{56,48},{64,72... | collective-permute-start | bytes 196616 | tf_op jit(solution)/shard_map/ppermute | solution.py:411
  4.3 26.0 %collective-permute-start = (bf16[128,2048]{1,0:T(8,128)(2,1)S(1)}, bf16[128,2048]{1,0:T(8,128)(2,1)S(1)}, u32[]{:S(2)}, u32[]{:S(2)}) collective-permute-start(bf16[128,2048]{1,0:T(8,128)(2,1)S(1)} %pad_maximum_fusion), channel_id=1, source_target_pairs={{0,8},{8,0},{16,24},{24,16},{32,40},{40,32},{48,56},{56,48},{64,72... | collective-permute-start | bytes 1572872 | tf_op jit(solution)/shard_map/ppermute | solution.py:411
  10.3 15.3 %collective-permute-start.2 = (bf16[256,256]{1,0:T(8,128)(2,1)}, bf16[256,256]{1,0:T(8,128)(2,1)S(1)}, u32[]{:S(2)}, u32[]{:S(2)}) collective-permute-start(bf16[256,256]{1,0:T(8,128)(2,1)} %gate.3.kv0), channel_id=1, source_target_pairs={{0,16},{8,24},{16,32},{24,40},{32,48},{40,56},{48,64},{56,72},{64,... | collective-permute-start | bytes 393224 | tf_op jit(solution)/shard_map/ppermute | solution.py:405
  15.3 10.3 %collective-permute-start.3 = (bf16[256,256]{1,0:T(8,128)(2,1)}, bf16[256,256]{1,0:T(8,128)(2,1)S(1)}, u32[]{:S(2)}, u32[]{:S(2)}) collective-permute-start(bf16[256,256]{1,0:T(8,128)(2,1)} %gate.3.kv0), channel_id=1, source_target_pairs={{0,32},{8,40},{16,48},{24,56},{32,64},{40,72},{48,80},{56,88},{64,... | collective-permute-start | bytes 393224 | tf_op jit(solution)/shard_map/ppermute | solution.py:405
  18.8 7.0 %collective-permute-start.4 = (bf16[256,256]{1,0:T(8,128)(2,1)}, bf16[256,256]{1,0:T(8,128)(2,1)S(1)}, u32[]{:S(2)}, u32[]{:S(2)}) collective-permute-start(bf16[256,256]{1,0:T(8,128)(2,1)} %gate.3.kv0), channel_id=1, source_target_pairs={{0,48},{8,56},{16,64},{24,72},{32,80},{40,88},{48,96},{56,104},{64... | collective-permute-start | bytes 393224 | tf_op jit(solution)/shard_map/ppermute | solution.py:405
  23.0 7.3 %collective-permute-start.5 = (bf16[256,256]{1,0:T(8,128)(2,1)}, bf16[256,256]{1,0:T(8,128)(2,1)S(1)}, u32[]{:S(2)}, u32[]{:S(2)}) collective-permute-start(bf16[256,256]{1,0:T(8,128)(2,1)} %gate.3.kv0), channel_id=1, source_target_pairs={{0,64},{8,72},{16,80},{24,88},{32,96},{40,104},{48,112},{56,120},{... | collective-permute-start | bytes 393224 | tf_op jit(solution)/shard_map/ppermute | solution.py:405
  25.6 4.7 %copy-start.10 = (bf16[256,256]{1,0:T(8,128)(2,1)}, bf16[256,256]{1,0:T(8,128)(2,1)S(1)}, u32[]{:S(2)}) copy-start(bf16[256,256]{1,0:T(8,128)(2,1)S(1)} %collective-permute-done.2.kv1.refs_2_) | copy-start | bytes 393220
  25.6 4.7 %copy-start.12 = (bf16[256,256]{1,0:T(8,128)(2,1)}, bf16[256,256]{1,0:T(8,128)(2,1)S(1)}, u32[]{:S(2)}) copy-start(bf16[256,256]{1,0:T(8,128)(2,1)S(1)} %collective-permute-done.3.kv2.refs_3_) | copy-start | bytes 393220
  25.8 4.5 %copy-start.14 = (bf16[256,256]{1,0:T(8,128)(2,1)}, bf16[256,256]{1,0:T(8,128)(2,1)S(1)}, u32[]{:S(2)}) copy-start(bf16[256,256]{1,0:T(8,128)(2,1)S(1)} %collective-permute-done.4.kv3.refs_4_) | copy-start | bytes 393220
  30.3 0.6 copy-start.16
  30.9 0.8 copy-start.3
  31.7 6.6 %copy-start.2 = (bf16[256,256]{1,0:T(8,128)(2,1)S(1)}, bf16[256,256]{1,0:T(8,128)(2,1)}, u32[]{:S(2)}) copy-start(bf16[256,256]{1,0:T(8,128)(2,1)} %gate.3.kv0) | copy-start | bytes 393220
  31.7 6.6 %copy-start.19 = (s32[4]{0:T(128)S(1)}, s32[4]{0:T(128)}, u32[]{:S(2)}) copy-start(s32[4]{0:T(128)} %doc_ref.3) | copy-start | bytes 52
  31.7 55.5 %all-to-all-start = ((bf16[16,400,256]{2,1,0:T(8,128)(2,1)}), bf16[16,400,256]{2,1,0:T(8,128)(2,1)S(1)}, u32[]{:S(2)}, u32[]{:S(2)}) async-start(bf16[16,400,256]{2,1,0:T(8,128)(2,1)} %gate.4), calls=%async_computation | async-start | bytes 6553600 | tf_op jit(solution)/shard_map/all_to_all | solution.py:578
  38.3 1.0 copy-start.4
  39.3 1.0 copy-start.8
  40.4 1.0 copy-start.9
  41.4 0.9 copy-start.11
  42.3 0.9 copy-start.13
  43.2 0.9 copy-start.15
  44.1 0.9 copy-start.17
  45.0 42.2 %copy-start.20 = (f32[32]{0:T(128)S(1)}, f32[32]{0:T(128)}, u32[]{:S(2)}) copy-start(f32[32]{0:T(128)} %rate_ref.1) | copy-start | bytes 388
  60.4 0.7 copy-start.5
  61.1 0.7 copy-start.6
  61.8 44.8 %collective-permute-start.10 = (bf16[256,256]{1,0:T(8,128)(2,1)}, bf16[256,256]{1,0:T(8,128)(2,1)S(1)}, u32[]{:S(2)}, u32[]{:S(2)}) collective-permute-start(bf16[256,256]{1,0:T(8,128)(2,1)} %get-tuple-element.40), channel_id=1, source_target_pairs={{64,0},{72,8},{80,16},{88,24},{96,32},{104,40},{112,48},{120,56},{... | collective-permute-start | bytes 393224 | tf_op jit(solution)/shard_map/ppermute | solution.py:405
  63.1 43.6 %collective-permute-start.7 = (bf16[256,256]{1,0:T(8,128)(2,1)}, bf16[256,256]{1,0:T(8,128)(2,1)}, u32[]{:S(2)}, u32[]{:S(2)}) collective-permute-start(bf16[256,256]{1,0:T(8,128)(2,1)} %get-tuple-element.37), channel_id=1, source_target_pairs={{16,0},{24,8},{32,16},{40,24},{48,32},{56,40},{64,48},{72,56},{80,... | collective-permute-start | bytes 393224 | tf_op jit(solution)/shard_map/ppermute | solution.py:405
  64.4 42.3 %collective-permute-start.8 = (bf16[256,256]{1,0:T(8,128)(2,1)}, bf16[256,256]{1,0:T(8,128)(2,1)}, u32[]{:S(2)}, u32[]{:S(2)}) collective-permute-start(bf16[256,256]{1,0:T(8,128)(2,1)} %get-tuple-element.38), channel_id=1, source_target_pairs={{32,0},{40,8},{48,16},{56,24},{64,32},{72,40},{80,48},{88,56},{96,... | collective-permute-start | bytes 393224 | tf_op jit(solution)/shard_map/ppermute | solution.py:405
  65.7 41.0 %collective-permute-start.9 = (bf16[256,256]{1,0:T(8,128)(2,1)}, bf16[256,256]{1,0:T(8,128)(2,1)}, u32[]{:S(2)}, u32[]{:S(2)}) collective-permute-start(bf16[256,256]{1,0:T(8,128)(2,1)} %get-tuple-element.39), channel_id=1, source_target_pairs={{48,0},{56,8},{64,16},{72,24},{80,32},{88,40},{96,48},{104,56},{11... | collective-permute-start | bytes 393224 | tf_op jit(solution)/shard_map/ppermute | solution.py:405
  67.0 39.7 %collective-permute-start.6 = (bf16[128,1024]{1,0:T(8,128)(2,1)}, bf16[128,1024]{1,0:T(8,128)(2,1)}, u32[]{:S(2)}, u32[]{:S(2)}) collective-permute-start(bf16[128,1024]{1,0:T(8,128)(2,1)} %get-tuple-element.36), channel_id=1, source_target_pairs={{0,8},{8,0},{16,24},{24,16},{32,40},{40,32},{48,56},{56,48},{64,72... | collective-permute-start | bytes 786440 | tf_op jit(solution)/shard_map/ppermute | solution.py:411
  87.3 0.8 copy-start.18
  103.9 1.4 copy-start.1
  106.7 0.7 copy-start.21
  107.3 4.1 %copy-start.7 = (bf16[128,1024]{1,0:T(8,128)(2,1)S(1)}, bf16[128,1024]{1,0:T(8,128)(2,1)}, u32[]{:S(2)}) copy-start(bf16[128,1024]{1,0:T(8,128)(2,1)} %copy-done.6) | copy-start | bytes 786436
  107.3 38.6 %all-to-all-start.1 = ((bf16[16,272,256]{2,1,0:T(8,128)(2,1)}), bf16[16,272,256]{2,1,0:T(8,128)(2,1)S(1)}, u32[]{:S(2)}, u32[]{:S(2)}) async-start(bf16[16,272,256]{2,1,0:T(8,128)(2,1)} %gate.5), calls=%async_computation.1 | async-start | bytes 4456448 | tf_op jit(solution)/shard_map/all_to_all | solution.py:578
  114.3 29.4 %collective-permute-start.11 = (bf16[128,256]{1,0:T(8,128)(2,1)}, bf16[128,256]{1,0:T(8,128)(2,1)S(1)}, u32[]{:S(2)}, u32[]{:S(2)}) collective-permute-start(bf16[128,256]{1,0:T(8,128)(2,1)} %get-tuple-element.49), channel_id=1, source_target_pairs={{0,8},{8,0},{16,24},{24,16},{32,40},{40,32},{48,56},{56,48},{64,72... | collective-permute-start | bytes 196616 | tf_op jit(solution)/shard_map/ppermute | solution.py:411
  143.8 0.6 copy-start.22

commit v3 on v2

--- a/solution.py
+++ b/solution.py
@@ -287,12 +287,11 @@
 
 
 def attention_kernel(
-    doc_ref, idx_ref, q_ref, do_ref, got_ref, kv0, kv1, kv2, kv3, kv4,
+    doc_ref, idx_ref, q_ref, do_ref, got_ref, kv_ref,
     dq_own, dq_sent, d0, d1, d2, d3, d4, kt_s, dk_s, dv_s, s_s, p_s,
 ):
-    kv_refs = (kv4, kv3, kv2, kv1, kv0)
     d_refs = (d4, d3, d2, d1, d0)
-    count = 2 * len(kv_refs)
+    count = 2 * len(d_refs)
     bounds = doc_bounds(doc_ref)
     scale = HD ** (-0.5)
     place = idx_ref[0]
@@ -310,10 +309,10 @@
         return slice((b % 2) * BLK, (b % 2 + 1) * BLK)
 
     def key_rows(b):
-        return kv_refs[b // 2][half(b), 0:HD]
+        return kv_ref[jnp.maximum(place - odd - BACK + b, 0), :, 0:HD]
 
     def value_rows(b):
-        return kv_refs[b // 2][half(b), HD : 2 * HD]
+        return kv_ref[jnp.maximum(place - odd - BACK + b, 0), :, HD : 2 * HD]
 
     def in_order(own, other):
         first = jnp.where(odd == 0, own, other)
@@ -372,20 +371,20 @@
         out[half(b), HD : 2 * HD] = dv_s[b].astype(out.dtype)
 
 
-def attention_core(doc_lengths, place, query, d_out, got, kv_pairs):
+def attention_core(doc_lengths, place, query, d_out, got, kv):
     smem = pl.BlockSpec(memory_space=pltpu.SMEM)
     vmem = pl.BlockSpec(memory_space=pltpu.VMEM)
-    pairs = len(kv_pairs)
+    pairs = BACK // 2 + 1
     count = 2 * pairs
     rows, width = query.shape
     part = jax.ShapeDtypeStruct((rows, width // 2), BF16)
-    kv_shape = kv_pairs[0].shape
+    kv_shape = (2 * rows, 2 * HD)
     outs = [part, part, jax.ShapeDtypeStruct(kv_shape, F32)]
     outs += [jax.ShapeDtypeStruct(kv_shape, BF16)] * (pairs - 1)
     return pl.pallas_call(
         attention_kernel,
         out_shape=outs,
-        in_specs=[smem, smem] + [vmem] * (3 + pairs),
+        in_specs=[smem, smem] + [vmem] * 4,
         out_specs=[vmem] * (2 + pairs),
         scratch_shapes=[
             pltpu.VMEM((count, HD, BLK), BF16),
@@ -397,7 +396,7 @@
         compiler_params=pltpu.CompilerParams(vmem_limit_bytes=16 * 2**20),
         cost_estimate=pl.CostEstimate(flops=4 * 10**9, bytes_accessed=4 * 2**20, transcendentals=3 * 10**6),
         name="attention",
-    )(doc_lengths, place, query, d_out, got, *kv_pairs)
+    )(doc_lengths, place, query, d_out, got, kv)
 
 
 def shift(a, by):
@@ -458,7 +457,9 @@
     )(x_in, grad, bc_sent, dt_raw)
 
 
-def unpack_kernel(part, dx_ref, dbc_ref, dt_ref, wx_ref, wbc_ref, sems):
+def unpack_kernel(
+    idx_ref, part, dq_own, dq_got, own, dx_ref, dbc_ref, dt_ref, wx_ref, wbc_ref, dq_ref, passed, sems
+):
     blocks = part.shape[0]
     half = blocks // 2
     copies = []
@@ -484,11 +485,16 @@
         dt_ref[2 * d : 2 * d + 1] = raw[:, :BLK]
         dt_ref[2 * d + 1 : 2 * d + 2] = raw[:, BLK:]
         wx_ref[:, d * 2 * HD : (d + 1) * 2 * HD] = small[2:6] + small[6:10]
+    odd = lax.rem(idx_ref[0], 2)
+    a = dq_own[...]
+    b = dq_got[...]
+    dq_ref[:, : a.shape[1]] = jnp.where(odd == 0, a, b)
+    dq_ref[:, a.shape[1] :] = jnp.where(odd == 0, b, a)
     for done in copies:
         done.wait()
 
 
-def unpack(received):
+def unpack(place, received, dq_own, dq_got, own):
     blocks = received.shape[0]
     hbm = pl.BlockSpec(memory_space=pltpu.HBM)
     vmem = pl.BlockSpec(memory_space=pltpu.VMEM)
@@ -500,14 +506,17 @@
             jax.ShapeDtypeStruct((2 * blocks, BLK), F32),
             jax.ShapeDtypeStruct((TAPS, blocks * 2 * HD), F32),
             jax.ShapeDtypeStruct((TAPS, 2, 2 * HD), F32),
+            jax.ShapeDtypeStruct((BLK, 2 * dq_own.shape[1]), BF16),
+            jax.ShapeDtypeStruct(own.shape, own.dtype),
         ],
-        in_specs=[vmem],
-        out_specs=[hbm, vmem, vmem, vmem, vmem],
+        in_specs=[pl.BlockSpec(memory_space=pltpu.SMEM), vmem, vmem, vmem, pl.BlockSpec(memory_space=pl.ANY)],
+        out_specs=[hbm, vmem, vmem, vmem, vmem, vmem, pl.BlockSpec(memory_space=pl.ANY)],
+        input_output_aliases={4: 6},
         scratch_shapes=[pltpu.SemaphoreType.DMA((blocks,))],
         compiler_params=pltpu.CompilerParams(vmem_limit_bytes=8 * 2**20),
         cost_estimate=pl.CostEstimate(flops=10**6, bytes_accessed=4 * 2**20, transcendentals=0),
         name="unpack",
-    )(received)
+    )(place, received, dq_own, dq_got, own)
 
 
 def gate_kernel(*refs):
@@ -523,11 +532,31 @@
         in_specs=[hbm] + [anywhere] * len(others),
         out_specs=hbm,
         input_output_aliases={0: 0},
+        compiler_params=pltpu.CompilerParams(vmem_limit_bytes=2**20),
         name="gate",
     )(value, *others)
 
 
-def kv_sum_kernel(idx_ref, own, r1, r2, r3, r4, after, mine, sent):
+def kv_pack_kernel(k_ref, v_ref, got, kv_ref):
+    for d in range(kv_ref.shape[0]):
+        head = slice((d % 2) * HD, (d % 2 + 1) * HD)
+        kv_ref[d] = jnp.concatenate([k_ref[:, head], v_ref[:, head]], axis=1)
+
+
+def kv_pack(key, value, got):
+    vmem = pl.BlockSpec(memory_space=pltpu.VMEM)
+    shape = (got.shape[0],) + key.shape
+    return pl.pallas_call(
+        kv_pack_kernel,
+        out_shape=jax.ShapeDtypeStruct(shape, BF16),
+        in_specs=[vmem, vmem, pl.BlockSpec(memory_space=pl.ANY)],
+        out_specs=vmem,
+        compiler_params=pltpu.CompilerParams(vmem_limit_bytes=4 * 2**20),
+        name="kv_pack",
+    )(key, value, got)
+
+
+def kv_sum_kernel(idx_ref, own, r1, r2, r3, r4, mine, sent):
     total = own[...]
     for got in (r1, r2, r3, r4):
         total = total + got[...].astype(F32)
@@ -539,18 +568,18 @@
     sent[...] = jnp.where(odd == 0, second, first)
 
 
-def kv_total(place, own, received, after):
+def kv_total(place, own, received):
     vmem = pl.BlockSpec(memory_space=pltpu.VMEM)
     half = jax.ShapeDtypeStruct((own.shape[0] // 2, own.shape[1]), BF16)
     return pl.pallas_call(
         kv_sum_kernel,
         out_shape=[half, half],
         in_specs=[pl.BlockSpec(memory_space=pltpu.SMEM)]
-        + [vmem] * (1 + len(received))
-        + [pl.BlockSpec(memory_space=pl.ANY)],
+        + [vmem] * (1 + len(received)),
         out_specs=[vmem, vmem],
+        compiler_params=pltpu.CompilerParams(vmem_limit_bytes=4 * 2**20),
         name="kv_total",
-    )(place, own, *received, after)
+    )(place, own, *received)
 
 
 def kv_place_kernel(idx_ref, mine, other, dk_ref, dv_ref):
@@ -570,6 +599,7 @@
         out_shape=[jax.ShapeDtypeStruct(mine.shape, BF16)] * 2,
         in_specs=[pl.BlockSpec(memory_space=pltpu.SMEM), vmem, vmem],
         out_specs=[vmem, vmem],
+        compiler_params=pltpu.CompilerParams(vmem_limit_bytes=4 * 2**20),
         name="kv_place",
     )(place, mine, other)
 
@@ -595,24 +625,20 @@
 
     bc_sent = bc_in.reshape(rows, 2, 2, HD).transpose(2, 0, 1, 3).reshape(2, rows, 2 * HD)
     packed = pack(x_in, grad_ssd, bc_sent, dt_raw, ctx)
-    kv_own = jnp.concatenate([half(key, odd), half(value, odd)], axis=1)
-    kv_got = partner(jnp.concatenate([half(key, 1 - odd), half(value, 1 - odd)], axis=1))
-    kv_pair = gate(jnp.concatenate(pick(kv_own, kv_got), axis=0), packed)
-    got_qo = partner(jnp.concatenate([half(query, 1 - odd), half(d_out, 1 - odd)], axis=1))
-    kv_pairs = [kv_pair] + [shift(kv_pair, 2 * by) for by in range(1, BACK // 2 + 1)]
-    got = swap(gate(packed, got_qo, *kv_pairs[1:]))
-    dq_own, dq_sent, *d_kv = attention_core(doc_lengths, place, query, d_out, got_qo, kv_pairs)
-    place_after, *d_kv = lax.optimization_barrier((place, *d_kv))
-    mixed = ssm_core(
-        doc_lengths, place_after, rate, got, conv_x, conv_bc.reshape(TAPS, 4 * HD)
+    qo = jnp.concatenate([half(query, 1 - odd), half(d_out, 1 - odd)], axis=1)
+    got = swap(packed)
+    kv = swap(kv_pack(key, value, got))
+    got_qo = partner(qo)
+    mixed = ssm_core(doc_lengths, place, rate, got, conv_x, conv_bc.reshape(TAPS, 4 * HD))
+    mixed, kv, got_qo = lax.optimization_barrier((mixed, kv, got_qo))
+    back = swap(mixed)
+    dq_own, dq_sent, *d_kv = attention_core(doc_lengths, place, query, d_out, got_qo, kv)
+    received = [shift(d_kv[by], -2 * by) for by in range(1, BACK // 2 + 1)]
+    d_x, d_bc, d_dt, d_wx, d_wbc, d_query, own = unpack(
+        place, back, dq_own, partner(dq_sent), d_kv[0]
     )
-    dq_got = partner(dq_sent)
-    received = [shift(d_kv[by], -2 * by) for by in range(1, BACK // 2 + 1)]
-    back = swap(gate(mixed, dq_got, *received))
-    mine, sent = kv_total(place, d_kv[0], received, mixed)
+    mine, sent = kv_total(place, own, received)
     d_key, d_value = kv_place(place, mine, partner(sent))
-    d_query = jnp.concatenate(pick(dq_own, dq_got), axis=1)
-    d_x, d_bc, d_dt, d_wx, d_wbc = unpack(back)
     return (
         d_x,
         d_bc.reshape(rows, 2, 2 * HD),

time: 149 us -> 137 us (0.919); the launches traced: 148 us -> 134 us
  blocking collectives: 0 us -> 48.3 us
  waiting for transfers between devices: 49.6 us -> 16.8 us
  starting transfers between devices: 36.4 us -> 20.4 us
  local copies, waits for them, and re-layouts: 18.6 us -> 8.75 us
  other arithmetic: 2.56 us -> 0.04 us
    all_to_all x0 -> x1, blocking collectives: none -> 48.3 us  [swap(): return lax.all_to_all(a, 'ctx', 0, 0, tiled=True)]
    all_to_all x2, waiting for transfers between devices: 18.2 us -> 0.84 us  [swap(): return lax.all_to_all(a, 'ctx', 0, 0, tiled=True)]
    ppermute x4 -> x3, waiting for transfers between devices: 26.7 us -> 11.5 us  [partner(): lax.ppermute(a, 'ctx', [(i, i ^ 1) for i in range(lax.axis_size('ctx'))])]
    ppermute x8 -> x4, starting transfers between devices: 20.4 us -> 5.16 us  [shift(): lax.ppermute(a, 'ctx', [(i, i + by) for i in range(devices) if 0 <= i + b...]
    unnamed x48 -> x27, local copies, waits for them, and re-layouts: 15.2 us -> 6.15 us
    ppermute x4 -> x3, starting transfers between devices: 6.14 us -> 4.36 us  [partner(): lax.ppermute(a, 'ctx', [(i, i ^ 1) for i in range(lax.axis_size('ctx'))])]
    concatenate x4 -> x1, other arithmetic: 1.54 us -> 0.04 us  [shards(): qo = jnp.concatenate([half(query, 1 - odd), half(d_out, 1 - odd)], axis=1)]
    ppermute x8 -> x4, waiting for transfers between devices: 4.7 us -> 4.48 us  [shift(): lax.ppermute(a, 'ctx', [(i, i + by) for i in range(devices) if 0 <= i + b...]
  transfers between devices with their start and end apart: 14 -> 9, of which waited for: 4 -> 6; matrix products, arithmetic and copies ran while one was open for 4% -> 1% of each run, Pallas kernels for 26% -> 25%
where the time goes in v3:
time: 137 us; the launch traced here: 134 us
  blocking collectives  48.3 us (35%)
  Pallas kernels  39.4 us (29%)
  starting transfers between devices  20.4 us (15%)
  waiting for transfers between devices  16.8 us (12%)
  local copies, waits for them, and re-layouts  8.75 us (6%)
    all_to_all x1, blocking collectives, swap(): return lax.all_to_all(a, 'ctx', 0, 0, tiled=True)  48.3 us
    pallas_call x1, Pallas kernels, attention_core(): pl.pallas_call(attention_kernel, out_shape=outs, in_specs=[smem, smem] +...  16.1 us
    pallas_call x1, Pallas kernels, ssm_core(): pl.pallas_call(ssm_kernel, out_shape=jax.ShapeDtypeStruct((blocks, 2 * BL...  15.7 us
    ppermute x3, waiting for transfers between devices, partner(): lax.ppermute(a, 'ctx', [(i, i ^ 1) for i in range(lax.axis_size('ctx'))])  11.5 us
    all_to_all x2, starting transfers between devices, swap(): return lax.all_to_all(a, 'ctx', 0, 0, tiled=True)  10.9 us
    unnamed x27, local copies, waits for them, and re-layouts  6.15 us
    ppermute x4, starting transfers between devices, shift(): lax.ppermute(a, 'ctx', [(i, i + by) for i in range(devices) if 0 <= i + b...  5.16 us
    ppermute x4, waiting for transfers between devices, shift(): lax.ppermute(a, 'ctx', [(i, i + by) for i in range(devices) if 0 <= i + b...  4.48 us
  transfers between devices with their start and end apart: 9, of which 6 were waited for; matrix products, arithmetic and copies ran while one was open for 1% of the time, Pallas kernels for 25%

profile of v3, /device:TPU:0, one launch (start us, length us, event | category | flops | bytes accessed | tf_op | source)
XLA Modules:
  0.0 134.5 jit_solution(2496165648204907260)
XLA Ops:
  0.6 0.0 copy-start
  0.6 0.9 copy-done
  1.5 0.1 bitcast_bitcast_fusion
  1.6 0.7 reshape.33.bc_ref
  2.4 3.9 %pack.1 = bf16[16,400,256]{2,1,0:T(8,128)(2,1)} custom-call(bf16[128,4096]{1,0:T(8,128)(2,1)} %x_ref.1, bf16[128,4096]{1,0:T(8,128)(2,1)} %g_ref.1, bf16[2,128,256]{2,1,0:T(8,128)(2,1)} %reshape.33.bc_ref, f32[32,128]{1,0:T(8,128)} %dt_ref.1), custom_call_target="tpu_custom_call" | custom-call | bytes 7340032 | tf_op jit(solution)/shard_map/pack/pallas_call | solution.py:445
  6.3 0.0 copy-start.5
  6.3 0.0 copy-start.6
  6.3 48.3 %all_to_all.15.r_ref.got = bf16[16,400,256]{2,1,0:T(8,128)(2,1)S(1)} all-to-all(bf16[16,400,256]{2,1,0:T(8,128)(2,1)} %pack.1), channel_id=1, replica_groups=mesh['ctx'=16,'head'=2,'dp'=4] {'ctx'}, dimensions={0} | all-to-all | bytes 6553600 | tf_op jit(solution)/shard_map/all_to_all | solution.py:608
  54.6 0.0 copy-done.5
  54.6 0.0 copy-done.6
  54.6 0.0 copy-start.12
  54.6 0.0 copy-start.9
  54.6 0.0 copy-start.10
  54.6 0.0 copy-start.11
  54.6 0.1 kv_pack.1
  54.7 0.0 copy-start.1
  54.7 1.0 copy-done.1
  55.7 4.3 %all-to-all-start.1 = ((bf16[16,128,256]{2,1,0:T(8,128)(2,1)}), bf16[16,128,256]{2,1,0:T(8,128)(2,1)}, u32[]{:S(2)}, u32[]{:S(2)}) async-start(bf16[16,128,256]{2,1,0:T(8,128)(2,1)} %copy-done.1), calls=%async_computation.1 | async-start | bytes 2097152 | tf_op jit(solution)/shard_map/all_to_all | solution.py:608
  60.0 1.1 constant_dynamic-slice_fusion
  61.2 1.8 %collective-permute-start = (bf16[128,2048]{1,0:T(8,128)(2,1)S(1)}, bf16[128,2048]{1,0:T(8,128)(2,1)S(1)}, u32[]{:S(2)}, u32[]{:S(2)}) collective-permute-start(bf16[128,2048]{1,0:T(8,128)(2,1)S(1)} %pad_maximum_fusion), channel_id=1, source_target_pairs={{0,8},{8,0},{16,24},{24,16},{32,40},{40,32},{48,56},{56,48},{64,72... | collective-permute-start | bytes 1572872 | tf_op jit(solution)/shard_map/ppermute | solution.py:410
  63.0 0.0 copy-done.12
  63.0 0.0 copy-done.9
  63.0 0.0 copy-done.10
  63.0 0.0 copy-done.11
  63.0 15.7 %mixer.1 = bf16[16,272,256]{2,1,0:T(8,128)(2,1)S(1)} custom-call(s32[4]{0:T(128)S(1)} %copy-done.11, s32[1]{0:T(128)} %bitcast.idx_ref, f32[32]{0:T(128)S(1)} %copy-done.10, bf16[16,400,256]{2,1,0:T(8,128)(2,1)S(1)} %all_to_all.15.r_ref.got, f32[4,4096]{1,0:T(4,128)S(1)} %copy-done.9, f32[4,512]{1,0:T(4,128)S(1)} %bitcast.10), custom_call_target="tpu_custom_call" | custom-call | flops 3000000000 | bytes 6291456 | tf_op jit(solution)/shard_map/mixer/pallas_call | solution.py:258
  78.7 0.0 copy-start.2
  78.7 1.4 %copy-done.2 = bf16[16,272,256]{2,1,0:T(8,128)(2,1)} copy-done((bf16[16,272,256]{2,1,0:T(8,128)(2,1)}, bf16[16,272,256]{2,1,0:T(8,128)(2,1)S(1)}, u32[]{:S(2)}) %copy-start.2) | copy-done | bytes 2228248
  80.1 0.0 copy-start.3
  80.1 3.4 %collective-permute-done.got_ref = bf16[128,2048]{1,0:T(8,128)(2,1)S(1)} collective-permute-done((bf16[128,2048]{1,0:T(8,128)(2,1)S(1)}, bf16[128,2048]{1,0:T(8,128)(2,1)S(1)}, u32[]{:S(2)}, u32[]{:S(2)}) %collective-permute-start) | collective-permute-done | bytes 524320 | tf_op jit(solution)/shard_map/ppermute | solution.py:410
  83.5 0.0 copy-start.7
  83.5 0.8 copy-done.7
  84.3 0.0 all-to-all-done.1.kv_ref
  84.3 6.5 %all-to-all-start.2 = ((bf16[16,272,256]{2,1,0:T(8,128)(2,1)}), bf16[16,272,256]{2,1,0:T(8,128)(2,1)S(1)}, u32[]{:S(2)}, u32[]{:S(2)}) async-start(bf16[16,272,256]{2,1,0:T(8,128)(2,1)} %copy-done.2), calls=%async_computation.2 | async-start | bytes 4456448 | tf_op jit(solution)/shard_map/all_to_all | solution.py:608
  90.8 0.0 copy-done.3
  90.8 0.0 copy-start.4
  90.8 1.0 copy-done.4
  91.9 0.0 copy-start.8
  91.9 1.0 copy-done.8
  92.9 16.1 %attention.1 = (bf16[128,1024]{1,0:T(8,128)(2,1)S(1)}, bf16[128,1024]{1,0:T(8,128)(2,1)S(1)}, f32[256,256]{1,0:T(8,128)S(1)}, bf16[256,256]{1,0:T(8,128)(2,1)}, ...) custom-call(s32[4]{0:T(128)S(1)} %copy-done.11, s32[1]{0:T(128)} %bitcast.idx_ref, ...), custom_call_target="tpu_custom_call" | custom-call | flops 4000000000 | bytes 4194304 | tf_op jit(solution)/shard_map/attention/pallas_call | solution.py:384
  109.0 1.9 %collective-permute-start.1 = (bf16[128,1024]{1,0:T(8,128)(2,1)S(1)}, bf16[128,1024]{1,0:T(8,128)(2,1)S(1)}, u32[]{:S(2)}, u32[]{:S(2)}) collective-permute-start(bf16[128,1024]{1,0:T(8,128)(2,1)S(1)} %get-tuple-element.33), channel_id=1, source_target_pairs={{0,8},{8,0},{16,24},{24,16},{32,40},{40,32},{48,56},{56,48},{64,72... | collective-permute-start | bytes 786440 | tf_op jit(solution)/shard_map/ppermute | solution.py:410
  110.9 1.3 collective-permute-start.2
  112.2 1.3 collective-permute-start.3
  113.5 1.3 collective-permute-start.4
  114.8 1.3 collective-permute-start.5
  116.1 5.1 %collective-permute-done.1.dq_got = bf16[128,1024]{1,0:T(8,128)(2,1)S(1)} collective-permute-done((bf16[128,1024]{1,0:T(8,128)(2,1)S(1)}, bf16[128,1024]{1,0:T(8,128)(2,1)S(1)}, u32[]{:S(2)}, u32[]{:S(2)}) %collective-permute-start.1) | collective-permute-done | bytes 262176 | tf_op jit(solution)/shard_map/ppermute | solution.py:410
  121.2 0.8 all-to-all-done.2.part
  122.0 1.9 %unpack.1 = (bf16[128,4096]{1,0:T(8,128)(2,1)}, bf16[128,512]{1,0:T(8,128)(2,1)S(1)}, f32[32,128]{1,0:T(8,128)}, f32[4,4096]{1,0:T(4,128)}, f32[4,2,256]{2,1,0:T...) custom-call(s32[1]{0:T(128)} %bitcast.idx_ref, ...), custom_call_target="tpu_custom_call", output_to_operand_aliasing={{6}: (4, {})} | custom-call | flops 1000000 | bytes 4194304 | tf_op jit(solution)/shard_map/unpack/pallas_call | solution.py:501
  124.0 1.0 collective-permute-done.2.r1
  125.0 0.0 collective-permute-done.3.r2
  125.0 3.4 %collective-permute-done.4.r3 = bf16[256,256]{1,0:T(8,128)(2,1)} collective-permute-done((bf16[256,256]{1,0:T(8,128)(2,1)}, bf16[256,256]{1,0:T(8,128)(2,1)}, u32[]{:S(2)}, u32[]{:S(2)}) %collective-permute-start.4) | collective-permute-done | bytes 131104 | tf_op jit(solution)/shard_map/ppermute | solution.py:404
  128.4 0.0 collective-permute-done.5.r4
  128.4 1.1 kv_total.1
  129.5 0.6 collective-permute-start.6
  130.1 0.7 reshape.35
  130.8 3.0 %collective-permute-done.6.other = bf16[128,256]{1,0:T(8,128)(2,1)S(1)} collective-permute-done((bf16[128,256]{1,0:T(8,128)(2,1)S(1)}, bf16[128,256]{1,0:T(8,128)(2,1)S(1)}, u32[]{:S(2)}, u32[]{:S(2)}) %collective-permute-start.6) | collective-permute-done | bytes 65568 | tf_op jit(solution)/shard_map/ppermute | solution.py:410
  133.8 0.7 kv_place.1
  (2 shorter events, 0.0 us)
Async XLA Ops:
  0.6 0.9 copy-start
  6.3 48.3 %copy-start.5 = (bf16[128,256]{1,0:T(8,128)(2,1)S(1)}, bf16[128,256]{1,0:T(8,128)(2,1)}, u32[]{:S(2)}) copy-start(bf16[128,256]{1,0:T(8,128)(2,1)} %k_ref.1) | copy-start | bytes 196612
  6.3 48.3 %copy-start.6 = (bf16[128,256]{1,0:T(8,128)(2,1)S(1)}, bf16[128,256]{1,0:T(8,128)(2,1)}, u32[]{:S(2)}) copy-start(bf16[128,256]{1,0:T(8,128)(2,1)} %v_ref.1) | copy-start | bytes 196612
  54.6 8.4 %copy-start.12 = (f32[4,2,256]{2,1,0:T(2,128)S(1)}, f32[4,2,256]{2,1,0:T(2,128)}, u32[]{:S(2)}) copy-start(f32[4,2,256]{2,1,0:T(2,128)} %param.15) | copy-start | bytes 24580
  54.6 8.4 %copy-start.9 = (f32[4,4096]{1,0:T(4,128)S(1)}, f32[4,4096]{1,0:T(4,128)}, u32[]{:S(2)}) copy-start(f32[4,4096]{1,0:T(4,128)} %wx_ref.1) | copy-start | bytes 196612
  54.6 8.4 %copy-start.10 = (f32[32]{0:T(128)S(1)}, f32[32]{0:T(128)}, u32[]{:S(2)}) copy-start(f32[32]{0:T(128)} %rate_ref.1) | copy-start | bytes 388
  54.6 8.4 %copy-start.11 = (s32[4]{0:T(128)S(1)}, s32[4]{0:T(128)}, u32[]{:S(2)}) copy-start(s32[4]{0:T(128)} %doc_ref.3) | copy-start | bytes 52
  54.7 1.0 copy-start.1
  55.7 28.6 %all-to-all-start.1 = ((bf16[16,128,256]{2,1,0:T(8,128)(2,1)}), bf16[16,128,256]{2,1,0:T(8,128)(2,1)}, u32[]{:S(2)}, u32[]{:S(2)}) async-start(bf16[16,128,256]{2,1,0:T(8,128)(2,1)} %copy-done.1), calls=%async_computation.1 | async-start | bytes 2097152 | tf_op jit(solution)/shard_map/all_to_all | solution.py:608
  61.2 22.3 %collective-permute-start = (bf16[128,2048]{1,0:T(8,128)(2,1)S(1)}, bf16[128,2048]{1,0:T(8,128)(2,1)S(1)}, u32[]{:S(2)}, u32[]{:S(2)}) collective-permute-start(bf16[128,2048]{1,0:T(8,128)(2,1)S(1)} %pad_maximum_fusion), channel_id=1, source_target_pairs={{0,8},{8,0},{16,24},{24,16},{32,40},{40,32},{48,56},{56,48},{64,72... | collective-permute-start | bytes 1572872 | tf_op jit(solution)/shard_map/ppermute | solution.py:410
  78.7 1.4 %copy-start.2 = (bf16[16,272,256]{2,1,0:T(8,128)(2,1)}, bf16[16,272,256]{2,1,0:T(8,128)(2,1)S(1)}, u32[]{:S(2)}) copy-start(bf16[16,272,256]{2,1,0:T(8,128)(2,1)S(1)} %mixer.1) | copy-start | bytes 6684676
  80.1 10.7 %copy-start.3 = (bf16[128,2048]{1,0:T(8,128)(2,1)S(1)}, bf16[128,2048]{1,0:T(8,128)(2,1)}, u32[]{:S(2)}) copy-start(bf16[128,2048]{1,0:T(8,128)(2,1)} %q_ref.1) | copy-start | bytes 1572868
  83.5 0.8 copy-start.7
  84.3 37.8 %all-to-all-start.2 = ((bf16[16,272,256]{2,1,0:T(8,128)(2,1)}), bf16[16,272,256]{2,1,0:T(8,128)(2,1)S(1)}, u32[]{:S(2)}, u32[]{:S(2)}) async-start(bf16[16,272,256]{2,1,0:T(8,128)(2,1)} %copy-done.2), calls=%async_computation.2 | async-start | bytes 4456448 | tf_op jit(solution)/shard_map/all_to_all | solution.py:608
  90.8 1.0 copy-start.4
  91.9 1.0 copy-start.8
  109.0 12.2 %collective-permute-start.1 = (bf16[128,1024]{1,0:T(8,128)(2,1)S(1)}, bf16[128,1024]{1,0:T(8,128)(2,1)S(1)}, u32[]{:S(2)}, u32[]{:S(2)}) collective-permute-start(bf16[128,1024]{1,0:T(8,128)(2,1)S(1)} %get-tuple-element.33), channel_id=1, source_target_pairs={{0,8},{8,0},{16,24},{24,16},{32,40},{40,32},{48,56},{56,48},{64,72... | collective-permute-start | bytes 786440 | tf_op jit(solution)/shard_map/ppermute | solution.py:410
  110.9 14.1 %collective-permute-start.2 = (bf16[256,256]{1,0:T(8,128)(2,1)}, bf16[256,256]{1,0:T(8,128)(2,1)S(1)}, u32[]{:S(2)}, u32[]{:S(2)}) collective-permute-start(bf16[256,256]{1,0:T(8,128)(2,1)} %get-tuple-element.42), channel_id=1, source_target_pairs={{16,0},{24,8},{32,16},{40,24},{48,32},{56,40},{64,48},{72,56},{80,... | collective-permute-start | bytes 393224 | tf_op jit(solution)/shard_map/ppermute | solution.py:404
  112.2 12.8 %collective-permute-start.3 = (bf16[256,256]{1,0:T(8,128)(2,1)}, bf16[256,256]{1,0:T(8,128)(2,1)S(1)}, u32[]{:S(2)}, u32[]{:S(2)}) collective-permute-start(bf16[256,256]{1,0:T(8,128)(2,1)} %get-tuple-element.43), channel_id=1, source_target_pairs={{32,0},{40,8},{48,16},{56,24},{64,32},{72,40},{80,48},{88,56},{96,... | collective-permute-start | bytes 393224 | tf_op jit(solution)/shard_map/ppermute | solution.py:404
  113.5 14.9 %collective-permute-start.4 = (bf16[256,256]{1,0:T(8,128)(2,1)}, bf16[256,256]{1,0:T(8,128)(2,1)}, u32[]{:S(2)}, u32[]{:S(2)}) collective-permute-start(bf16[256,256]{1,0:T(8,128)(2,1)} %get-tuple-element.44), channel_id=1, source_target_pairs={{48,0},{56,8},{64,16},{72,24},{80,32},{88,40},{96,48},{104,56},{11... | collective-permute-start | bytes 393224 | tf_op jit(solution)/shard_map/ppermute | solution.py:404
  114.8 13.6 %collective-permute-start.5 = (bf16[256,256]{1,0:T(8,128)(2,1)}, bf16[256,256]{1,0:T(8,128)(2,1)}, u32[]{:S(2)}, u32[]{:S(2)}) collective-permute-start(bf16[256,256]{1,0:T(8,128)(2,1)} %get-tuple-element.45), channel_id=1, source_target_pairs={{64,0},{72,8},{80,16},{88,24},{96,32},{104,40},{112,48},{120,56},{... | collective-permute-start | bytes 393224 | tf_op jit(solution)/shard_map/ppermute | solution.py:404
  129.5 4.3 %collective-permute-start.6 = (bf16[128,256]{1,0:T(8,128)(2,1)S(1)}, bf16[128,256]{1,0:T(8,128)(2,1)S(1)}, u32[]{:S(2)}, u32[]{:S(2)}) collective-permute-start(bf16[128,256]{1,0:T(8,128)(2,1)S(1)} %get-tuple-element.47), channel_id=1, source_target_pairs={{0,8},{8,0},{16,24},{24,16},{32,40},{40,32},{48,56},{56,48},{64,72... | collective-permute-start | bytes 196616 | tf_op jit(solution)/shard_map/ppermute | solution.py:410

commit v4 on v3

--- a/solution.py
+++ b/solution.py
@@ -81,8 +81,8 @@
     wx = wx_ref[:, pl.ds(pl.multiple_of(place * 256, 256), 256)]
     wbc = jnp.concatenate(
         [
-            wbc_ref[:, pl.ds(pl.multiple_of(group * 128, 128), 128)],
-            wbc_ref[:, pl.ds(pl.multiple_of(256 + group * 128, 128), 128)],
+            wbc_ref[:, 0, pl.ds(pl.multiple_of(group * 128, 128), 128)],
+            wbc_ref[:, 1, pl.ds(pl.multiple_of(group * 128, 128), 128)],
         ],
         axis=1,
     )
@@ -410,7 +410,9 @@
     return lax.ppermute(a, "ctx", [(i, i ^ 1) for i in range(lax.axis_size("ctx"))])
 
 
-def pack_kernel(x_ref, g_ref, bc_ref, dt_ref, out_ref, buf, in_sems, out_sems):
+def pack_kernel(
+    x_ref, g_ref, bc_ref, dt_ref, k_ref, v_ref, out_ref, kv_ref, buf, kv_buf, in_sems, out_sems, kv_sem
+):
     blocks = out_ref.shape[0]
     loads = []
     for d in range(blocks):
@@ -422,39 +424,53 @@
         for one in pair:
             one.start()
         loads.append(pair)
+    b_all = bc_ref[:, 0, :]
+    c_all = bc_ref[:, 1, :]
+    bc = [
+        jnp.concatenate([b_all[:, at : at + HD], c_all[:, at : at + HD]], axis=1) for at in (0, HD)
+    ]
     for d in range(blocks):
-        buf[d, 2 * BLK : 3 * BLK] = bc_ref[d // (blocks // 2)]
+        buf[d, 2 * BLK : 3 * BLK] = bc[d // (blocks // 2)]
         raw = jnp.concatenate([dt_ref[2 * d : 2 * d + 1], dt_ref[2 * d + 1 : 2 * d + 2]], axis=1)
         hi = raw.astype(BF16).astype(F32)
         mid = (raw - hi).astype(BF16).astype(F32)
         parts = [hi, mid, raw - hi - mid, jnp.zeros((13, 2 * BLK), F32)]
         buf[d, 3 * BLK : 3 * BLK + 16] = jnp.concatenate(parts, axis=0).astype(BF16)
+        head = slice((d % 2) * HD, (d % 2 + 1) * HD)
+        kv_buf[d] = jnp.concatenate([k_ref[:, head], v_ref[:, head]], axis=1)
     stores = []
     for d in range(blocks):
         for one in loads[d]:
             one.wait()
         stores.append(pltpu.make_async_copy(buf.at[d], out_ref.at[d], out_sems.at[d]))
         stores[-1].start()
+    stores.append(pltpu.make_async_copy(kv_buf, kv_ref, kv_sem))
+    stores[-1].start()
     for one in stores:
         one.wait()
 
 
-def pack(x_in, grad, bc_sent, dt_raw, blocks):
+def pack(x_in, grad, bc_sent, dt_raw, key, value, blocks):
     hbm = pl.BlockSpec(memory_space=pltpu.HBM)
     vmem = pl.BlockSpec(memory_space=pltpu.VMEM)
     return pl.pallas_call(
         pack_kernel,
-        out_shape=jax.ShapeDtypeStruct((blocks, 3 * BLK + 16, 2 * HD), BF16),
-        in_specs=[hbm, hbm, vmem, vmem],
-        out_specs=hbm,
+        out_shape=[
+            jax.ShapeDtypeStruct((blocks, 3 * BLK + 16, 2 * HD), BF16),
+            jax.ShapeDtypeStruct((blocks, BLK, 2 * HD), BF16),
+        ],
+        in_specs=[hbm, hbm, vmem, vmem, vmem, vmem],
+        out_specs=[hbm, hbm],
         scratch_shapes=[
             pltpu.VMEM((blocks, 3 * BLK + 16, 2 * HD), BF16),
+            pltpu.VMEM((blocks, BLK, 2 * HD), BF16),
             pltpu.SemaphoreType.DMA((2 * blocks,)),
             pltpu.SemaphoreType.DMA((blocks,)),
+            pltpu.SemaphoreType.DMA(()),
         ],
         cost_estimate=pl.CostEstimate(flops=0, bytes_accessed=7 * 2**20, transcendentals=0),
         name="pack",
-    )(x_in, grad, bc_sent, dt_raw)
+    )(x_in, grad, bc_sent, dt_raw, key, value)
 
 
 def unpack_kernel(
@@ -623,13 +639,13 @@
     def pick(own, other):
         return jnp.where(odd == 0, own, other), jnp.where(odd == 0, other, own)
 
-    bc_sent = bc_in.reshape(rows, 2, 2, HD).transpose(2, 0, 1, 3).reshape(2, rows, 2 * HD)
-    packed = pack(x_in, grad_ssd, bc_sent, dt_raw, ctx)
+    packed, kv_sent = pack(x_in, grad_ssd, bc_in, dt_raw, key, value, ctx)
     qo = jnp.concatenate([half(query, 1 - odd), half(d_out, 1 - odd)], axis=1)
     got = swap(packed)
-    kv = swap(kv_pack(key, value, got))
+    got, kv_sent = lax.optimization_barrier((got, kv_sent))
+    kv = swap(kv_sent)
     got_qo = partner(qo)
-    mixed = ssm_core(doc_lengths, place, rate, got, conv_x, conv_bc.reshape(TAPS, 4 * HD))
+    mixed = ssm_core(doc_lengths, place, rate, got, conv_x, conv_bc)
     mixed, kv, got_qo = lax.optimization_barrier((mixed, kv, got_qo))
     back = swap(mixed)
     dq_own, dq_sent, *d_kv = attention_core(doc_lengths, place, query, d_out, got_qo, kv)

time: 137 us -> 134 us (0.978)
  local copies, waits for them, and re-layouts: 8.75 us -> 6.04 us
    unnamed x27 -> x18, local copies, waits for them, and re-layouts: 6.15 us -> 4.28 us
    pallas_call x2 -> x1, Pallas kernels: 3.95 us -> 4.31 us  [pack(): pl.pallas_call(pack_kernel, out_shape=[jax.ShapeDtypeStruct((blocks, 3 *...]
  transfers between devices with their start and end apart: 9 -> 9, of which waited for: 6 -> 6; matrix products, arithmetic and copies ran while one was open for 1% -> 1% of each run, Pallas kernels for 25% -> 26%
where the time goes in v4:
time: 134 us; the launch traced here: 132 us
  blocking collectives  48.2 us (36%)
  Pallas kernels  39.7 us (30%)
  starting transfers between devices  20.5 us (15%)
  waiting for transfers between devices  16.6 us (12%)
  local copies, waits for them, and re-layouts  6.04 us (5%)
    all_to_all x1, blocking collectives, swap(): return lax.all_to_all(a, 'ctx', 0, 0, tiled=True)  48.2 us
    pallas_call x1, Pallas kernels, attention_core(): pl.pallas_call(attention_kernel, out_shape=outs, in_specs=[smem, smem] +...  16.1 us
    pallas_call x1, Pallas kernels, ssm_core(): pl.pallas_call(ssm_kernel, out_shape=jax.ShapeDtypeStruct((blocks, 2 * BL...  15.8 us
    ppermute x3, waiting for transfers between devices, partner(): lax.ppermute(a, 'ctx', [(i, i ^ 1) for i in range(lax.axis_size('ctx'))])  11.4 us
    all_to_all x2, starting transfers between devices, swap(): return lax.all_to_all(a, 'ctx', 0, 0, tiled=True)  11 us
    ppermute x4, starting transfers between devices, shift(): lax.ppermute(a, 'ctx', [(i, i + by) for i in range(devices) if 0 <= i + b...  5.16 us
    ppermute x4, waiting for transfers between devices, shift(): lax.ppermute(a, 'ctx', [(i, i + by) for i in range(devices) if 0 <= i + b...  4.37 us
    ppermute x3, starting transfers between devices, partner(): lax.ppermute(a, 'ctx', [(i, i ^ 1) for i in range(lax.axis_size('ctx'))])  4.36 us
  transfers between devices with their start and end apart: 9, of which 6 were waited for; matrix products, arithmetic and copies ran while one was open for 1% of the time, Pallas kernels for 26%

profile of v4, /device:TPU:0, one launch (start us, length us, event | category | flops | bytes accessed | tf_op | source)
XLA Modules:
  0.0 131.9 jit_solution(30293948911465294)
XLA Ops:
  0.6 4.3 %pack.1 = (bf16[16,400,256]{2,1,0:T(8,128)(2,1)}, bf16[16,128,256]{2,1,0:T(8,128)(2,1)}) custom-call(bf16[128,4096]{1,0:T(8,128)(2,1)} %x_ref.1, bf16[128,4096]{1,0:T(8,128)(2,1)} %g_ref.1, bf16[128,2,256]{2,1,0:T(2,128)(2,1)} %bc_ref.1, f32[32,128]{1,0:T(8,128)} %dt_ref.1, bf16[128,256]{1,0:T(8,128)(2,1)} %k_ref.1, bf16[128,256]{1,0:T(8,128)(2,1)} %v_ref.1), custom_call_target="tpu_custom_call" | custom-call | bytes 7340032 | tf_op jit(solution)/shard_map/pack/pallas_call | solution.py:456
  5.0 48.2 %all_to_all.15.r_ref = bf16[16,400,256]{2,1,0:T(8,128)(2,1)S(1)} all-to-all(bf16[16,400,256]{2,1,0:T(8,128)(2,1)} %get-tuple-element.33), channel_id=1, replica_groups=mesh['ctx'=16,'head'=2,'dp'=4] {'ctx'}, dimensions={0} | all-to-all | bytes 6553600 | tf_op jit(solution)/shard_map/all_to_all | solution.py:624
  53.1 0.0 copy-start.5
  53.1 0.0 copy-start.6
  53.1 0.0 copy-start.7
  53.1 0.0 copy-start.8
  53.1 4.5 %all-to-all-start.1 = ((bf16[16,128,256]{2,1,0:T(8,128)(2,1)}), bf16[16,128,256]{2,1,0:T(8,128)(2,1)}, u32[]{:S(2)}, u32[]{:S(2)}) async-start(bf16[16,128,256]{2,1,0:T(8,128)(2,1)} %get-tuple-element.36), calls=%async_computation.1 | async-start | bytes 2097152 | tf_op jit(solution)/shard_map/all_to_all | solution.py:624
  57.6 1.1 constant_dynamic-slice_fusion
  58.7 1.8 %collective-permute-start = (bf16[128,2048]{1,0:T(8,128)(2,1)S(1)}, bf16[128,2048]{1,0:T(8,128)(2,1)S(1)}, u32[]{:S(2)}, u32[]{:S(2)}) collective-permute-start(bf16[128,2048]{1,0:T(8,128)(2,1)S(1)} %pad_maximum_fusion), channel_id=1, source_target_pairs={{0,8},{8,0},{16,24},{24,16},{32,40},{40,32},{48,56},{56,48},{64,72... | collective-permute-start | bytes 1572872 | tf_op jit(solution)/shard_map/ppermute | solution.py:410
  60.5 0.0 copy-done.5
  60.5 0.0 copy-done.6
  60.5 0.0 copy-done.7
  60.5 0.0 copy-done.8
  60.5 15.8 %mixer.1 = bf16[16,272,256]{2,1,0:T(8,128)(2,1)S(1)} custom-call(s32[4]{0:T(128)S(1)} %copy-done.8, s32[1]{0:T(128)} %bitcast.idx_ref, f32[32]{0:T(128)S(1)} %copy-done.7, bf16[16,400,256]{2,1,0:T(8,128)(2,1)S(1)} %all_to_all.15.r_ref, f32[4,4096]{1,0:T(4,128)S(1)} %copy-done.5, f32[4,2,256]{2,1,0:T(2,128)S(1)} %copy-done.6), custom_call_target="tpu_custom_call" | custom-call | flops 3000000000 | bytes 6291456 | tf_op jit(solution)/shard_map/mixer/pallas_call | solution.py:258
  76.3 0.0 copy-start
  76.3 1.4 %copy-done = bf16[16,272,256]{2,1,0:T(8,128)(2,1)} copy-done((bf16[16,272,256]{2,1,0:T(8,128)(2,1)}, bf16[16,272,256]{2,1,0:T(8,128)(2,1)S(1)}, u32[]{:S(2)}) %copy-start) | copy-done | bytes 2228248
  77.7 0.0 copy-start.1
  77.7 3.3 %collective-permute-done.got_ref = bf16[128,2048]{1,0:T(8,128)(2,1)S(1)} collective-permute-done((bf16[128,2048]{1,0:T(8,128)(2,1)S(1)}, bf16[128,2048]{1,0:T(8,128)(2,1)S(1)}, u32[]{:S(2)}, u32[]{:S(2)}) %collective-permute-start) | collective-permute-done | bytes 524320 | tf_op jit(solution)/shard_map/ppermute | solution.py:410
  81.0 0.0 copy-start.3
  81.0 0.8 copy-done.3
  81.8 0.0 all-to-all-done.1.kv_ref
  81.8 6.5 %all-to-all-start.2 = ((bf16[16,272,256]{2,1,0:T(8,128)(2,1)}), bf16[16,272,256]{2,1,0:T(8,128)(2,1)S(1)}, u32[]{:S(2)}, u32[]{:S(2)}) async-start(bf16[16,272,256]{2,1,0:T(8,128)(2,1)} %copy-done), calls=%async_computation.2 | async-start | bytes 4456448 | tf_op jit(solution)/shard_map/all_to_all | solution.py:624
  88.4 0.0 copy-done.1
  88.4 0.0 copy-start.2
  88.4 1.0 copy-done.2
  89.4 0.0 copy-start.4
  89.4 1.0 copy-done.4
  90.5 16.1 %attention.1 = (bf16[128,1024]{1,0:T(8,128)(2,1)S(1)}, bf16[128,1024]{1,0:T(8,128)(2,1)S(1)}, f32[256,256]{1,0:T(8,128)S(1)}, bf16[256,256]{1,0:T(8,128)(2,1)}, ...) custom-call(s32[4]{0:T(128)S(1)} %copy-done.8, s32[1]{0:T(128)} %bitcast.idx_ref, ...), custom_call_target="tpu_custom_call" | custom-call | flops 4000000000 | bytes 4194304 | tf_op jit(solution)/shard_map/attention/pallas_call | solution.py:384
  106.6 1.9 %collective-permute-start.1 = (bf16[128,1024]{1,0:T(8,128)(2,1)S(1)}, bf16[128,1024]{1,0:T(8,128)(2,1)S(1)}, u32[]{:S(2)}, u32[]{:S(2)}) collective-permute-start(bf16[128,1024]{1,0:T(8,128)(2,1)S(1)} %get-tuple-element.41), channel_id=1, source_target_pairs={{0,8},{8,0},{16,24},{24,16},{32,40},{40,32},{48,56},{56,48},{64,72... | collective-permute-start | bytes 786440 | tf_op jit(solution)/shard_map/ppermute | solution.py:410
  108.5 1.3 collective-permute-start.2
  109.8 1.3 collective-permute-start.3
  111.1 1.3 collective-permute-start.4
  112.4 1.3 collective-permute-start.5
  113.7 5.1 %collective-permute-done.1.dq_got = bf16[128,1024]{1,0:T(8,128)(2,1)S(1)} collective-permute-done((bf16[128,1024]{1,0:T(8,128)(2,1)S(1)}, bf16[128,1024]{1,0:T(8,128)(2,1)S(1)}, u32[]{:S(2)}, u32[]{:S(2)}) %collective-permute-start.1) | collective-permute-done | bytes 262176 | tf_op jit(solution)/shard_map/ppermute | solution.py:410
  118.8 0.8 all-to-all-done.2.part
  119.6 1.9 %unpack.1 = (bf16[128,4096]{1,0:T(8,128)(2,1)}, bf16[128,512]{1,0:T(8,128)(2,1)S(1)}, f32[32,128]{1,0:T(8,128)}, f32[4,4096]{1,0:T(4,128)}, f32[4,2,256]{2,1,0:T...) custom-call(s32[1]{0:T(128)} %bitcast.idx_ref, ...), custom_call_target="tpu_custom_call", output_to_operand_aliasing={{6}: (4, {})} | custom-call | flops 1000000 | bytes 4194304 | tf_op jit(solution)/shard_map/unpack/pallas_call | solution.py:517
  121.5 1.0 collective-permute-done.2.r1
  122.5 0.0 collective-permute-done.3.r2
  122.6 3.3 %collective-permute-done.4.r3 = bf16[256,256]{1,0:T(8,128)(2,1)S(1)} collective-permute-done((bf16[256,256]{1,0:T(8,128)(2,1)}, bf16[256,256]{1,0:T(8,128)(2,1)S(1)}, u32[]{:S(2)}, u32[]{:S(2)}) %collective-permute-start.4) | collective-permute-done | bytes 131104 | tf_op jit(solution)/shard_map/ppermute | solution.py:404
  125.9 0.0 collective-permute-done.5.r4
  125.9 1.0 kv_total.1
  126.9 0.6 collective-permute-start.6
  127.5 0.7 reshape.23
  128.2 3.0 %collective-permute-done.6.other = bf16[128,256]{1,0:T(8,128)(2,1)S(1)} collective-permute-done((bf16[128,256]{1,0:T(8,128)(2,1)S(1)}, bf16[128,256]{1,0:T(8,128)(2,1)S(1)}, u32[]{:S(2)}, u32[]{:S(2)}) %collective-permute-start.6) | collective-permute-done | bytes 65568 | tf_op jit(solution)/shard_map/ppermute | solution.py:410
  131.2 0.7 kv_place.1
  (1 shorter events, 0.0 us)
Async XLA Ops:
  53.1 7.4 %copy-start.5 = (f32[4,4096]{1,0:T(4,128)S(1)}, f32[4,4096]{1,0:T(4,128)}, u32[]{:S(2)}) copy-start(f32[4,4096]{1,0:T(4,128)} %wx_ref.1) | copy-start | bytes 196612
  53.1 7.4 %copy-start.6 = (f32[4,2,256]{2,1,0:T(2,128)S(1)}, f32[4,2,256]{2,1,0:T(2,128)}, u32[]{:S(2)}) copy-start(f32[4,2,256]{2,1,0:T(2,128)} %wbc_ref.1) | copy-start | bytes 24580
  53.1 7.4 %copy-start.7 = (f32[32]{0:T(128)S(1)}, f32[32]{0:T(128)}, u32[]{:S(2)}) copy-start(f32[32]{0:T(128)} %rate_ref.1) | copy-start | bytes 388
  53.1 7.4 %copy-start.8 = (s32[4]{0:T(128)S(1)}, s32[4]{0:T(128)}, u32[]{:S(2)}) copy-start(s32[4]{0:T(128)} %doc_ref.3) | copy-start | bytes 52
  53.1 28.7 %all-to-all-start.1 = ((bf16[16,128,256]{2,1,0:T(8,128)(2,1)}), bf16[16,128,256]{2,1,0:T(8,128)(2,1)}, u32[]{:S(2)}, u32[]{:S(2)}) async-start(bf16[16,128,256]{2,1,0:T(8,128)(2,1)} %get-tuple-element.36), calls=%async_computation.1 | async-start | bytes 2097152 | tf_op jit(solution)/shard_map/all_to_all | solution.py:624
  58.7 22.3 %collective-permute-start = (bf16[128,2048]{1,0:T(8,128)(2,1)S(1)}, bf16[128,2048]{1,0:T(8,128)(2,1)S(1)}, u32[]{:S(2)}, u32[]{:S(2)}) collective-permute-start(bf16[128,2048]{1,0:T(8,128)(2,1)S(1)} %pad_maximum_fusion), channel_id=1, source_target_pairs={{0,8},{8,0},{16,24},{24,16},{32,40},{40,32},{48,56},{56,48},{64,72... | collective-permute-start | bytes 1572872 | tf_op jit(solution)/shard_map/ppermute | solution.py:410
  76.3 1.4 %copy-start = (bf16[16,272,256]{2,1,0:T(8,128)(2,1)}, bf16[16,272,256]{2,1,0:T(8,128)(2,1)S(1)}, u32[]{:S(2)}) copy-start(bf16[16,272,256]{2,1,0:T(8,128)(2,1)S(1)} %mixer.1) | copy-start | bytes 6684676
  77.7 10.7 %copy-start.1 = (bf16[128,2048]{1,0:T(8,128)(2,1)S(1)}, bf16[128,2048]{1,0:T(8,128)(2,1)}, u32[]{:S(2)}) copy-start(bf16[128,2048]{1,0:T(8,128)(2,1)} %q_ref.1) | copy-start | bytes 1572868
  81.0 0.8 copy-start.3
  81.8 37.8 %all-to-all-start.2 = ((bf16[16,272,256]{2,1,0:T(8,128)(2,1)}), bf16[16,272,256]{2,1,0:T(8,128)(2,1)S(1)}, u32[]{:S(2)}, u32[]{:S(2)}) async-start(bf16[16,272,256]{2,1,0:T(8,128)(2,1)} %copy-done), calls=%async_computation.2 | async-start | bytes 4456448 | tf_op jit(solution)/shard_map/all_to_all | solution.py:624
  88.4 1.0 copy-start.2
  89.4 1.0 copy-start.4
  106.6 12.2 %collective-permute-start.1 = (bf16[128,1024]{1,0:T(8,128)(2,1)S(1)}, bf16[128,1024]{1,0:T(8,128)(2,1)S(1)}, u32[]{:S(2)}, u32[]{:S(2)}) collective-permute-start(bf16[128,1024]{1,0:T(8,128)(2,1)S(1)} %get-tuple-element.41), channel_id=1, source_target_pairs={{0,8},{8,0},{16,24},{24,16},{32,40},{40,32},{48,56},{56,48},{64,72... | collective-permute-start | bytes 786440 | tf_op jit(solution)/shard_map/ppermute | solution.py:410
  108.5 14.1 %collective-permute-start.2 = (bf16[256,256]{1,0:T(8,128)(2,1)}, bf16[256,256]{1,0:T(8,128)(2,1)S(1)}, u32[]{:S(2)}, u32[]{:S(2)}) collective-permute-start(bf16[256,256]{1,0:T(8,128)(2,1)} %get-tuple-element.50), channel_id=1, source_target_pairs={{16,0},{24,8},{32,16},{40,24},{48,32},{56,40},{64,48},{72,56},{80,... | collective-permute-start | bytes 393224 | tf_op jit(solution)/shard_map/ppermute | solution.py:404
  109.8 12.8 %collective-permute-start.3 = (bf16[256,256]{1,0:T(8,128)(2,1)}, bf16[256,256]{1,0:T(8,128)(2,1)S(1)}, u32[]{:S(2)}, u32[]{:S(2)}) collective-permute-start(bf16[256,256]{1,0:T(8,128)(2,1)} %get-tuple-element.51), channel_id=1, source_target_pairs={{32,0},{40,8},{48,16},{56,24},{64,32},{72,40},{80,48},{88,56},{96,... | collective-permute-start | bytes 393224 | tf_op jit(solution)/shard_map/ppermute | solution.py:404
  111.1 14.8 %collective-permute-start.4 = (bf16[256,256]{1,0:T(8,128)(2,1)}, bf16[256,256]{1,0:T(8,128)(2,1)S(1)}, u32[]{:S(2)}, u32[]{:S(2)}) collective-permute-start(bf16[256,256]{1,0:T(8,128)(2,1)} %get-tuple-element.52), channel_id=1, source_target_pairs={{48,0},{56,8},{64,16},{72,24},{80,32},{88,40},{96,48},{104,56},{11... | collective-permute-start | bytes 393224 | tf_op jit(solution)/shard_map/ppermute | solution.py:404
  112.4 13.5 %collective-permute-start.5 = (bf16[256,256]{1,0:T(8,128)(2,1)}, bf16[256,256]{1,0:T(8,128)(2,1)}, u32[]{:S(2)}, u32[]{:S(2)}) collective-permute-start(bf16[256,256]{1,0:T(8,128)(2,1)} %get-tuple-element.53), channel_id=1, source_target_pairs={{64,0},{72,8},{80,16},{88,24},{96,32},{104,40},{112,48},{120,56},{... | collective-permute-start | bytes 393224 | tf_op jit(solution)/shard_map/ppermute | solution.py:404
  126.9 4.3 %collective-permute-start.6 = (bf16[128,256]{1,0:T(8,128)(2,1)S(1)}, bf16[128,256]{1,0:T(8,128)(2,1)S(1)}, u32[]{:S(2)}, u32[]{:S(2)}) collective-permute-start(bf16[128,256]{1,0:T(8,128)(2,1)S(1)} %get-tuple-element.55), channel_id=1, source_target_pairs={{0,8},{8,0},{16,24},{24,16},{32,40},{40,32},{48,56},{56,48},{64,72... | collective-permute-start | bytes 196616 | tf_op jit(solution)/shard_map/ppermute | solution.py:410

commit v5 on v4

--- a/solution.py
+++ b/solution.py
@@ -13,7 +13,7 @@
 BACK = 8
 LOG2E = 1.4426950408889634
 NEG_BIG = -1e30
-UNROLL = 4
+UNROLL = 8
 
 
 def dot_nn(a, b):
@@ -287,7 +287,7 @@
 
 
 def attention_kernel(
-    doc_ref, idx_ref, q_ref, do_ref, got_ref, kv_ref,
+    doc_ref, idx_ref, q_ref, do_ref, got_q_ref, got_do_ref, kv_ref,
     dq_own, dq_sent, d0, d1, d2, d3, d4, kt_s, dk_s, dv_s, s_s, p_s,
 ):
     d_refs = (d4, d3, d2, d1, d0)
@@ -300,7 +300,7 @@
     jrow = lax.broadcasted_iota(jnp.int32, (BLK, 2 * BLK), 0)
     icol = lax.broadcasted_iota(jnp.int32, (BLK, 2 * BLK), 1)
     start = start_at(base + icol[0:1], bounds) - base
-    heads = got_ref.shape[1] // (2 * HD)
+    heads = got_q_ref.shape[1] // HD
 
     def rows8(a):
         return a.reshape(BLK // 8, 8, 2 * BLK)
@@ -327,9 +327,9 @@
     def turn(head, carry):
         at = pl.multiple_of(head * HD, HD)
         own_at = pl.multiple_of((odd * heads + head) * HD, HD)
-        q = in_order(q_ref[:, pl.ds(own_at, HD)], got_ref[:, pl.ds(at, HD)])
+        q = in_order(q_ref[:, pl.ds(own_at, HD)], got_q_ref[:, pl.ds(at, HD)])
         do = in_order(
-            do_ref[:, pl.ds(own_at, HD)], got_ref[:, pl.ds(pl.multiple_of(heads * HD + at, HD), HD)]
+            do_ref[:, pl.ds(own_at, HD)], got_do_ref[:, pl.ds(at, HD)]
         )
         top = jnp.full((8, 2 * BLK), NEG_BIG, F32)
         for b in range(count):
@@ -371,7 +371,7 @@
         out[half(b), HD : 2 * HD] = dv_s[b].astype(out.dtype)
 
 
-def attention_core(doc_lengths, place, query, d_out, got, kv):
+def attention_core(doc_lengths, place, query, d_out, got_q, got_do, kv):
     smem = pl.BlockSpec(memory_space=pltpu.SMEM)
     vmem = pl.BlockSpec(memory_space=pltpu.VMEM)
     pairs = BACK // 2 + 1
@@ -384,7 +384,7 @@
     return pl.pallas_call(
         attention_kernel,
         out_shape=outs,
-        in_specs=[smem, smem] + [vmem] * 4,
+        in_specs=[smem, smem] + [vmem] * 5,
         out_specs=[vmem] * (2 + pairs),
         scratch_shapes=[
             pltpu.VMEM((count, HD, BLK), BF16),
@@ -396,7 +396,7 @@
         compiler_params=pltpu.CompilerParams(vmem_limit_bytes=16 * 2**20),
         cost_estimate=pl.CostEstimate(flops=4 * 10**9, bytes_accessed=4 * 2**20, transcendentals=3 * 10**6),
         name="attention",
-    )(doc_lengths, place, query, d_out, got, kv)
+    )(doc_lengths, place, query, d_out, got_q, got_do, kv)
 
 
 def shift(a, by):
@@ -535,43 +535,6 @@
     )(place, received, dq_own, dq_got, own)
 
 
-def gate_kernel(*refs):
-    pass
-
-
-def gate(value, *others):
-    hbm = pl.BlockSpec(memory_space=pltpu.HBM)
-    anywhere = pl.BlockSpec(memory_space=pl.ANY)
-    return pl.pallas_call(
-        gate_kernel,
-        out_shape=jax.ShapeDtypeStruct(value.shape, value.dtype),
-        in_specs=[hbm] + [anywhere] * len(others),
-        out_specs=hbm,
-        input_output_aliases={0: 0},
-        compiler_params=pltpu.CompilerParams(vmem_limit_bytes=2**20),
-        name="gate",
-    )(value, *others)
-
-
-def kv_pack_kernel(k_ref, v_ref, got, kv_ref):
-    for d in range(kv_ref.shape[0]):
-        head = slice((d % 2) * HD, (d % 2 + 1) * HD)
-        kv_ref[d] = jnp.concatenate([k_ref[:, head], v_ref[:, head]], axis=1)
-
-
-def kv_pack(key, value, got):
-    vmem = pl.BlockSpec(memory_space=pltpu.VMEM)
-    shape = (got.shape[0],) + key.shape
-    return pl.pallas_call(
-        kv_pack_kernel,
-        out_shape=jax.ShapeDtypeStruct(shape, BF16),
-        in_specs=[vmem, vmem, pl.BlockSpec(memory_space=pl.ANY)],
-        out_specs=vmem,
-        compiler_params=pltpu.CompilerParams(vmem_limit_bytes=4 * 2**20),
-        name="kv_pack",
-    )(key, value, got)
-
-
 def kv_sum_kernel(idx_ref, own, r1, r2, r3, r4, mine, sent):
     total = own[...]
     for got in (r1, r2, r3, r4):
@@ -640,15 +603,15 @@
         return jnp.where(odd == 0, own, other), jnp.where(odd == 0, other, own)
 
     packed, kv_sent = pack(x_in, grad_ssd, bc_in, dt_raw, key, value, ctx)
-    qo = jnp.concatenate([half(query, 1 - odd), half(d_out, 1 - odd)], axis=1)
     got = swap(packed)
     got, kv_sent = lax.optimization_barrier((got, kv_sent))
     kv = swap(kv_sent)
-    got_qo = partner(qo)
+    got_q = partner(half(query, 1 - odd))
+    got_do = partner(half(d_out, 1 - odd))
     mixed = ssm_core(doc_lengths, place, rate, got, conv_x, conv_bc)
-    mixed, kv, got_qo = lax.optimization_barrier((mixed, kv, got_qo))
+    mixed, kv, got_q, got_do = lax.optimization_barrier((mixed, kv, got_q, got_do))
     back = swap(mixed)
-    dq_own, dq_sent, *d_kv = attention_core(doc_lengths, place, query, d_out, got_qo, kv)
+    dq_own, dq_sent, *d_kv = attention_core(doc_lengths, place, query, d_out, got_q, got_do, kv)
     received = [shift(d_kv[by], -2 * by) for by in range(1, BACK // 2 + 1)]
     d_x, d_bc, d_dt, d_wx, d_wbc, d_query, own = unpack(
         place, back, dq_own, partner(dq_sent), d_kv[0]

time: 134 us -> 134 us (level)
  local copies, waits for them, and re-layouts: 6.04 us -> 7.56 us
    ppermute x3 -> x4, waiting for transfers between devices: 11.4 us -> 10.1 us  [partner(): lax.ppermute(a, 'ctx', [(i, i ^ 1) for i in range(lax.axis_size('ctx'))])]
    ppermute x3 -> x4, starting transfers between devices: 4.36 us -> 4.75 us  [partner(): lax.ppermute(a, 'ctx', [(i, i ^ 1) for i in range(lax.axis_size('ctx'))])]
  transfers between devices with their start and end apart: 9 -> 10, of which waited for: 6 -> 6; matrix products, arithmetic and copies ran while one was open for 1% -> 2% of each run, Pallas kernels for 26% -> 25%
where the time goes in v5:
time: 134 us; the launch traced here: 132 us
  blocking collectives  48.3 us (36%)
  Pallas kernels  39.1 us (29%)
  starting transfers between devices  20.8 us (16%)
  waiting for transfers between devices  15.3 us (11%)
  local copies, waits for them, and re-layouts  7.56 us (6%)
    all_to_all x1, blocking collectives, swap(): return lax.all_to_all(a, 'ctx', 0, 0, tiled=True)  48.3 us
    pallas_call x1, Pallas kernels, attention_core(): pl.pallas_call(attention_kernel, out_shape=outs, in_specs=[smem, smem] +...  16.1 us
    pallas_call x1, Pallas kernels, ssm_core(): pl.pallas_call(ssm_kernel, out_shape=jax.ShapeDtypeStruct((blocks, 2 * BL...  15.1 us
    all_to_all x2, starting transfers between devices, swap(): return lax.all_to_all(a, 'ctx', 0, 0, tiled=True)  10.9 us
    ppermute x4, waiting for transfers between devices, partner(): lax.ppermute(a, 'ctx', [(i, i ^ 1) for i in range(lax.axis_size('ctx'))])  10.1 us
    ppermute x4, starting transfers between devices, shift(): lax.ppermute(a, 'ctx', [(i, i + by) for i in range(devices) if 0 <= i + b...  5.16 us
    unnamed x18, local copies, waits for them, and re-layouts  4.93 us
    ppermute x4, starting transfers between devices, partner(): lax.ppermute(a, 'ctx', [(i, i ^ 1) for i in range(lax.axis_size('ctx'))])  4.75 us
  transfers between devices with their start and end apart: 10, of which 6 were waited for; matrix products, arithmetic and copies ran while one was open for 2% of the time, Pallas kernels for 25%

profile of v5, /device:TPU:0, one launch (start us, length us, event | category | flops | bytes accessed | tf_op | source)
XLA Modules:
  0.0 131.8 jit_solution(2754810842664731141)
XLA Ops:
  0.6 4.3 %pack.1 = (bf16[16,400,256]{2,1,0:T(8,128)(2,1)}, bf16[16,128,256]{2,1,0:T(8,128)(2,1)}) custom-call(bf16[128,4096]{1,0:T(8,128)(2,1)} %x_ref.1, bf16[128,4096]{1,0:T(8,128)(2,1)} %g_ref.1, bf16[128,2,256]{2,1,0:T(2,128)(2,1)} %bc_ref.1, f32[32,128]{1,0:T(8,128)} %dt_ref.1, bf16[128,256]{1,0:T(8,128)(2,1)} %k_ref.1, bf16[128,256]{1,0:T(8,128)(2,1)} %v_ref.1), custom_call_target="tpu_custom_call" | custom-call | bytes 7340032 | tf_op jit(solution)/shard_map/pack/pallas_call | solution.py:456
  5.0 0.0 copy-start.6
  5.0 0.0 copy-start.7
  5.0 0.0 copy-start.8
  5.0 48.3 %all_to_all.15.r_ref = bf16[16,400,256]{2,1,0:T(8,128)(2,1)S(1)} all-to-all(bf16[16,400,256]{2,1,0:T(8,128)(2,1)} %get-tuple-element.34), channel_id=1, replica_groups=mesh['ctx'=16,'head'=2,'dp'=4] {'ctx'}, dimensions={0} | all-to-all | bytes 6553600 | tf_op jit(solution)/shard_map/all_to_all | solution.py:587
  53.3 4.3 %all-to-all-start.1 = ((bf16[16,128,256]{2,1,0:T(8,128)(2,1)}), bf16[16,128,256]{2,1,0:T(8,128)(2,1)}, u32[]{:S(2)}, u32[]{:S(2)}) async-start(bf16[16,128,256]{2,1,0:T(8,128)(2,1)} %get-tuple-element.37), calls=%async_computation.1 | async-start | bytes 2097152 | tf_op jit(solution)/shard_map/all_to_all | solution.py:587
  57.6 1.0 constant_dynamic-slice_fusion.1
  58.6 1.8 %collective-permute-start = (bf16[128,1024]{1,0:T(8,128)(2,1)S(1)}, bf16[128,1024]{1,0:T(8,128)(2,1)S(1)}, u32[]{:S(2)}, u32[]{:S(2)}) collective-permute-start(bf16[128,1024]{1,0:T(8,128)(2,1)S(1)} %constant_dynamic-slice_fusion.1), channel_id=1, source_target_pairs={{0,8},{8,0},{16,24},{24,16},{32,40},{40,32},{48,56},{56,48},{64,72... | collective-permute-start | bytes 786440 | tf_op jit(solution)/shard_map/ppermute | solution.py:410
  60.4 1.0 constant_dynamic-slice_fusion
  61.4 0.4 collective-permute-start.1
  61.8 0.0 copy-done.6
  61.8 0.0 copy-done.7
  61.8 0.0 copy-done.8
  61.8 0.0 copy-start.5
  61.8 0.8 copy-done.5
  62.6 15.1 %mixer.1 = bf16[16,272,256]{2,1,0:T(8,128)(2,1)S(1)} custom-call(s32[4]{0:T(128)S(1)} %copy-done.8, s32[1]{0:T(128)} %bitcast.idx_ref, f32[32]{0:T(128)S(1)} %copy-done.7, bf16[16,400,256]{2,1,0:T(8,128)(2,1)S(1)} %all_to_all.15.r_ref, f32[4,4096]{1,0:T(4,128)S(1)} %copy-done.5, f32[4,2,256]{2,1,0:T(2,128)S(1)} %copy-done.6), custom_call_target="tpu_custom_call" | custom-call | flops 3000000000 | bytes 6291456 | tf_op jit(solution)/shard_map/mixer/pallas_call | solution.py:258
  77.7 0.0 copy-start
  77.7 1.4 %copy-done = bf16[16,272,256]{2,1,0:T(8,128)(2,1)} copy-done((bf16[16,272,256]{2,1,0:T(8,128)(2,1)}, bf16[16,272,256]{2,1,0:T(8,128)(2,1)S(1)}, u32[]{:S(2)}) %copy-start) | copy-done | bytes 2228248
  79.1 0.0 copy-start.1
  79.1 0.0 collective-permute-done.got_q_ref
  79.1 1.9 %collective-permute-done.1.got_do_ref = bf16[128,1024]{1,0:T(8,128)(2,1)S(1)} collective-permute-done((bf16[128,1024]{1,0:T(8,128)(2,1)S(1)}, bf16[128,1024]{1,0:T(8,128)(2,1)S(1)}, u32[]{:S(2)}, u32[]{:S(2)}) %collective-permute-start.1) | collective-permute-done | bytes 262176 | tf_op jit(solution)/shard_map/ppermute | solution.py:410
  81.1 0.0 copy-start.3
  81.1 0.7 copy-done.3
  81.8 0.0 all-to-all-done.1.kv_ref
  81.8 6.5 %all-to-all-start.2 = ((bf16[16,272,256]{2,1,0:T(8,128)(2,1)}), bf16[16,272,256]{2,1,0:T(8,128)(2,1)S(1)}, u32[]{:S(2)}, u32[]{:S(2)}) async-start(bf16[16,272,256]{2,1,0:T(8,128)(2,1)} %copy-done), calls=%async_computation.2 | async-start | bytes 4456448 | tf_op jit(solution)/shard_map/all_to_all | solution.py:587
  88.3 0.0 copy-done.1
  88.3 0.0 copy-start.2
  88.3 1.0 copy-done.2
  89.4 0.0 copy-start.4
  89.4 0.9 copy-done.4
  90.3 16.1 %attention.1 = (bf16[128,1024]{1,0:T(8,128)(2,1)S(1)}, bf16[128,1024]{1,0:T(8,128)(2,1)S(1)}, f32[256,256]{1,0:T(8,128)S(1)}, bf16[256,256]{1,0:T(8,128)(2,1)}, ...) custom-call(s32[4]{0:T(128)S(1)} %copy-done.8, s32[1]{0:T(128)} %bitcast.idx_ref, ...), custom_call_target="tpu_custom_call" | custom-call | flops 4000000000 | bytes 4194304 | tf_op jit(solution)/shard_map/attention/pallas_call | solution.py:384
  106.4 1.9 %collective-permute-start.2 = (bf16[128,1024]{1,0:T(8,128)(2,1)S(1)}, bf16[128,1024]{1,0:T(8,128)(2,1)S(1)}, u32[]{:S(2)}, u32[]{:S(2)}) collective-permute-start(bf16[128,1024]{1,0:T(8,128)(2,1)S(1)} %get-tuple-element.43), channel_id=1, source_target_pairs={{0,8},{8,0},{16,24},{24,16},{32,40},{40,32},{48,56},{56,48},{64,72... | collective-permute-start | bytes 786440 | tf_op jit(solution)/shard_map/ppermute | solution.py:410
  108.3 1.3 collective-permute-start.3
  109.6 1.3 collective-permute-start.4
  110.9 1.3 collective-permute-start.5
  112.2 1.3 collective-permute-start.6
  113.5 5.2 %collective-permute-done.2.dq_got = bf16[128,1024]{1,0:T(8,128)(2,1)S(1)} collective-permute-done((bf16[128,1024]{1,0:T(8,128)(2,1)S(1)}, bf16[128,1024]{1,0:T(8,128)(2,1)S(1)}, u32[]{:S(2)}, u32[]{:S(2)}) %collective-permute-start.2) | collective-permute-done | bytes 262176 | tf_op jit(solution)/shard_map/ppermute | solution.py:410
  118.7 0.8 all-to-all-done.2.part
  119.5 1.9 %unpack.1 = (bf16[128,4096]{1,0:T(8,128)(2,1)}, bf16[128,512]{1,0:T(8,128)(2,1)S(1)}, f32[32,128]{1,0:T(8,128)}, f32[4,4096]{1,0:T(4,128)}, f32[4,2,256]{2,1,0:T...) custom-call(s32[1]{0:T(128)} %bitcast.idx_ref, ...), custom_call_target="tpu_custom_call", output_to_operand_aliasing={{6}: (4, {})} | custom-call | flops 1000000 | bytes 4194304 | tf_op jit(solution)/shard_map/unpack/pallas_call | solution.py:517
  121.4 1.0 collective-permute-done.3.r1
  122.5 0.0 collective-permute-done.4.r2
  122.5 3.3 %collective-permute-done.5.r3 = bf16[256,256]{1,0:T(8,128)(2,1)S(1)} collective-permute-done((bf16[256,256]{1,0:T(8,128)(2,1)}, bf16[256,256]{1,0:T(8,128)(2,1)S(1)}, u32[]{:S(2)}, u32[]{:S(2)}) %collective-permute-start.5) | collective-permute-done | bytes 131104 | tf_op jit(solution)/shard_map/ppermute | solution.py:404
  125.8 0.0 collective-permute-done.6.r4
  125.8 1.0 kv_total.1
  126.8 0.6 collective-permute-start.7
  127.5 0.7 reshape.23
  128.1 3.0 %collective-permute-done.7.other = bf16[128,256]{1,0:T(8,128)(2,1)S(1)} collective-permute-done((bf16[128,256]{1,0:T(8,128)(2,1)S(1)}, bf16[128,256]{1,0:T(8,128)(2,1)S(1)}, u32[]{:S(2)}, u32[]{:S(2)}) %collective-permute-start.7) | collective-permute-done | bytes 65568 | tf_op jit(solution)/shard_map/ppermute | solution.py:410
  131.2 0.7 kv_place.1
Async XLA Ops:
  5.0 56.8 %copy-start.6 = (f32[4,2,256]{2,1,0:T(2,128)S(1)}, f32[4,2,256]{2,1,0:T(2,128)}, u32[]{:S(2)}) copy-start(f32[4,2,256]{2,1,0:T(2,128)} %wbc_ref.1) | copy-start | bytes 24580
  5.0 56.8 %copy-start.7 = (f32[32]{0:T(128)S(1)}, f32[32]{0:T(128)}, u32[]{:S(2)}) copy-start(f32[32]{0:T(128)} %rate_ref.1) | copy-start | bytes 388
  5.0 56.8 %copy-start.8 = (s32[4]{0:T(128)S(1)}, s32[4]{0:T(128)}, u32[]{:S(2)}) copy-start(s32[4]{0:T(128)} %doc_ref.3) | copy-start | bytes 52
  53.3 28.5 %all-to-all-start.1 = ((bf16[16,128,256]{2,1,0:T(8,128)(2,1)}), bf16[16,128,256]{2,1,0:T(8,128)(2,1)}, u32[]{:S(2)}, u32[]{:S(2)}) async-start(bf16[16,128,256]{2,1,0:T(8,128)(2,1)} %get-tuple-element.37), calls=%async_computation.1 | async-start | bytes 2097152 | tf_op jit(solution)/shard_map/all_to_all | solution.py:587
  58.6 20.5 %collective-permute-start = (bf16[128,1024]{1,0:T(8,128)(2,1)S(1)}, bf16[128,1024]{1,0:T(8,128)(2,1)S(1)}, u32[]{:S(2)}, u32[]{:S(2)}) collective-permute-start(bf16[128,1024]{1,0:T(8,128)(2,1)S(1)} %constant_dynamic-slice_fusion.1), channel_id=1, source_target_pairs={{0,8},{8,0},{16,24},{24,16},{32,40},{40,32},{48,56},{56,48},{64,72... | collective-permute-start | bytes 786440 | tf_op jit(solution)/shard_map/ppermute | solution.py:410
  61.4 19.7 %collective-permute-start.1 = (bf16[128,1024]{1,0:T(8,128)(2,1)S(1)}, bf16[128,1024]{1,0:T(8,128)(2,1)S(1)}, u32[]{:S(2)}, u32[]{:S(2)}) collective-permute-start(bf16[128,1024]{1,0:T(8,128)(2,1)S(1)} %constant_dynamic-slice_fusion), channel_id=1, source_target_pairs={{0,8},{8,0},{16,24},{24,16},{32,40},{40,32},{48,56},{56,48},{64,72... | collective-permute-start | bytes 786440 | tf_op jit(solution)/shard_map/ppermute | solution.py:410
  61.8 0.8 copy-start.5
  77.7 1.4 %copy-start = (bf16[16,272,256]{2,1,0:T(8,128)(2,1)}, bf16[16,272,256]{2,1,0:T(8,128)(2,1)S(1)}, u32[]{:S(2)}) copy-start(bf16[16,272,256]{2,1,0:T(8,128)(2,1)S(1)} %mixer.1) | copy-start | bytes 6684676
  79.1 9.2 %copy-start.1 = (bf16[128,2048]{1,0:T(8,128)(2,1)S(1)}, bf16[128,2048]{1,0:T(8,128)(2,1)}, u32[]{:S(2)}) copy-start(bf16[128,2048]{1,0:T(8,128)(2,1)} %q_ref.1) | copy-start | bytes 1572868
  81.1 0.7 copy-start.3
  81.8 37.8 %all-to-all-start.2 = ((bf16[16,272,256]{2,1,0:T(8,128)(2,1)}), bf16[16,272,256]{2,1,0:T(8,128)(2,1)S(1)}, u32[]{:S(2)}, u32[]{:S(2)}) async-start(bf16[16,272,256]{2,1,0:T(8,128)(2,1)} %copy-done), calls=%async_computation.2 | async-start | bytes 4456448 | tf_op jit(solution)/shard_map/all_to_all | solution.py:587
  88.3 1.0 copy-start.2
  89.4 0.9 copy-start.4
  106.4 12.3 %collective-permute-start.2 = (bf16[128,1024]{1,0:T(8,128)(2,1)S(1)}, bf16[128,1024]{1,0:T(8,128)(2,1)S(1)}, u32[]{:S(2)}, u32[]{:S(2)}) collective-permute-start(bf16[128,1024]{1,0:T(8,128)(2,1)S(1)} %get-tuple-element.43), channel_id=1, source_target_pairs={{0,8},{8,0},{16,24},{24,16},{32,40},{40,32},{48,56},{56,48},{64,72... | collective-permute-start | bytes 786440 | tf_op jit(solution)/shard_map/ppermute | solution.py:410
  108.3 14.2 %collective-permute-start.3 = (bf16[256,256]{1,0:T(8,128)(2,1)}, bf16[256,256]{1,0:T(8,128)(2,1)S(1)}, u32[]{:S(2)}, u32[]{:S(2)}) collective-permute-start(bf16[256,256]{1,0:T(8,128)(2,1)} %get-tuple-element.52), channel_id=1, source_target_pairs={{16,0},{24,8},{32,16},{40,24},{48,32},{56,40},{64,48},{72,56},{80,... | collective-permute-start | bytes 393224 | tf_op jit(solution)/shard_map/ppermute | solution.py:404
  109.6 12.9 %collective-permute-start.4 = (bf16[256,256]{1,0:T(8,128)(2,1)}, bf16[256,256]{1,0:T(8,128)(2,1)S(1)}, u32[]{:S(2)}, u32[]{:S(2)}) collective-permute-start(bf16[256,256]{1,0:T(8,128)(2,1)} %get-tuple-element.53), channel_id=1, source_target_pairs={{32,0},{40,8},{48,16},{56,24},{64,32},{72,40},{80,48},{88,56},{96,... | collective-permute-start | bytes 393224 | tf_op jit(solution)/shard_map/ppermute | solution.py:404
  110.9 14.9 %collective-permute-start.5 = (bf16[256,256]{1,0:T(8,128)(2,1)}, bf16[256,256]{1,0:T(8,128)(2,1)S(1)}, u32[]{:S(2)}, u32[]{:S(2)}) collective-permute-start(bf16[256,256]{1,0:T(8,128)(2,1)} %get-tuple-element.54), channel_id=1, source_target_pairs={{48,0},{56,8},{64,16},{72,24},{80,32},{88,40},{96,48},{104,56},{11... | collective-permute-start | bytes 393224 | tf_op jit(solution)/shard_map/ppermute | solution.py:404
  112.2 13.6 %collective-permute-start.6 = (bf16[256,256]{1,0:T(8,128)(2,1)}, bf16[256,256]{1,0:T(8,128)(2,1)}, u32[]{:S(2)}, u32[]{:S(2)}) collective-permute-start(bf16[256,256]{1,0:T(8,128)(2,1)} %get-tuple-element.55), channel_id=1, source_target_pairs={{64,0},{72,8},{80,16},{88,24},{96,32},{104,40},{112,48},{120,56},{... | collective-permute-start | bytes 393224 | tf_op jit(solution)/shard_map/ppermute | solution.py:404
  126.8 4.3 %collective-permute-start.7 = (bf16[128,256]{1,0:T(8,128)(2,1)S(1)}, bf16[128,256]{1,0:T(8,128)(2,1)S(1)}, u32[]{:S(2)}, u32[]{:S(2)}) collective-permute-start(bf16[128,256]{1,0:T(8,128)(2,1)S(1)} %get-tuple-element.57), channel_id=1, source_target_pairs={{0,8},{8,0},{16,24},{24,16},{32,40},{40,32},{48,56},{56,48},{64,72... | collective-permute-start | bytes 196616 | tf_op jit(solution)/shard_map/ppermute | solution.py:410

commit v6 on v5

--- a/solution.py
+++ b/solution.py
@@ -411,7 +411,8 @@
 
 
 def pack_kernel(
-    x_ref, g_ref, bc_ref, dt_ref, k_ref, v_ref, out_ref, kv_ref, buf, kv_buf, in_sems, out_sems, kv_sem
+    idx_ref, x_ref, g_ref, bc_ref, dt_ref, k_ref, v_ref, q_ref, do_ref, out_ref, kv_ref, qs_ref, dos_ref,
+    buf, kv_buf, qo_buf, in_sems, out_sems, kv_sem, qo_sems,
 ):
     blocks = out_ref.shape[0]
     loads = []
@@ -424,11 +425,20 @@
         for one in pair:
             one.start()
         loads.append(pair)
+    half = qs_ref.shape[1]
+    at = pl.multiple_of((1 - lax.rem(idx_ref[0], 2)) * half, half)
+    qo_loads = [
+        pltpu.make_async_copy(src.at[:, pl.ds(at, half)], qo_buf.at[k], qo_sems.at[k])
+        for k, src in enumerate((q_ref, do_ref))
+    ]
+    for one in qo_loads:
+        one.start()
     b_all = bc_ref[:, 0, :]
     c_all = bc_ref[:, 1, :]
     bc = [
         jnp.concatenate([b_all[:, at : at + HD], c_all[:, at : at + HD]], axis=1) for at in (0, HD)
     ]
+    stores = []
     for d in range(blocks):
         buf[d, 2 * BLK : 3 * BLK] = bc[d // (blocks // 2)]
         raw = jnp.concatenate([dt_ref[2 * d : 2 * d + 1], dt_ref[2 * d + 1 : 2 * d + 2]], axis=1)
@@ -436,41 +446,49 @@
         mid = (raw - hi).astype(BF16).astype(F32)
         parts = [hi, mid, raw - hi - mid, jnp.zeros((13, 2 * BLK), F32)]
         buf[d, 3 * BLK : 3 * BLK + 16] = jnp.concatenate(parts, axis=0).astype(BF16)
-        head = slice((d % 2) * HD, (d % 2 + 1) * HD)
-        kv_buf[d] = jnp.concatenate([k_ref[:, head], v_ref[:, head]], axis=1)
-    stores = []
-    for d in range(blocks):
         for one in loads[d]:
             one.wait()
         stores.append(pltpu.make_async_copy(buf.at[d], out_ref.at[d], out_sems.at[d]))
         stores[-1].start()
+    for d in range(blocks):
+        head = slice((d % 2) * HD, (d % 2 + 1) * HD)
+        kv_buf[d] = jnp.concatenate([k_ref[:, head], v_ref[:, head]], axis=1)
     stores.append(pltpu.make_async_copy(kv_buf, kv_ref, kv_sem))
     stores[-1].start()
+    for k, dst in enumerate((qs_ref, dos_ref)):
+        qo_loads[k].wait()
+        stores.append(pltpu.make_async_copy(qo_buf.at[k], dst, qo_sems.at[2 + k]))
+        stores[-1].start()
     for one in stores:
         one.wait()
 
 
-def pack(x_in, grad, bc_sent, dt_raw, key, value, blocks):
+def pack(place, x_in, grad, bc_sent, dt_raw, key, value, query, d_out, blocks):
     hbm = pl.BlockSpec(memory_space=pltpu.HBM)
     vmem = pl.BlockSpec(memory_space=pltpu.VMEM)
+    part = jax.ShapeDtypeStruct((BLK, query.shape[1] // 2), BF16)
     return pl.pallas_call(
         pack_kernel,
         out_shape=[
             jax.ShapeDtypeStruct((blocks, 3 * BLK + 16, 2 * HD), BF16),
             jax.ShapeDtypeStruct((blocks, BLK, 2 * HD), BF16),
+            part,
+            part,
         ],
-        in_specs=[hbm, hbm, vmem, vmem, vmem, vmem],
-        out_specs=[hbm, hbm],
+        in_specs=[pl.BlockSpec(memory_space=pltpu.SMEM), hbm, hbm, vmem, vmem, vmem, vmem, hbm, hbm],
+        out_specs=[hbm] * 4,
         scratch_shapes=[
             pltpu.VMEM((blocks, 3 * BLK + 16, 2 * HD), BF16),
             pltpu.VMEM((blocks, BLK, 2 * HD), BF16),
+            pltpu.VMEM((2,) + part.shape, BF16),
             pltpu.SemaphoreType.DMA((2 * blocks,)),
             pltpu.SemaphoreType.DMA((blocks,)),
             pltpu.SemaphoreType.DMA(()),
+            pltpu.SemaphoreType.DMA((4,)),
         ],
         cost_estimate=pl.CostEstimate(flops=0, bytes_accessed=7 * 2**20, transcendentals=0),
         name="pack",
-    )(x_in, grad, bc_sent, dt_raw, key, value)
+    )(place, x_in, grad, bc_sent, dt_raw, key, value, query, d_out)
 
 
 def unpack_kernel(
@@ -602,12 +620,14 @@
     def pick(own, other):
         return jnp.where(odd == 0, own, other), jnp.where(odd == 0, other, own)
 
-    packed, kv_sent = pack(x_in, grad_ssd, bc_in, dt_raw, key, value, ctx)
+    packed, kv_sent, q_sent, do_sent = pack(
+        place, x_in, grad_ssd, bc_in, dt_raw, key, value, query, d_out, ctx
+    )
     got = swap(packed)
     got, kv_sent = lax.optimization_barrier((got, kv_sent))
     kv = swap(kv_sent)
-    got_q = partner(half(query, 1 - odd))
-    got_do = partner(half(d_out, 1 - odd))
+    got_q = partner(q_sent)
+    got_do = partner(do_sent)
     mixed = ssm_core(doc_lengths, place, rate, got, conv_x, conv_bc)
     mixed, kv, got_q, got_do = lax.optimization_barrier((mixed, kv, got_q, got_do))
     back = swap(mixed)

time: 134 us -> 134 us (level)
    dynamic_slice x2 -> x0, local copies, waits for them, and re-layouts: 1.94 us -> none  [half(): lax.dynamic_slice_in_dim(a, which * (a.shape[1] // 2), a.shape[1] // 2, 1)]
    ppermute x4, waiting for transfers between devices: 10.1 us -> 11.7 us  [partner(): lax.ppermute(a, 'ctx', [(i, i ^ 1) for i in range(lax.axis_size('ctx'))])]
    unnamed x18 -> x26, local copies, waits for them, and re-layouts: 4.93 us -> 6.36 us
  transfers between devices with their start and end apart: 10 -> 10, of which waited for: 6 -> 7; matrix products, arithmetic and copies ran while one was open for 2% -> 1% of each run, Pallas kernels for 25% -> 25%
where the time goes in v6:
time: 134 us; the launch traced here: 131 us
  blocking collectives  48.3 us (36%)
  Pallas kernels  38.3 us (29%)
  starting transfers between devices  20.7 us (15%)
  waiting for transfers between devices  15.9 us (12%)
  local copies, waits for them, and re-layouts  7.05 us (5%)
    all_to_all x1, blocking collectives, swap(): return lax.all_to_all(a, 'ctx', 0, 0, tiled=True)  48.3 us
    pallas_call x1, Pallas kernels, attention_core(): pl.pallas_call(attention_kernel, out_shape=outs, in_specs=[smem, smem] +...  16.1 us
    pallas_call x1, Pallas kernels, ssm_core(): pl.pallas_call(ssm_kernel, out_shape=jax.ShapeDtypeStruct((blocks, 2 * BL...  15.1 us
    ppermute x4, waiting for transfers between devices, partner(): lax.ppermute(a, 'ctx', [(i, i ^ 1) for i in range(lax.axis_size('ctx'))])  11.7 us
    all_to_all x2, starting transfers between devices, swap(): return lax.all_to_all(a, 'ctx', 0, 0, tiled=True)  10.9 us
    unnamed x26, local copies, waits for them, and re-layouts  6.36 us
    ppermute x4, starting transfers between devices, shift(): lax.ppermute(a, 'ctx', [(i, i + by) for i in range(devices) if 0 <= i + b...  5.16 us
    ppermute x4, starting transfers between devices, partner(): lax.ppermute(a, 'ctx', [(i, i ^ 1) for i in range(lax.axis_size('ctx'))])  4.67 us
  transfers between devices with their start and end apart: 10, of which 7 were waited for; matrix products, arithmetic and copies ran while one was open for 1% of the time, Pallas kernels for 25%

profile of v6, /device:TPU:0, one launch (start us, length us, event | category | flops | bytes accessed | tf_op | source)
XLA Modules:
  0.0 131.1 jit_solution(14967835008846929236)
XLA Ops:
  0.6 4.5 %pack.1 = (bf16[16,400,256]{2,1,0:T(8,128)(2,1)}, bf16[16,128,256]{2,1,0:T(8,128)(2,1)}, bf16[128,1024]{1,0:T(8,128)(2,1)}, bf16[128,1024]{1,0:T(8,128)(2,1)}) custom-call(s32[1]{0:T(128)} %bitcast.idx_ref, bf16[128,4096]{1,0:T(8,128)(2,1)} %x_ref.1, bf16[128,4096]{1,0:T(8,128)(2,1)} %g_ref.1, bf16[128,2,256]{2,1,0:T(2,128)(2,1)} %bc_ref.1, ...), custom_call_target="tpu_custom_call" | custom-call | bytes 7340032 | tf_op jit(solution)/shard_map/pack/pallas_call | solution.py:470
  5.1 0.0 copy-start.9
  5.1 0.0 copy-start.10
  5.2 0.0 copy-start.11
  5.2 0.0 copy-start.12
  5.2 48.3 %all_to_all.15.r_ref = bf16[16,400,256]{2,1,0:T(8,128)(2,1)S(1)} all-to-all(bf16[16,400,256]{2,1,0:T(8,128)(2,1)} %get-tuple-element.36), channel_id=1, replica_groups=mesh['ctx'=16,'head'=2,'dp'=4] {'ctx'}, dimensions={0} | all-to-all | bytes 6553600 | tf_op jit(solution)/shard_map/all_to_all | solution.py:605
  53.5 4.3 %all-to-all-start.1 = ((bf16[16,128,256]{2,1,0:T(8,128)(2,1)}), bf16[16,128,256]{2,1,0:T(8,128)(2,1)}, u32[]{:S(2)}, u32[]{:S(2)}) async-start(bf16[16,128,256]{2,1,0:T(8,128)(2,1)} %get-tuple-element.39), calls=%async_computation.1 | async-start | bytes 2097152 | tf_op jit(solution)/shard_map/all_to_all | solution.py:605
  57.8 1.7 %collective-permute-start = (bf16[128,1024]{1,0:T(8,128)(2,1)}, bf16[128,1024]{1,0:T(8,128)(2,1)S(1)}, u32[]{:S(2)}, u32[]{:S(2)}) collective-permute-start(bf16[128,1024]{1,0:T(8,128)(2,1)} %get-tuple-element.40), channel_id=1, source_target_pairs={{0,8},{8,0},{16,24},{24,16},{32,40},{40,32},{48,56},{56,48},{64,72... | collective-permute-start | bytes 786440 | tf_op jit(solution)/shard_map/ppermute | solution.py:410
  59.6 0.4 collective-permute-start.1
  59.9 0.0 copy-done.9
  59.9 0.0 copy-done.10
  59.9 0.0 copy-done.11
  59.9 0.0 copy-done.12
  59.9 15.1 %mixer.1 = bf16[16,272,256]{2,1,0:T(8,128)(2,1)S(1)} custom-call(s32[4]{0:T(128)S(1)} %copy-done.12, s32[1]{0:T(128)} %bitcast.idx_ref, f32[32]{0:T(128)S(1)} %copy-done.11, bf16[16,400,256]{2,1,0:T(8,128)(2,1)S(1)} %all_to_all.15.r_ref, f32[4,4096]{1,0:T(4,128)S(1)} %copy-done.9, f32[4,2,256]{2,1,0:T(2,128)S(1)} %copy-done.10), custom_call_target="tpu_custom_call" | custom-call | flops 3000000000 | bytes 6291456 | tf_op jit(solution)/shard_map/mixer/pallas_call | solution.py:258
  75.0 0.0 copy-start
  75.1 1.4 %copy-done = bf16[16,272,256]{2,1,0:T(8,128)(2,1)} copy-done((bf16[16,272,256]{2,1,0:T(8,128)(2,1)}, bf16[16,272,256]{2,1,0:T(8,128)(2,1)S(1)}, u32[]{:S(2)}) %copy-start) | copy-done | bytes 2228248
  76.4 0.0 copy-start.1
  76.4 0.0 copy-start.2
  76.4 1.8 %collective-permute-done.got_q_ref = bf16[128,1024]{1,0:T(8,128)(2,1)S(1)} collective-permute-done((bf16[128,1024]{1,0:T(8,128)(2,1)}, bf16[128,1024]{1,0:T(8,128)(2,1)S(1)}, u32[]{:S(2)}, u32[]{:S(2)}) %collective-permute-start) | collective-permute-done | bytes 262176 | tf_op jit(solution)/shard_map/ppermute | solution.py:410
  78.2 0.0 copy-start.5
  78.2 0.7 copy-done.5
  78.9 2.3 %collective-permute-done.1.got_do_ref = bf16[128,1024]{1,0:T(8,128)(2,1)S(1)} collective-permute-done((bf16[128,1024]{1,0:T(8,128)(2,1)}, bf16[128,1024]{1,0:T(8,128)(2,1)S(1)}, u32[]{:S(2)}, u32[]{:S(2)}) %collective-permute-start.1) | collective-permute-done | bytes 262176 | tf_op jit(solution)/shard_map/ppermute | solution.py:410
  81.3 0.0 copy-start.7
  81.3 0.7 copy-done.7
  82.0 0.0 all-to-all-done.1.kv_ref
  82.0 6.5 %all-to-all-start.2 = ((bf16[16,272,256]{2,1,0:T(8,128)(2,1)}), bf16[16,272,256]{2,1,0:T(8,128)(2,1)S(1)}, u32[]{:S(2)}, u32[]{:S(2)}) async-start(bf16[16,272,256]{2,1,0:T(8,128)(2,1)} %copy-done), calls=%async_computation.2 | async-start | bytes 4456448 | tf_op jit(solution)/shard_map/all_to_all | solution.py:605
  88.5 0.0 copy-done.1
  88.5 0.0 copy-done.2
  88.5 0.0 copy-start.6
  88.5 0.9 copy-done.6
  89.5 0.0 copy-start.8
  89.5 0.9 copy-done.8
  90.4 16.1 %attention.1 = (bf16[128,1024]{1,0:T(8,128)(2,1)S(1)}, bf16[128,1024]{1,0:T(8,128)(2,1)S(1)}, f32[256,256]{1,0:T(8,128)S(1)}, bf16[256,256]{1,0:T(8,128)(2,1)}, ...) custom-call(s32[4]{0:T(128)S(1)} %copy-done.12, s32[1]{0:T(128)} %bitcast.idx_ref, ...), custom_call_target="tpu_custom_call" | custom-call | flops 4000000000 | bytes 4194304 | tf_op jit(solution)/shard_map/attention/pallas_call | solution.py:384
  106.5 0.0 copy-start.3
  106.5 0.7 copy-done.3
  107.2 1.9 %collective-permute-start.2 = (bf16[128,1024]{1,0:T(8,128)(2,1)S(1)}, bf16[128,1024]{1,0:T(8,128)(2,1)S(1)}, u32[]{:S(2)}, u32[]{:S(2)}) collective-permute-start(bf16[128,1024]{1,0:T(8,128)(2,1)S(1)} %get-tuple-element.47), channel_id=1, source_target_pairs={{0,8},{8,0},{16,24},{24,16},{32,40},{40,32},{48,56},{56,48},{64,72... | collective-permute-start | bytes 786440 | tf_op jit(solution)/shard_map/ppermute | solution.py:410
  109.1 1.3 collective-permute-start.3
  110.4 1.3 collective-permute-start.4
  111.7 1.3 collective-permute-start.5
  113.0 1.3 collective-permute-start.6
  114.3 4.6 %collective-permute-done.2.dq_got = bf16[128,1024]{1,0:T(8,128)(2,1)S(1)} collective-permute-done((bf16[128,1024]{1,0:T(8,128)(2,1)S(1)}, bf16[128,1024]{1,0:T(8,128)(2,1)S(1)}, u32[]{:S(2)}, u32[]{:S(2)}) %collective-permute-start.2) | collective-permute-done | bytes 262176 | tf_op jit(solution)/shard_map/ppermute | solution.py:410
  118.9 0.8 all-to-all-done.2.part
  119.7 0.0 copy-start.4
  119.7 0.9 copy-done.4
  120.7 1.9 %unpack.1 = (bf16[128,4096]{1,0:T(8,128)(2,1)}, bf16[128,512]{1,0:T(8,128)(2,1)S(1)}, f32[32,128]{1,0:T(8,128)}, f32[4,4096]{1,0:T(4,128)}, f32[4,2,256]{2,1,0:T...) custom-call(s32[1]{0:T(128)} %bitcast.idx_ref, ...), custom_call_target="tpu_custom_call", output_to_operand_aliasing={{6}: (4, {})} | custom-call | flops 1000000 | bytes 4194304 | tf_op jit(solution)/shard_map/unpack/pallas_call | solution.py:535
  122.6 0.1 collective-permute-done.3.r1
  122.7 0.0 collective-permute-done.4.r2
  122.7 3.3 %collective-permute-done.5.r3 = bf16[256,256]{1,0:T(8,128)(2,1)S(1)} collective-permute-done((bf16[256,256]{1,0:T(8,128)(2,1)}, bf16[256,256]{1,0:T(8,128)(2,1)S(1)}, u32[]{:S(2)}, u32[]{:S(2)}) %collective-permute-start.5) | collective-permute-done | bytes 131104 | tf_op jit(solution)/shard_map/ppermute | solution.py:404
  126.0 0.0 collective-permute-done.6.r4
  126.0 0.1 kv_total.1
  126.1 0.6 collective-permute-start.7
  126.7 0.7 reshape.23
  127.4 3.0 %collective-permute-done.7.other = bf16[128,256]{1,0:T(8,128)(2,1)S(1)} collective-permute-done((bf16[128,256]{1,0:T(8,128)(2,1)S(1)}, bf16[128,256]{1,0:T(8,128)(2,1)S(1)}, u32[]{:S(2)}, u32[]{:S(2)}) %collective-permute-start.7) | collective-permute-done | bytes 65568 | tf_op jit(solution)/shard_map/ppermute | solution.py:410
  130.4 0.7 kv_place.1
Async XLA Ops:
  5.1 54.8 %copy-start.9 = (f32[4,4096]{1,0:T(4,128)S(1)}, f32[4,4096]{1,0:T(4,128)}, u32[]{:S(2)}) copy-start(f32[4,4096]{1,0:T(4,128)} %wx_ref.1) | copy-start | bytes 196612
  5.1 54.8 %copy-start.10 = (f32[4,2,256]{2,1,0:T(2,128)S(1)}, f32[4,2,256]{2,1,0:T(2,128)}, u32[]{:S(2)}) copy-start(f32[4,2,256]{2,1,0:T(2,128)} %wbc_ref.1) | copy-start | bytes 24580
  5.2 54.8 %copy-start.11 = (f32[32]{0:T(128)S(1)}, f32[32]{0:T(128)}, u32[]{:S(2)}) copy-start(f32[32]{0:T(128)} %rate_ref.1) | copy-start | bytes 388
  5.2 54.8 %copy-start.12 = (s32[4]{0:T(128)S(1)}, s32[4]{0:T(128)}, u32[]{:S(2)}) copy-start(s32[4]{0:T(128)} %doc_ref.3) | copy-start | bytes 52
  53.5 28.5 %all-to-all-start.1 = ((bf16[16,128,256]{2,1,0:T(8,128)(2,1)}), bf16[16,128,256]{2,1,0:T(8,128)(2,1)}, u32[]{:S(2)}, u32[]{:S(2)}) async-start(bf16[16,128,256]{2,1,0:T(8,128)(2,1)} %get-tuple-element.39), calls=%async_computation.1 | async-start | bytes 2097152 | tf_op jit(solution)/shard_map/all_to_all | solution.py:605
  57.8 20.4 %collective-permute-start = (bf16[128,1024]{1,0:T(8,128)(2,1)}, bf16[128,1024]{1,0:T(8,128)(2,1)S(1)}, u32[]{:S(2)}, u32[]{:S(2)}) collective-permute-start(bf16[128,1024]{1,0:T(8,128)(2,1)} %get-tuple-element.40), channel_id=1, source_target_pairs={{0,8},{8,0},{16,24},{24,16},{32,40},{40,32},{48,56},{56,48},{64,72... | collective-permute-start | bytes 786440 | tf_op jit(solution)/shard_map/ppermute | solution.py:410
  59.6 21.7 %collective-permute-start.1 = (bf16[128,1024]{1,0:T(8,128)(2,1)}, bf16[128,1024]{1,0:T(8,128)(2,1)S(1)}, u32[]{:S(2)}, u32[]{:S(2)}) collective-permute-start(bf16[128,1024]{1,0:T(8,128)(2,1)} %get-tuple-element.41), channel_id=1, source_target_pairs={{0,8},{8,0},{16,24},{24,16},{32,40},{40,32},{48,56},{56,48},{64,72... | collective-permute-start | bytes 786440 | tf_op jit(solution)/shard_map/ppermute | solution.py:410
  75.0 1.4 %copy-start = (bf16[16,272,256]{2,1,0:T(8,128)(2,1)}, bf16[16,272,256]{2,1,0:T(8,128)(2,1)S(1)}, u32[]{:S(2)}) copy-start(bf16[16,272,256]{2,1,0:T(8,128)(2,1)S(1)} %mixer.1) | copy-start | bytes 6684676
  76.4 12.1 %copy-start.1 = (bf16[128,2048]{1,0:T(8,128)(2,1)S(1)}, bf16[128,2048]{1,0:T(8,128)(2,1)}, u32[]{:S(2)}) copy-start(bf16[128,2048]{1,0:T(8,128)(2,1)} %q_ref.3) | copy-start | bytes 1572868
  76.4 12.1 %copy-start.2 = (bf16[128,2048]{1,0:T(8,128)(2,1)S(1)}, bf16[128,2048]{1,0:T(8,128)(2,1)}, u32[]{:S(2)}) copy-start(bf16[128,2048]{1,0:T(8,128)(2,1)} %do_ref.3) | copy-start | bytes 1572868
  78.2 0.7 copy-start.5
  81.3 0.7 copy-start.7
  82.0 37.8 %all-to-all-start.2 = ((bf16[16,272,256]{2,1,0:T(8,128)(2,1)}), bf16[16,272,256]{2,1,0:T(8,128)(2,1)S(1)}, u32[]{:S(2)}, u32[]{:S(2)}) async-start(bf16[16,272,256]{2,1,0:T(8,128)(2,1)} %copy-done), calls=%async_computation.2 | async-start | bytes 4456448 | tf_op jit(solution)/shard_map/all_to_all | solution.py:605
  88.5 1.0 copy-start.6
  89.5 0.9 copy-start.8
  106.5 0.7 copy-start.3
  107.2 11.7 %collective-permute-start.2 = (bf16[128,1024]{1,0:T(8,128)(2,1)S(1)}, bf16[128,1024]{1,0:T(8,128)(2,1)S(1)}, u32[]{:S(2)}, u32[]{:S(2)}) collective-permute-start(bf16[128,1024]{1,0:T(8,128)(2,1)S(1)} %get-tuple-element.47), channel_id=1, source_target_pairs={{0,8},{8,0},{16,24},{24,16},{32,40},{40,32},{48,56},{56,48},{64,72... | collective-permute-start | bytes 786440 | tf_op jit(solution)/shard_map/ppermute | solution.py:410
  109.1 13.5 %collective-permute-start.3 = (bf16[256,256]{1,0:T(8,128)(2,1)}, bf16[256,256]{1,0:T(8,128)(2,1)S(1)}, u32[]{:S(2)}, u32[]{:S(2)}) collective-permute-start(bf16[256,256]{1,0:T(8,128)(2,1)} %get-tuple-element.56), channel_id=1, source_target_pairs={{16,0},{24,8},{32,16},{40,24},{48,32},{56,40},{64,48},{72,56},{80,... | collective-permute-start | bytes 393224 | tf_op jit(solution)/shard_map/ppermute | solution.py:404
  110.4 12.2 %collective-permute-start.4 = (bf16[256,256]{1,0:T(8,128)(2,1)}, bf16[256,256]{1,0:T(8,128)(2,1)S(1)}, u32[]{:S(2)}, u32[]{:S(2)}) collective-permute-start(bf16[256,256]{1,0:T(8,128)(2,1)} %get-tuple-element.57), channel_id=1, source_target_pairs={{32,0},{40,8},{48,16},{56,24},{64,32},{72,40},{80,48},{88,56},{96,... | collective-permute-start | bytes 393224 | tf_op jit(solution)/shard_map/ppermute | solution.py:404
  111.7 14.3 %collective-permute-start.5 = (bf16[256,256]{1,0:T(8,128)(2,1)}, bf16[256,256]{1,0:T(8,128)(2,1)S(1)}, u32[]{:S(2)}, u32[]{:S(2)}) collective-permute-start(bf16[256,256]{1,0:T(8,128)(2,1)} %get-tuple-element.58), channel_id=1, source_target_pairs={{48,0},{56,8},{64,16},{72,24},{80,32},{88,40},{96,48},{104,56},{11... | collective-permute-start | bytes 393224 | tf_op jit(solution)/shard_map/ppermute | solution.py:404
  113.0 13.0 %collective-permute-start.6 = (bf16[256,256]{1,0:T(8,128)(2,1)}, bf16[256,256]{1,0:T(8,128)(2,1)S(1)}, u32[]{:S(2)}, u32[]{:S(2)}) collective-permute-start(bf16[256,256]{1,0:T(8,128)(2,1)} %get-tuple-element.59), channel_id=1, source_target_pairs={{64,0},{72,8},{80,16},{88,24},{96,32},{104,40},{112,48},{120,56},{... | collective-permute-start | bytes 393224 | tf_op jit(solution)/shard_map/ppermute | solution.py:404
  119.7 1.0 copy-start.4
  126.1 4.3 %collective-permute-start.7 = (bf16[128,256]{1,0:T(8,128)(2,1)S(1)}, bf16[128,256]{1,0:T(8,128)(2,1)S(1)}, u32[]{:S(2)}, u32[]{:S(2)}) collective-permute-start(bf16[128,256]{1,0:T(8,128)(2,1)S(1)} %get-tuple-element.61), channel_id=1, source_target_pairs={{0,8},{8,0},{16,24},{24,16},{32,40},{40,32},{48,56},{56,48},{64,72... | collective-permute-start | bytes 196616 | tf_op jit(solution)/shard_map/ppermute | solution.py:410

commit v7 on v6

--- a/solution.py
+++ b/solution.py
@@ -13,7 +13,7 @@
 BACK = 8
 LOG2E = 1.4426950408889634
 NEG_BIG = -1e30
-UNROLL = 8
+UNROLL = 4
 
 
 def dot_nn(a, b):

time: 134 us -> 134 us (level)
  transfers between devices with their start and end apart: 10 -> 10, of which waited for: 7 -> 7; matrix products, arithmetic and copies ran while one was open for 1% -> 1% of each run, Pallas kernels for 25% -> 26%
where the time goes in v7:
time: 134 us; the launch traced here: 131 us
  blocking collectives  48.3 us (36%)
  Pallas kernels  39 us (29%)
  starting transfers between devices  20.7 us (15%)
  waiting for transfers between devices  15.3 us (11%)
  local copies, waits for them, and re-layouts  7.05 us (5%)
    all_to_all x1, blocking collectives, swap(): return lax.all_to_all(a, 'ctx', 0, 0, tiled=True)  48.3 us
    pallas_call x1, Pallas kernels, attention_core(): pl.pallas_call(attention_kernel, out_shape=outs, in_specs=[smem, smem] +...  16.1 us
    pallas_call x1, Pallas kernels, ssm_core(): pl.pallas_call(ssm_kernel, out_shape=jax.ShapeDtypeStruct((blocks, 2 * BL...  15.7 us
    ppermute x4, waiting for transfers between devices, partner(): lax.ppermute(a, 'ctx', [(i, i ^ 1) for i in range(lax.axis_size('ctx'))])  11.1 us
    all_to_all x2, starting transfers between devices, swap(): return lax.all_to_all(a, 'ctx', 0, 0, tiled=True)  10.9 us
    unnamed x26, local copies, waits for them, and re-layouts  6.36 us
    ppermute x4, starting transfers between devices, shift(): lax.ppermute(a, 'ctx', [(i, i + by) for i in range(devices) if 0 <= i + b...  5.16 us
    ppermute x4, starting transfers between devices, partner(): lax.ppermute(a, 'ctx', [(i, i ^ 1) for i in range(lax.axis_size('ctx'))])  4.67 us
  transfers between devices with their start and end apart: 10, of which 7 were waited for; matrix products, arithmetic and copies ran while one was open for 1% of the time, Pallas kernels for 26%

profile of v7, /device:TPU:0, one launch (start us, length us, event | category | flops | bytes accessed | tf_op | source)
XLA Modules:
  0.0 131.1 jit_solution(18351181465703408271)
XLA Ops:
  0.6 4.5 %pack.1 = (bf16[16,400,256]{2,1,0:T(8,128)(2,1)}, bf16[16,128,256]{2,1,0:T(8,128)(2,1)}, bf16[128,1024]{1,0:T(8,128)(2,1)}, bf16[128,1024]{1,0:T(8,128)(2,1)}) custom-call(s32[1]{0:T(128)} %bitcast.idx_ref, bf16[128,4096]{1,0:T(8,128)(2,1)} %x_ref.1, bf16[128,4096]{1,0:T(8,128)(2,1)} %g_ref.1, bf16[128,2,256]{2,1,0:T(2,128)(2,1)} %bc_ref.1, ...), custom_call_target="tpu_custom_call" | custom-call | bytes 7340032 | tf_op jit(solution)/shard_map/pack/pallas_call | solution.py:470
  5.1 0.0 copy-start.9
  5.1 0.0 copy-start.10
  5.2 0.0 copy-start.11
  5.2 0.0 copy-start.12
  5.2 48.3 %all_to_all.15.r_ref = bf16[16,400,256]{2,1,0:T(8,128)(2,1)S(1)} all-to-all(bf16[16,400,256]{2,1,0:T(8,128)(2,1)} %get-tuple-element.36), channel_id=1, replica_groups=mesh['ctx'=16,'head'=2,'dp'=4] {'ctx'}, dimensions={0} | all-to-all | bytes 6553600 | tf_op jit(solution)/shard_map/all_to_all | solution.py:605
  53.5 4.3 %all-to-all-start.1 = ((bf16[16,128,256]{2,1,0:T(8,128)(2,1)}), bf16[16,128,256]{2,1,0:T(8,128)(2,1)}, u32[]{:S(2)}, u32[]{:S(2)}) async-start(bf16[16,128,256]{2,1,0:T(8,128)(2,1)} %get-tuple-element.39), calls=%async_computation.1 | async-start | bytes 2097152 | tf_op jit(solution)/shard_map/all_to_all | solution.py:605
  57.8 1.7 %collective-permute-start = (bf16[128,1024]{1,0:T(8,128)(2,1)}, bf16[128,1024]{1,0:T(8,128)(2,1)S(1)}, u32[]{:S(2)}, u32[]{:S(2)}) collective-permute-start(bf16[128,1024]{1,0:T(8,128)(2,1)} %get-tuple-element.40), channel_id=1, source_target_pairs={{0,8},{8,0},{16,24},{24,16},{32,40},{40,32},{48,56},{56,48},{64,72... | collective-permute-start | bytes 786440 | tf_op jit(solution)/shard_map/ppermute | solution.py:410
  59.6 0.4 collective-permute-start.1
  59.9 0.0 copy-done.9
  59.9 0.0 copy-done.10
  59.9 0.0 copy-done.11
  59.9 0.0 copy-done.12
  59.9 15.7 %mixer.1 = bf16[16,272,256]{2,1,0:T(8,128)(2,1)S(1)} custom-call(s32[4]{0:T(128)S(1)} %copy-done.12, s32[1]{0:T(128)} %bitcast.idx_ref, f32[32]{0:T(128)S(1)} %copy-done.11, bf16[16,400,256]{2,1,0:T(8,128)(2,1)S(1)} %all_to_all.15.r_ref, f32[4,4096]{1,0:T(4,128)S(1)} %copy-done.9, f32[4,2,256]{2,1,0:T(2,128)S(1)} %copy-done.10), custom_call_target="tpu_custom_call" | custom-call | flops 3000000000 | bytes 6291456 | tf_op jit(solution)/shard_map/mixer/pallas_call | solution.py:258
  75.7 0.0 copy-start
  75.7 1.4 %copy-done = bf16[16,272,256]{2,1,0:T(8,128)(2,1)} copy-done((bf16[16,272,256]{2,1,0:T(8,128)(2,1)}, bf16[16,272,256]{2,1,0:T(8,128)(2,1)S(1)}, u32[]{:S(2)}) %copy-start) | copy-done | bytes 2228248
  77.1 0.0 copy-start.1
  77.1 0.0 copy-start.2
  77.1 1.1 collective-permute-done.got_q_ref
  78.2 0.0 copy-start.5
  78.2 0.7 copy-done.5
  78.9 2.3 %collective-permute-done.1.got_do_ref = bf16[128,1024]{1,0:T(8,128)(2,1)S(1)} collective-permute-done((bf16[128,1024]{1,0:T(8,128)(2,1)}, bf16[128,1024]{1,0:T(8,128)(2,1)S(1)}, u32[]{:S(2)}, u32[]{:S(2)}) %collective-permute-start.1) | collective-permute-done | bytes 262176 | tf_op jit(solution)/shard_map/ppermute | solution.py:410
  81.3 0.0 copy-start.7
  81.3 0.7 copy-done.7
  82.0 0.0 all-to-all-done.1.kv_ref
  82.0 6.5 %all-to-all-start.2 = ((bf16[16,272,256]{2,1,0:T(8,128)(2,1)}), bf16[16,272,256]{2,1,0:T(8,128)(2,1)S(1)}, u32[]{:S(2)}, u32[]{:S(2)}) async-start(bf16[16,272,256]{2,1,0:T(8,128)(2,1)} %copy-done), calls=%async_computation.2 | async-start | bytes 4456448 | tf_op jit(solution)/shard_map/all_to_all | solution.py:605
  88.5 0.0 copy-done.1
  88.5 0.0 copy-done.2
  88.5 0.0 copy-start.6
  88.5 0.9 copy-done.6
  89.5 0.0 copy-start.8
  89.5 0.9 copy-done.8
  90.4 16.1 %attention.1 = (bf16[128,1024]{1,0:T(8,128)(2,1)S(1)}, bf16[128,1024]{1,0:T(8,128)(2,1)S(1)}, f32[256,256]{1,0:T(8,128)S(1)}, bf16[256,256]{1,0:T(8,128)(2,1)}, ...) custom-call(s32[4]{0:T(128)S(1)} %copy-done.12, s32[1]{0:T(128)} %bitcast.idx_ref, ...), custom_call_target="tpu_custom_call" | custom-call | flops 4000000000 | bytes 4194304 | tf_op jit(solution)/shard_map/attention/pallas_call | solution.py:384
  106.5 0.0 copy-start.3
  106.5 0.7 copy-done.3
  107.2 1.9 %collective-permute-start.2 = (bf16[128,1024]{1,0:T(8,128)(2,1)S(1)}, bf16[128,1024]{1,0:T(8,128)(2,1)S(1)}, u32[]{:S(2)}, u32[]{:S(2)}) collective-permute-start(bf16[128,1024]{1,0:T(8,128)(2,1)S(1)} %get-tuple-element.47), channel_id=1, source_target_pairs={{0,8},{8,0},{16,24},{24,16},{32,40},{40,32},{48,56},{56,48},{64,72... | collective-permute-start | bytes 786440 | tf_op jit(solution)/shard_map/ppermute | solution.py:410
  109.1 1.3 collective-permute-start.3
  110.4 1.3 collective-permute-start.4
  111.7 1.3 collective-permute-start.5
  113.0 1.3 collective-permute-start.6
  114.3 4.6 %collective-permute-done.2.dq_got = bf16[128,1024]{1,0:T(8,128)(2,1)S(1)} collective-permute-done((bf16[128,1024]{1,0:T(8,128)(2,1)S(1)}, bf16[128,1024]{1,0:T(8,128)(2,1)S(1)}, u32[]{:S(2)}, u32[]{:S(2)}) %collective-permute-start.2) | collective-permute-done | bytes 262176 | tf_op jit(solution)/shard_map/ppermute | solution.py:410
  118.9 0.8 all-to-all-done.2.part
  119.7 0.0 copy-start.4
  119.7 0.9 copy-done.4
  120.7 1.9 %unpack.1 = (bf16[128,4096]{1,0:T(8,128)(2,1)}, bf16[128,512]{1,0:T(8,128)(2,1)S(1)}, f32[32,128]{1,0:T(8,128)}, f32[4,4096]{1,0:T(4,128)}, f32[4,2,256]{2,1,0:T...) custom-call(s32[1]{0:T(128)} %bitcast.idx_ref, ...), custom_call_target="tpu_custom_call", output_to_operand_aliasing={{6}: (4, {})} | custom-call | flops 1000000 | bytes 4194304 | tf_op jit(solution)/shard_map/unpack/pallas_call | solution.py:535
  122.6 0.1 collective-permute-done.3.r1
  122.7 0.0 collective-permute-done.4.r2
  122.7 3.3 %collective-permute-done.5.r3 = bf16[256,256]{1,0:T(8,128)(2,1)S(1)} collective-permute-done((bf16[256,256]{1,0:T(8,128)(2,1)}, bf16[256,256]{1,0:T(8,128)(2,1)S(1)}, u32[]{:S(2)}, u32[]{:S(2)}) %collective-permute-start.5) | collective-permute-done | bytes 131104 | tf_op jit(solution)/shard_map/ppermute | solution.py:404
  126.0 0.0 collective-permute-done.6.r4
  126.0 0.1 kv_total.1
  126.1 0.6 collective-permute-start.7
  126.7 0.7 reshape.23
  127.4 3.0 %collective-permute-done.7.other = bf16[128,256]{1,0:T(8,128)(2,1)S(1)} collective-permute-done((bf16[128,256]{1,0:T(8,128)(2,1)S(1)}, bf16[128,256]{1,0:T(8,128)(2,1)S(1)}, u32[]{:S(2)}, u32[]{:S(2)}) %collective-permute-start.7) | collective-permute-done | bytes 65568 | tf_op jit(solution)/shard_map/ppermute | solution.py:410
  130.4 0.7 kv_place.1
Async XLA Ops:
  5.1 54.8 %copy-start.9 = (f32[4,4096]{1,0:T(4,128)S(1)}, f32[4,4096]{1,0:T(4,128)}, u32[]{:S(2)}) copy-start(f32[4,4096]{1,0:T(4,128)} %wx_ref.1) | copy-start | bytes 196612
  5.1 54.8 %copy-start.10 = (f32[4,2,256]{2,1,0:T(2,128)S(1)}, f32[4,2,256]{2,1,0:T(2,128)}, u32[]{:S(2)}) copy-start(f32[4,2,256]{2,1,0:T(2,128)} %wbc_ref.1) | copy-start | bytes 24580
  5.2 54.8 %copy-start.11 = (f32[32]{0:T(128)S(1)}, f32[32]{0:T(128)}, u32[]{:S(2)}) copy-start(f32[32]{0:T(128)} %rate_ref.1) | copy-start | bytes 388
  5.2 54.8 %copy-start.12 = (s32[4]{0:T(128)S(1)}, s32[4]{0:T(128)}, u32[]{:S(2)}) copy-start(s32[4]{0:T(128)} %doc_ref.3) | copy-start | bytes 52
  53.5 28.5 %all-to-all-start.1 = ((bf16[16,128,256]{2,1,0:T(8,128)(2,1)}), bf16[16,128,256]{2,1,0:T(8,128)(2,1)}, u32[]{:S(2)}, u32[]{:S(2)}) async-start(bf16[16,128,256]{2,1,0:T(8,128)(2,1)} %get-tuple-element.39), calls=%async_computation.1 | async-start | bytes 2097152 | tf_op jit(solution)/shard_map/all_to_all | solution.py:605
  57.8 20.4 %collective-permute-start = (bf16[128,1024]{1,0:T(8,128)(2,1)}, bf16[128,1024]{1,0:T(8,128)(2,1)S(1)}, u32[]{:S(2)}, u32[]{:S(2)}) collective-permute-start(bf16[128,1024]{1,0:T(8,128)(2,1)} %get-tuple-element.40), channel_id=1, source_target_pairs={{0,8},{8,0},{16,24},{24,16},{32,40},{40,32},{48,56},{56,48},{64,72... | collective-permute-start | bytes 786440 | tf_op jit(solution)/shard_map/ppermute | solution.py:410
  59.6 21.7 %collective-permute-start.1 = (bf16[128,1024]{1,0:T(8,128)(2,1)}, bf16[128,1024]{1,0:T(8,128)(2,1)S(1)}, u32[]{:S(2)}, u32[]{:S(2)}) collective-permute-start(bf16[128,1024]{1,0:T(8,128)(2,1)} %get-tuple-element.41), channel_id=1, source_target_pairs={{0,8},{8,0},{16,24},{24,16},{32,40},{40,32},{48,56},{56,48},{64,72... | collective-permute-start | bytes 786440 | tf_op jit(solution)/shard_map/ppermute | solution.py:410
  75.7 1.4 %copy-start = (bf16[16,272,256]{2,1,0:T(8,128)(2,1)}, bf16[16,272,256]{2,1,0:T(8,128)(2,1)S(1)}, u32[]{:S(2)}) copy-start(bf16[16,272,256]{2,1,0:T(8,128)(2,1)S(1)} %mixer.1) | copy-start | bytes 6684676
  77.1 11.4 %copy-start.1 = (bf16[128,2048]{1,0:T(8,128)(2,1)S(1)}, bf16[128,2048]{1,0:T(8,128)(2,1)}, u32[]{:S(2)}) copy-start(bf16[128,2048]{1,0:T(8,128)(2,1)} %q_ref.3) | copy-start | bytes 1572868
  77.1 11.4 %copy-start.2 = (bf16[128,2048]{1,0:T(8,128)(2,1)S(1)}, bf16[128,2048]{1,0:T(8,128)(2,1)}, u32[]{:S(2)}) copy-start(bf16[128,2048]{1,0:T(8,128)(2,1)} %do_ref.3) | copy-start | bytes 1572868
  78.2 0.7 copy-start.5
  81.3 0.7 copy-start.7
  82.0 37.8 %all-to-all-start.2 = ((bf16[16,272,256]{2,1,0:T(8,128)(2,1)}), bf16[16,272,256]{2,1,0:T(8,128)(2,1)S(1)}, u32[]{:S(2)}, u32[]{:S(2)}) async-start(bf16[16,272,256]{2,1,0:T(8,128)(2,1)} %copy-done), calls=%async_computation.2 | async-start | bytes 4456448 | tf_op jit(solution)/shard_map/all_to_all | solution.py:605
  88.5 1.0 copy-start.6
  89.5 0.9 copy-start.8
  106.5 0.7 copy-start.3
  107.2 11.7 %collective-permute-start.2 = (bf16[128,1024]{1,0:T(8,128)(2,1)S(1)}, bf16[128,1024]{1,0:T(8,128)(2,1)S(1)}, u32[]{:S(2)}, u32[]{:S(2)}) collective-permute-start(bf16[128,1024]{1,0:T(8,128)(2,1)S(1)} %get-tuple-element.47), channel_id=1, source_target_pairs={{0,8},{8,0},{16,24},{24,16},{32,40},{40,32},{48,56},{56,48},{64,72... | collective-permute-start | bytes 786440 | tf_op jit(solution)/shard_map/ppermute | solution.py:410
  109.1 13.5 %collective-permute-start.3 = (bf16[256,256]{1,0:T(8,128)(2,1)}, bf16[256,256]{1,0:T(8,128)(2,1)S(1)}, u32[]{:S(2)}, u32[]{:S(2)}) collective-permute-start(bf16[256,256]{1,0:T(8,128)(2,1)} %get-tuple-element.56), channel_id=1, source_target_pairs={{16,0},{24,8},{32,16},{40,24},{48,32},{56,40},{64,48},{72,56},{80,... | collective-permute-start | bytes 393224 | tf_op jit(solution)/shard_map/ppermute | solution.py:404
  110.4 12.2 %collective-permute-start.4 = (bf16[256,256]{1,0:T(8,128)(2,1)}, bf16[256,256]{1,0:T(8,128)(2,1)S(1)}, u32[]{:S(2)}, u32[]{:S(2)}) collective-permute-start(bf16[256,256]{1,0:T(8,128)(2,1)} %get-tuple-element.57), channel_id=1, source_target_pairs={{32,0},{40,8},{48,16},{56,24},{64,32},{72,40},{80,48},{88,56},{96,... | collective-permute-start | bytes 393224 | tf_op jit(solution)/shard_map/ppermute | solution.py:404
  111.7 14.3 %collective-permute-start.5 = (bf16[256,256]{1,0:T(8,128)(2,1)}, bf16[256,256]{1,0:T(8,128)(2,1)S(1)}, u32[]{:S(2)}, u32[]{:S(2)}) collective-permute-start(bf16[256,256]{1,0:T(8,128)(2,1)} %get-tuple-element.58), channel_id=1, source_target_pairs={{48,0},{56,8},{64,16},{72,24},{80,32},{88,40},{96,48},{104,56},{11... | collective-permute-start | bytes 393224 | tf_op jit(solution)/shard_map/ppermute | solution.py:404
  113.0 13.0 %collective-permute-start.6 = (bf16[256,256]{1,0:T(8,128)(2,1)}, bf16[256,256]{1,0:T(8,128)(2,1)S(1)}, u32[]{:S(2)}, u32[]{:S(2)}) collective-permute-start(bf16[256,256]{1,0:T(8,128)(2,1)} %get-tuple-element.59), channel_id=1, source_target_pairs={{64,0},{72,8},{80,16},{88,24},{96,32},{104,40},{112,48},{120,56},{... | collective-permute-start | bytes 393224 | tf_op jit(solution)/shard_map/ppermute | solution.py:404
  119.7 1.0 copy-start.4
  126.1 4.3 %collective-permute-start.7 = (bf16[128,256]{1,0:T(8,128)(2,1)S(1)}, bf16[128,256]{1,0:T(8,128)(2,1)S(1)}, u32[]{:S(2)}, u32[]{:S(2)}) collective-permute-start(bf16[128,256]{1,0:T(8,128)(2,1)S(1)} %get-tuple-element.61), channel_id=1, source_target_pairs={{0,8},{8,0},{16,24},{24,16},{32,40},{40,32},{48,56},{56,48},{64,72... | collective-permute-start | bytes 196616 | tf_op jit(solution)/shard_map/ppermute | solution.py:410
